TPU v7x, 32 devices: a whole 2x2x4 slice. The times are simulated.
32 devices in a mesh: dp: 4 (over x, core), expert: 8 (over z, y).
Axes of the slice: x: 2, y: 2, z: 4, core: 2. Of those that a mesh axis runs over, the one named last changes fastest.
Arguments:
- tokens: bfloat16 [4096, 3072], P(('dp', 'expert')), may hold values from -6 to 6
- target: bfloat16 [4096, 3072], P(('dp', 'expert')), may hold values from -3 to 3
- routes: int32 [4096, 1], P(('dp', 'expert')), may hold values from 0 to 7; in each aligned block of 128 rows (0 to 127, 128 to 255, ...) at most 24 rows name the same one
- thresholds: int32 [8, 2048], P('expert', 'dp'), may hold values from 0 to 3
- enc_weight: bfloat16 [8, 3072, 2048], P('expert', None, 'dp'), may hold values from -0.109375 to 0.109375
- dec_weight: bfloat16 [8, 3072, 2048], P('expert', None, 'dp'), may hold values from -0.125 to 0.125
Outputs:
- recon: bfloat16 [4096, 3072], P(('dp', 'expert'))
- grad_enc: bfloat16 [8, 3072, 2048], P('expert', None, 'dp')
- grad_dec: bfloat16 [8, 3072, 2048], P('expert', None, 'dp')
Inputs may be any that keep to these rules, and one draw needn't show every extreme that they name: `routes`: within the rows of one device no expert is named by more than 24 rows, a bound that some block reaches.
All inputs are finite; a program needn't handle non-finite values.
Results may differ from a plain program's by a relative error of at most 0.012.
Values may be sent and summed in bfloat16 or wider, within the bound.
No kernel may reach another device: no remote copies, remote signals or barrier semaphores. Data moves between devices by JAX's collectives and lax.ppermute only.
A program may use at most 128 MiB of HBM per device.

v0:
```python
import jax
import jax.numpy as jnp
from jax import lax
from jax.sharding import PartitionSpec as P

error_scale = 0.03125


def slot_table(route_col, experts, capacity):
    choices = route_col[:, 0]
    one_hot = (choices[:, None] == jnp.arange(experts, dtype=jnp.int32)[None, :]).astype(jnp.int32)
    ranking = jnp.sum((jnp.cumsum(one_hot, axis=0) - 1) * one_hot, axis=1)
    slot_idx = choices * capacity + ranking
    positions = jnp.arange(experts * capacity, dtype=jnp.int32)
    return (positions[:, None] == slot_idx[None, :]).astype(jnp.bfloat16)


def local(tokens, target, routes, thresholds, enc_weight, dec_weight):
    experts = lax.axis_size("expert")
    per_dev = tokens.shape[0]
    features = tokens.shape[1]
    capacity = 3 * per_dev // (2 * experts)
    placing = slot_table(routes, experts, capacity)
    outbox = (
        jnp.dot(placing, tokens, preferred_element_type=jnp.float32)
        .astype(jnp.bfloat16)
        .reshape(experts, capacity, features)
    )
    column_rows = lax.all_gather(outbox[:, None], "dp", axis=1, tiled=True)
    arrived = lax.all_to_all(column_rows, "expert", split_axis=0, concat_axis=0, tiled=True)
    row_axis = 1
    leading = arrived.shape[:2]
    arrived_rows = arrived.reshape(-1, features)
    enc_part = enc_weight[0]
    dec_part = dec_weight[0]
    shifts = 0.25 * thresholds[0].astype(jnp.float32)
    latent_pre = jnp.dot(arrived_rows, enc_part, preferred_element_type=jnp.float32) - shifts
    squash = jax.nn.sigmoid(4.0 * latent_pre)
    activity = (latent_pre * squash).astype(jnp.bfloat16)
    derivative = squash + 4.0 * latent_pre * squash * (1.0 - squash)
    partials = lax.dot_general(
        activity, dec_part, (((1,), (1,)), ((), ())), preferred_element_type=jnp.float32
    )
    own_sums = lax.psum_scatter(
        partials.reshape(leading + (capacity, features)).astype(jnp.bfloat16),
        "dp",
        scatter_dimension=row_axis,
        tiled=True,
    )
    recon_rows = own_sums.reshape(experts, capacity, features)
    returned = lax.all_to_all(recon_rows, "expert", split_axis=0, concat_axis=0, tiled=True)
    recon = lax.dot_general(
        placing,
        returned.reshape(-1, features),
        (((0,), (0,)), ((), ())),
        preferred_element_type=jnp.float32,
    ).astype(jnp.bfloat16)
    error_tok = ((recon.astype(jnp.float32) - target.astype(jnp.float32)) * error_scale).astype(
        jnp.bfloat16
    )
    error_box = (
        jnp.dot(placing, error_tok, preferred_element_type=jnp.float32)
        .astype(jnp.bfloat16)
        .reshape(experts, capacity, features)
    )
    column_errors = lax.all_gather(error_box[:, None], "dp", axis=1, tiled=True)
    error_in = lax.all_to_all(column_errors, "expert", split_axis=0, concat_axis=0, tiled=True)
    error_rows = error_in.reshape(-1, features)
    grad_dec = lax.dot_general(
        error_rows, activity, (((0,), (0,)), ((), ())), preferred_element_type=jnp.float32
    ).astype(jnp.bfloat16)
    grad_act = jnp.dot(error_rows, dec_part, preferred_element_type=jnp.float32)
    grad_pre = (grad_act * derivative).astype(jnp.bfloat16)
    grad_enc = lax.dot_general(
        arrived_rows, grad_pre, (((0,), (0,)), ((), ())), preferred_element_type=jnp.float32
    ).astype(jnp.bfloat16)
    return (recon, grad_enc[None], grad_dec[None])


def solution(mesh):
    in_specs = (
        P(("dp", "expert"), None),
        P(("dp", "expert"), None),
        P(("dp", "expert"), None),
        P("expert", "dp"),
        P("expert", None, "dp"),
        P("expert", None, "dp"),
    )
    out_specs = (P(("dp", "expert"), None), P("expert", None, "dp"), P("expert", None, "dp"))
    return jax.shard_map(local, mesh=mesh, in_specs=in_specs, out_specs=out_specs, check_vma=False)
```

profile of v0, /device:TPU:0, one launch (start us, length us, event | category | flops | bytes accessed | tf_op | source)
XLA Modules:
  0.0 475.0 jit_solution(13983144485925192504)
XLA Ops:
  7.2 0.9 fusion.10
  8.1 0.2 reduce_window_sum.11
  8.3 0.8 select_reduce_fusion
  9.1 0.7 multiply_add_fusion
  9.8 2.6 convolution_convert_fusion.4
  12.4 40.3 %all-gather.3.cloned.1.call-done = bf16[8,4,24,3072]{3,2,1,0:T(8,128)(2,1)} async-done(((bf16[8,1,24,3072]{3,2,1,0:T(8,128)(2,1)}), bf16[8,4,24,3072]{3,2,1,0:T(8,128)(2,1)}) %all-gather.3.cloned.1.call-update) | async-done | bytes 4718608 | tf_op jit(solution)/shard_map/all_gather | solution.py:29
  52.7 5.5 %all-to-all-start = ((bf16[8,4,24,3072]{3,2,1,0:T(8,128)(2,1)}), bf16[8,4,24,3072]{3,2,1,0:T(8,128)(2,1)}, u32[]{:S(2)}, u32[]{:S(2)}) async-start(bf16[8,4,24,3072]{3,2,1,0:T(8,128)(2,1)} %all-gather.3.cloned.1.call-done), calls=%async_computation | async-start | bytes 9437184 | tf_op jit(solution)/shard_map/all_to_all | solution.py:30
  58.3 104.9 %all-to-all-done = bf16[8,4,24,3072]{3,2,1,0:T(8,128)(2,1)} async-done(((bf16[8,4,24,3072]{3,2,1,0:T(8,128)(2,1)}), bf16[8,4,24,3072]{3,2,1,0:T(8,128)(2,1)}, u32[]{:S(2)}, u32[]{:S(2)}) %all-to-all-start) | async-done | bytes 4718624 | tf_op jit(solution)/shard_map/all_to_all | solution.py:30
  163.2 7.2 %multiply_convert_fusion.2 = (bf16[768,512]{1,0:T(8,128)(2,1)S(1)}, f32[768,512]{1,0:T(8,128)}) fusion(f32[512]{0:T(512)S(1)} %bitcast.62, bf16[768,3072]{1,0:T(8,128)(2,1)} %bitcast.3, bf16[1,3072,512]{2,1,0:T(8,128)(2,1)} %param.10), kind=kOutput, calls=%fused_computation.15 | convolution fusion | flops 2418671616 | bytes 10225664 | tf_op jit(solution)/shard_map/dot_general | solution.py:37
  170.4 0.9 copy-done.5
  171.3 4.4 convolution_convert_fusion
  175.7 0.0 all-gather.5.cloned.1.call-start
  175.7 0.6 copy-done.7
  176.3 0.6 dynamic-slice
  176.9 91.1 %all-reduce.3.cloned.1.call-done = bf16[8,4,24,3072]{3,2,1,0:T(8,128)(2,1)} async-done(((bf16[8,4,24,3072]{3,2,1,0:T(8,128)(2,1)}), bf16[8,4,24,3072]{3,2,1,0:T(8,128)(2,1)}) %all-reduce.3.cloned.1.call-update) | async-done | bytes 4718608
  268.0 2.0 dynamic-slice_bitcast_fusion
  270.0 34.1 %all_to_all.15 = bf16[8,24,3072]{2,1,0:T(8,128)(2,1)S(1)} all-to-all(bf16[8,24,3072]{2,1,0:T(8,128)(2,1)S(1)} %dynamic-slice_bitcast_fusion), channel_id=1, replica_groups=mesh['dp'=4,'expert'=8] {'expert'}, dimensions={0} | all-to-all | bytes 2359296 | tf_op jit(solution)/shard_map/all_to_all | solution.py:51
  304.0 0.4 convolution_convert_fusion.5
  304.5 0.9 copy-done.2
  305.4 1.5 convolution_convert_fusion.3
  306.9 35.8 %all-gather.5.cloned.1.call-done = bf16[8,4,24,3072]{3,2,1,0:T(8,128)(2,1)} async-done(((bf16[8,1,24,3072]{3,2,1,0:T(8,128)(2,1)}), bf16[8,4,24,3072]{3,2,1,0:T(8,128)(2,1)}) %all-gather.5.cloned.1.call-update) | async-done | bytes 4718608 | tf_op jit(solution)/shard_map/all_gather | solution.py:66
  342.7 110.4 %all_to_all.16 = bf16[8,4,24,3072]{3,2,1,0:T(8,128)(2,1)S(1)} all-to-all(bf16[8,4,24,3072]{3,2,1,0:T(8,128)(2,1)} %all-gather.5.cloned.1.call-done), channel_id=1, replica_groups=mesh['dp'=4,'expert'=8] {'expert'}, dimensions={0} | all-to-all | bytes 9437184 | tf_op jit(solution)/shard_map/all_to_all | solution.py:67
  453.1 4.0 fusion.1
  457.2 11.3 %fusion = bf16[1,3072,512]{2,1,0:T(8,128)(2,1)} fusion(bf16[768,3072]{1,0:T(8,128)(2,1)} %bitcast.3, bf16[768,3072]{1,0:T(8,128)(2,1)} %bitcast.56, bf16[1,3072,512]{2,1,0:T(8,128)(2,1)S(1)} %copy-done, f32[768,512]{1,0:T(8,128)} %get-tuple-element.4, f32[512]{0:T(512)S(1)} %bitcast.63), kind=kOutput, calls=%fused_computation.3 | convolution fusion | flops 4837736448 | bytes 17303552 | tf_op jit(solution)/shard_map/dot_general | solution.py:74
  (19 shorter events, 0.2 us)
Async XLA Ops:
  7.2 164.1 %copy-start = (bf16[1,3072,512]{2,1,0:T(8,128)(2,1)S(1)}, bf16[1,3072,512]{2,1,0:T(8,128)(2,1)}, u32[]{:S(2)}) copy-start(bf16[1,3072,512]{2,1,0:T(8,128)(2,1)} %param.11) | copy-start | bytes 9437188
  7.2 45.6 %all-gather.3.cloned.1.call-start = ((), (), s32[]{:S(2)}) async-start(), calls=%async_computation.3 | async-start | bytes 5898240 | tf_op jit(solution)/shard_map/all_gather | solution.py:29
  12.4 45.9 %copy-start.4 = (s32[1,512]{1,0:T(1,128)S(1)}, s32[1,512]{1,0:T(1,128)}, u32[]{:S(2)}) copy-start(s32[1,512]{1,0:T(1,128)} %param.9) | copy-start | bytes 6148
  52.7 110.5 %all-to-all-start = ((bf16[8,4,24,3072]{3,2,1,0:T(8,128)(2,1)}), bf16[8,4,24,3072]{3,2,1,0:T(8,128)(2,1)}, u32[]{:S(2)}, u32[]{:S(2)}) async-start(bf16[8,4,24,3072]{3,2,1,0:T(8,128)(2,1)} %all-gather.3.cloned.1.call-done), calls=%async_computation | async-start | bytes 9437184 | tf_op jit(solution)/shard_map/all_to_all | solution.py:30
  58.2 209.7 %all-reduce.3.cloned.1.call-start = ((), (), s32[]{:S(2)}) async-start(), calls=%async_computation.5 | async-start | bytes 9437184
  170.4 0.9 copy-start.5
  175.6 0.7 copy-start.7
  175.7 167.0 %all-gather.5.cloned.1.call-start = ((), (), s32[]{:S(2)}) async-start(), calls=%async_computation.4 | async-start | bytes 5898240 | tf_op jit(solution)/shard_map/all_gather | solution.py:66
  304.0 1.3 copy-start.3
  304.5 0.9 copy-start.2
  342.7 110.4 %copy-start.6 = (bf16[768,512]{1,0:T(8,128)(2,1)S(1)}, bf16[768,512]{1,0:T(8,128)(2,1)}, u32[]{:S(2)}) copy-start(bf16[768,512]{1,0:T(8,128)(2,1)} %copy-done.5) | copy-start | bytes 2359300
  453.1 4.0 copy-start.1
Sparse Core Ops, SparseCore 0:
  12.5 40.1 all-gather.2
  175.8 92.1 all-reduce.2
  307.0 35.6 all-gather.4
where the time goes:
time: 475 us
  waiting for transfers between devices  272 us (57%)
  blocking collectives  145 us (31%)
  matrix products  31.4 us (7%)
  between operations  13.8 us (3%)
  starting transfers between devices  5.63 us (1%)
  local copies, waits for them, and re-layouts  4.93 us (1%)
    all_to_all x1, blocking collectives, local(): lax.all_to_all(column_errors, 'expert', split_axis=0, concat_axis=0, tile...  110 us
    all_to_all x1, waiting for transfers between devices, local(): lax.all_to_all(column_rows, 'expert', split_axis=0, concat_axis=0, tiled=...  105 us
    unnamed x4, waiting for transfers between devices  91.1 us
    all_gather x1, waiting for transfers between devices, local(): column_rows = lax.all_gather(outbox[:, None], 'dp', axis=1, tiled=True)  40.3 us
    all_gather x1, waiting for transfers between devices, local(): column_errors = lax.all_gather(error_box[:, None], 'dp', axis=1, tiled=True)  35.8 us
    all_to_all x1, blocking collectives, local(): lax.all_to_all(recon_rows, 'expert', split_axis=0, concat_axis=0, tiled=T...  34.1 us
    dot_general x1, matrix products, local(): lax.dot_general(arrived_rows, grad_pre, (((0,), (0,)), ((), ())), preferr...  11.3 us
  transfers between devices with their start and end apart: 4, of which 4 were waited for; matrix products, arithmetic and copies ran while one was open for 0% of the time, Pallas kernels for 0%

commit v1 on v0

v1 whole, which is shorter than its diff:
```python
import functools

import jax
import jax.numpy as jnp
from jax import lax
from jax.experimental import pallas as pl
from jax.experimental.pallas import tpu as pltpu
from jax.sharding import PartitionSpec as P

error_scale = 0.03125
absent_mark = 1024.0
GROUPS = 2
f32 = jnp.float32
bf16 = jnp.bfloat16
VMEM_LIMIT = 60 * 1024 * 1024


def dot(a, b, on_a, on_b):
    return lax.dot_general(a, b, (((on_a,), (on_b,)), ((), ())), preferred_element_type=f32)


def call(kernel, name, out_shape, grid, in_specs, out_specs, scratch, flops, moved):
    return pl.pallas_call(
        kernel,
        name=name,
        out_shape=out_shape,
        grid=grid,
        in_specs=in_specs,
        out_specs=out_specs,
        scratch_shapes=scratch,
        cost_estimate=pl.CostEstimate(flops=flops, bytes_accessed=moved, transcendentals=0),
        compiler_params=pltpu.CompilerParams(
            vmem_limit_bytes=VMEM_LIMIT, dimension_semantics=("arbitrary",) * len(grid)
        ),
    )


def swap(v, distance):
    n = lax.axis_size("dp")
    return lax.ppermute(v, "dp", [(i, i ^ distance) for i in range(n)])


def pass_on(v, distance):
    n = lax.axis_size("expert")
    return lax.ppermute(v, "expert", [(i, i ^ distance) for i in range(n)])


def after(v, *first):
    return lax.optimization_barrier((v,) + first)[0]


def slot_columns(route_col, capacity):
    tokens = route_col.shape[0]
    lanes = lax.broadcasted_iota(jnp.int32, (tokens, 128), 1)
    one_hot = (route_col == lanes).astype(bf16)
    earlier = (
        lax.broadcasted_iota(jnp.int32, (tokens, tokens), 1)
        < lax.broadcasted_iota(jnp.int32, (tokens, tokens), 0)
    ).astype(bf16)
    before = dot(earlier, one_hot, 1, 0)
    rank = jnp.sum(before * one_hot.astype(f32), axis=1, keepdims=True).astype(jnp.int32)
    return route_col * capacity + rank


def place_kernel(experts, capacity, routes_ref, tokens_ref, target_ref, placing_ref, *outs):
    slot = slot_columns(routes_ref[...], capacity)
    tokens = slot.shape[0]
    slots = experts * capacity
    placing = (slot == lax.broadcasted_iota(jnp.int32, (tokens, slots), 1)).astype(f32)
    placing_ref[...] = placing.astype(bf16)
    by_slot = placing.T
    filled = jnp.sum(by_slot, axis=1, keepdims=True)
    by_slot = by_slot.astype(bf16)
    mark = (1.0 - filled) * absent_mark
    rows = dot(by_slot, tokens_ref[...], 1, 0).astype(bf16)
    wanted = (dot(by_slot, target_ref[...], 1, 0) + mark).astype(bf16)
    half = len(outs) // 2
    size = slots // half
    for k in range(half):
        outs[k][...] = rows[k * size : (k + 1) * size]
        outs[half + k][...] = wanted[k * size : (k + 1) * size]


def place(routes, tokens, target, experts, capacity):
    per_dev, features = tokens.shape
    slots = experts * capacity
    pairs = experts // 2
    size = 2 * capacity
    cut = size % 16 == 0
    count, rows = (pairs, size) if cut else (1, slots)
    steps = 2
    cols = lambda rows: pl.BlockSpec((rows, features // steps), lambda i: (0, i))
    whole = lambda *shape: pl.BlockSpec(shape, lambda i: (0, 0))
    outs = call(
        functools.partial(place_kernel, experts, capacity),
        "place",
        [jax.ShapeDtypeStruct((per_dev, slots), bf16)]
        + [jax.ShapeDtypeStruct((rows, features), bf16)] * (2 * count),
        (steps,),
        [whole(per_dev, 1), cols(per_dev), cols(per_dev)],
        [whole(per_dev, slots)] + [cols(rows)] * (2 * count),
        [],
        4 * slots * per_dev * features,
        2 * 2 * (per_dev + slots) * features,
    )(routes, tokens, target)
    boxes, wanted = outs[1 : 1 + count], outs[1 + count :]
    if not cut:
        boxes, wanted = [[v[0][size * k : size * (k + 1)] for k in range(pairs)] for v in (boxes, wanted)]
    return outs[0], boxes, wanted


def forward_kernel(steps, count, *refs):
    blocks = refs[:count]
    thr, enc, dec, act_ref, slope_ref, near_ref, far_ref, send_ref, pre = refs[count:]
    i = pl.program_id(0)
    size = act_ref.shape[0] // 4

    @pl.when(i < steps)
    def _():
        x = jnp.concatenate([b[...] for b in blocks], axis=0)
        part = dot(x, enc[...], 1, 0)

        @pl.when(i == 0)
        def _():
            pre[...] = part

        @pl.when(i > 0)
        def _():
            pre[...] += part

    @pl.when(i == steps - 1)
    def _():
        latent = pre[...] - 0.25 * thr[...].astype(f32)
        squash = jax.nn.sigmoid(4.0 * latent)
        act_ref[...] = (latent * squash).astype(bf16)
        slope_ref[...] = squash + 4.0 * latent * squash * (1.0 - squash)

    @pl.when(i >= steps)
    def _():
        part = dot(act_ref[...], dec[...], 1, 1)
        near_ref[...] = part[:size]
        send_ref[:size] = part[size : 2 * size].astype(bf16)
        far_ref[...] = part[2 * size : 3 * size]
        send_ref[size:] = part[3 * size :].astype(bf16)


def forward(blocks, thresholds, enc, dec):
    count = len(blocks)
    features = blocks[0].shape[1]
    size = sum(b.shape[0] for b in blocks) // 4
    latents = enc.shape[1]
    steps = 2
    wide = features // steps
    early = lambda i: jnp.minimum(i, steps - 1)
    late = lambda i: jnp.maximum(i - steps, 0)
    fixed = lambda *shape: pl.BlockSpec(shape, lambda i: (0, 0))
    col_out = lambda rows: pl.BlockSpec((rows, wide), lambda i: (0, late(i)))
    return call(
        functools.partial(forward_kernel, steps, count),
        "forward",
        [
            jax.ShapeDtypeStruct((4 * size, latents), bf16),
            jax.ShapeDtypeStruct((4 * size, latents), f32),
            jax.ShapeDtypeStruct((size, features), f32),
            jax.ShapeDtypeStruct((size, features), f32),
            jax.ShapeDtypeStruct((2 * size, features), bf16),
        ],
        (2 * steps,),
        [pl.BlockSpec((b.shape[0], wide), lambda i: (0, early(i))) for b in blocks]
        + [
            fixed(1, latents),
            pl.BlockSpec((wide, latents), lambda i: (early(i), 0)),
            pl.BlockSpec((wide, latents), lambda i: (late(i), 0)),
        ],
        [fixed(4 * size, latents), fixed(4 * size, latents), col_out(size), col_out(size), col_out(2 * size)],
        [pltpu.VMEM((4 * size, latents), f32)],
        2 * 2 * 4 * size * features * latents,
        4 * features * latents + 24 * size * features,
    )(*blocks, thresholds, enc, dec)


def make_error(near, got, across, wanted):
    recon = (near + got.astype(f32) + across.astype(f32)).astype(bf16)
    goal = wanted.astype(f32)
    error = (recon.astype(f32) - goal) * error_scale
    return recon, jnp.where(goal < 0.5 * absent_mark, error, 0.0).astype(bf16)


def back_kernel(steps, e0, e1, e2, e3, dec, slope, out_ref, total):
    i = pl.program_id(0)
    e = jnp.concatenate([e0[...], e1[...], e2[...], e3[...]], axis=0)
    part = dot(e, dec[...], 1, 0)

    @pl.when(i == 0)
    def _():
        total[...] = part

    @pl.when(i > 0)
    def _():
        total[...] += part

    @pl.when(i == steps - 1)
    def _():
        out_ref[...] = (total[...] * slope[...]).astype(bf16)


def back(errors, dec, slope):
    size, features = errors[0].shape
    latents = dec.shape[1]
    steps = 2
    wide = features // steps
    fixed = pl.BlockSpec((4 * size, latents), lambda i: (0, 0))
    return call(
        functools.partial(back_kernel, steps),
        "back",
        jax.ShapeDtypeStruct((4 * size, latents), bf16),
        (steps,),
        [pl.BlockSpec((size, wide), lambda i: (0, i))] * 4
        + [pl.BlockSpec((wide, latents), lambda i: (i, 0)), fixed],
        fixed,
        [pltpu.VMEM((4 * size, latents), f32)],
        2 * 4 * size * features * latents,
        2 * features * latents + 8 * size * features,
    )(*errors, dec, slope)


def weight_grad_kernel(count, *refs):
    blocks = refs[:count]
    sides = refs[count : count + GROUPS]
    out_ref = refs[-1]
    left = jnp.concatenate([b[...] for b in blocks], axis=0)
    right = jnp.concatenate([s[...] for s in sides], axis=0)
    out_ref[0] = dot(left, right, 0, 0).astype(bf16)


def weight_grad(name, blocks, sides):
    features = blocks[0].shape[1]
    size = sum(b.shape[0] for b in blocks)
    latents = sides[0].shape[1]
    wide = features // 3
    return call(
        functools.partial(weight_grad_kernel, len(blocks)),
        name,
        jax.ShapeDtypeStruct((1, features, latents), bf16),
        (features // wide,),
        [pl.BlockSpec((b.shape[0], wide), lambda i: (0, i)) for b in blocks]
        + [pl.BlockSpec(s.shape, lambda i: (0, 0)) for s in sides],
        pl.BlockSpec((1, wide, latents), lambda i: (0, i, 0)),
        [],
        2 * size * features * latents,
        2 * features * latents + 2 * size * features,
    )(*blocks, *sides)


def collect_kernel(capacity, count, placing, *refs):
    out = refs[-1]
    came = jnp.concatenate([r[...] for r in refs[:count]], axis=0)
    passed = jnp.concatenate([r[...] for r in refs[count:-1]], axis=0)
    tokens, slots = placing.shape
    lane = lax.broadcasted_iota(jnp.int32, (tokens, slots), 1)
    direct = jnp.where((lane // capacity) % 2 == 0, placing[...], jnp.zeros((), bf16))
    picks = lax.broadcasted_iota(jnp.int32, (slots, slots // 2), 0)
    place = lax.broadcasted_iota(jnp.int32, (slots, slots // 2), 1)
    source = (place // capacity) * 2 * capacity + capacity + place % capacity
    via = dot(placing[...], (picks == source).astype(bf16), 1, 0).astype(bf16)
    out[...] = (dot(direct, came, 1, 0) + dot(via, passed, 1, 0)).astype(bf16)


def collect(placing, came, passed, capacity):
    tokens, slots = placing.shape
    features = came[0].shape[1]
    steps = 2
    wide = features // steps
    cols = lambda rows: pl.BlockSpec((rows, wide), lambda i: (0, i))
    return call(
        functools.partial(collect_kernel, capacity, len(came)),
        "collect",
        jax.ShapeDtypeStruct((tokens, features), bf16),
        (steps,),
        [pl.BlockSpec((tokens, slots), lambda i: (0, 0))] + [cols(v.shape[0]) for v in came + passed],
        cols(tokens),
        [],
        3 * slots * tokens * features,
        2 * (2 * slots + tokens) * features,
    )(placing, *came, *passed)


def local(tokens, target, routes, thresholds, enc_weight, dec_weight):
    experts = lax.axis_size("expert")
    half = lax.axis_size("dp") // 2
    per_dev, features = tokens.shape
    capacity = 3 * per_dev // (2 * experts)
    enc = enc_weight[0]
    dec = dec_weight[0]
    pairs = experts // 2
    own = lax.axis_index("expert")
    placing, box, wanted_box = place(routes ^ own, tokens, target, experts, capacity)

    def outer(v, k):
        return v if k == 0 else pass_on(v, 2 * k)

    def join(arrays):
        return arrays[0] if len(arrays) == 1 else jnp.concatenate(arrays, axis=0)

    def settle(landed, *first):
        direct = [v[:capacity] for v in landed]
        via = pass_on(after(join([v[capacity:] for v in landed]), *first), 1)
        return join([v for j, d in enumerate(direct) for v in (d, via[j * capacity : (j + 1) * capacity])])

    def gather(mine):
        far = swap(mine, half)
        return [mine, swap(mine, 1), far, swap(far, 1)]

    quarter = pairs // 4
    spans = [(0, quarter), (quarter, 2 * quarter), (2 * quarter, pairs)]
    landed = [outer(box[k], k) for k in range(pairs)]
    blocks = []
    first = []
    for low, high in spans:
        mine = settle(landed[low:high], *first)
        blocks.append(gather(mine))
        first = [blocks[-1][2]]

    goal_start = (blocks[1][2], *landed[1:])
    aims = [outer(after(wanted_box[k], *goal_start), k) for k in range(pairs)]

    rows = [[b for r in range(4) for b in (blocks[0][r], blocks[1][r])], blocks[2]]
    first = blocks[2][0]
    acts, slopes, nears, gots, acrosses, sums = [], [], [], [], [], []
    for g in range(GROUPS):
        ready = [after(rows[g][0], first)] + rows[g][1:]
        act, slope, near, far, send = forward(ready, thresholds, enc, dec)
        got = swap(send, 1)
        size = near.shape[0]
        first = (far + got[size:].astype(f32)).astype(bf16)
        acts.append(act)
        slopes.append(slope)
        nears.append(near)
        gots.append(got[:size])
        sums.append(first)
        acrosses.append(swap(first, half))

    spans = [(0, 2 * quarter), (2 * quarter, pairs)]
    errors, homes = [], []
    first = (acts[1], blocks[2][3])
    for g, (low, high) in enumerate(spans):
        wanted = settle(aims[low:high], acts[0])
        recon, error = make_error(nears[g], gots[g], after(acrosses[g], *first), wanted)
        homes += [outer(recon[2 * capacity * j : 2 * capacity * (j + 1)], low + j) for j in range(high - low)]
        errors.append(gather(error))
        first = (error,)

    grad_pres = []
    first = errors[1][0]
    for g in range(GROUPS):
        ready = [after(errors[g][0], first)] + errors[g][1:]
        grad_pres.append(back(ready, dec, slopes[g]))
        first = grad_pres[-1]
    passed = []
    for (low, high), first in zip(spans, (errors[1][0], grad_pres[1])):
        passed.append(pass_on(after(join([v[capacity:] for v in homes[low:high]]), first), 1))
    came = [join(homes[i * quarter : (i + 1) * quarter]) for i in range(4)]
    flat = lambda groups: [b for group in groups for b in group]
    grad_dec = weight_grad("grad_dec", flat(errors), acts)
    grad_enc = weight_grad("grad_enc", flat(rows), grad_pres)
    recon = collect(after(placing, grad_enc), came, passed, capacity)
    return recon, grad_enc, grad_dec


def solution(mesh):
    in_specs = (
        P(("dp", "expert"), None),
        P(("dp", "expert"), None),
        P(("dp", "expert"), None),
        P("expert", "dp"),
        P("expert", None, "dp"),
        P("expert", None, "dp"),
    )
    out_specs = (P(("dp", "expert"), None), P("expert", None, "dp"), P("expert", None, "dp"))
    return jax.shard_map(local, mesh=mesh, in_specs=in_specs, out_specs=out_specs, check_vma=False)
```

time: 475 us -> 178 us (0.37)
  waiting for transfers between devices: 272 us -> 87 us
  blocking collectives: 145 us -> 0 us
  Pallas kernels: 0 us -> 46.7 us
  matrix products: 31.4 us -> 0 us
  starting transfers between devices: 5.63 us -> 31 us
  between operations: 13.8 us -> 1.12 us
    all_to_all x2 -> x0, blocking collectives: 145 us -> none  [the longest x1 110 us: local(): lax.all_to_all(column_errors, 'expert', split_axis=0, concat_axis=0, tile...]
    all_to_all x1 -> x0, waiting for transfers between devices: 105 us -> none  [local(): lax.all_to_all(column_rows, 'expert', split_axis=0, concat_axis=0, tiled=...]
    unnamed x4 -> x0, waiting for transfers between devices: 91.1 us -> none
    ppermute x0 -> x35, waiting for transfers between devices: none -> 87 us  [the longest x16 53.2 us: pass_on(): return lax.ppermute(v, 'expert', [(i, i ^ distance) for i in range(n)])]
    all_gather x2 -> x0, waiting for transfers between devices: 76.1 us -> none  [the longest x1 40.3 us: local(): column_rows = lax.all_gather(outbox[:, None], 'dp', axis=1, tiled=True)]
    pallas_call x0 -> x8, Pallas kernels: none -> 46.7 us  [the longest x2 16.9 us: forward(): call(functools.partial(forward_kernel, steps, count), 'forward', [jax.Sha...]
    dot_general x7 -> x0, matrix products: 31.4 us -> none  [the longest x1 11.3 us: local(): lax.dot_general(arrived_rows, grad_pre, (((0,), (0,)), ((), ())), preferr...]
    ppermute x0 -> x35, starting transfers between devices: none -> 31 us  [the longest x16 22.6 us: pass_on(): return lax.ppermute(v, 'expert', [(i, i ^ distance) for i in range(n)])]
  transfers between devices with their start and end apart: 4 -> 35, of which waited for: 4 -> 14; matrix products, arithmetic and copies ran while one was open for 0% -> 4% of each run, Pallas kernels for 0% -> 22%
where the time goes in v1:
time: 178 us
  waiting for transfers between devices  87 us (49%)
  Pallas kernels  46.7 us (26%)
  starting transfers between devices  31 us (17%)
  local copies, waits for them, and re-layouts  7.32 us (4%)
  other arithmetic  4.53 us (3%)
    ppermute x16, waiting for transfers between devices, pass_on(): return lax.ppermute(v, 'expert', [(i, i ^ distance) for i in range(n)])  53.2 us
    ppermute x19, waiting for transfers between devices, swap(): return lax.ppermute(v, 'dp', [(i, i ^ distance) for i in range(n)])  33.8 us
    ppermute x16, starting transfers between devices, pass_on(): return lax.ppermute(v, 'expert', [(i, i ^ distance) for i in range(n)])  22.6 us
    pallas_call x2, Pallas kernels, forward(): call(functools.partial(forward_kernel, steps, count), 'forward', [jax.Sha...  16.9 us
    pallas_call x2, Pallas kernels, weight_grad(): call(functools.partial(weight_grad_kernel, len(blocks)), name, jax.ShapeD...  13.5 us
    pallas_call x2, Pallas kernels, back(): call(functools.partial(back_kernel, steps), 'back', jax.ShapeDtypeStruct(...  9.39 us
    ppermute x19, starting transfers between devices, swap(): return lax.ppermute(v, 'dp', [(i, i ^ distance) for i in range(n)])  8.43 us
    pallas_call x1, Pallas kernels, place(): call(functools.partial(place_kernel, experts, capacity), 'place', [jax.Sh...  3.82 us
  transfers between devices with their start and end apart: 35, of which 14 were waited for; matrix products, arithmetic and copies ran while one was open for 4% of the time, Pallas kernels for 22%

profile of v1, /device:TPU:0, one launch (start us, length us, event | category | flops | bytes accessed | tf_op | source)
XLA Modules:
  0.0 177.8 jit_solution(9541961715527839882)
XLA Ops:
  2.0 3.8 %place.1 = (bf16[128,192]{1,0:T(8,128)(2,1)}, bf16[48,3072]{1,0:T(8,128)(2,1)}, bf16[48,3072]{1,0:T(8,128)(2,1)}, bf16[48,3072]{1,0:T(8,128)(2,1)}, bf16[48,3072...) custom-call(s32[128,1]{1,0:T(8,128)} %broadcast_xor_fusion.routes_re, ...), custom_call_target="tpu_custom_call" | custom-call | flops 301989888 | bytes 3932160 | tf_op jit(solution)/shard_map/place/pallas_call | solution.py:94
  6.8 3.0 %collective-permute-start = (bf16[24,3072]{1,0:T(8,128)(2,1)S(1)}, bf16[24,3072]{1,0:T(8,128)(2,1)S(1)}, u32[]{:S(2)}, u32[]{:S(2)}) collective-permute-start(bf16[24,3072]{1,0:T(8,128)(2,1)S(1)} %get-tuple-element.104), channel_id=1, source_target_pairs={{0,1},{1,0},{2,3},{3,2},{4,5},{5,4},{6,7},{7,6},{8,9},{9,8},{10,11... | collective-permute-start | bytes 442376 | tf_op jit(solution)/shard_map/ppermute | solution.py:45
  11.5 2.6 %collective-permute-start.9 = (bf16[48,3072]{1,0:T(8,128)(2,1)}, bf16[48,3072]{1,0:T(8,128)(2,1)S(1)}, u32[]{:S(2)}, u32[]{:S(2)}) collective-permute-start(bf16[48,3072]{1,0:T(8,128)(2,1)} %get-tuple-element.43), channel_id=1, source_target_pairs={{0,4},{1,5},{2,6},{3,7},{4,0},{5,1},{6,2},{7,3},{8,12},{9,13},{10,... | collective-permute-start | bytes 884744 | tf_op jit(solution)/shard_map/ppermute | solution.py:45
  16.0 8.0 %collective-permute-done.1 = bf16[48,3072]{1,0:T(8,128)(2,1)S(1)} collective-permute-done((bf16[48,3072]{1,0:T(8,128)(2,1)}, bf16[48,3072]{1,0:T(8,128)(2,1)S(1)}, u32[]{:S(2)}, u32[]{:S(2)}) %collective-permute-start.1) | collective-permute-done | bytes 294944 | tf_op jit(solution)/shard_map/ppermute | solution.py:45
  24.0 11.2 %collective-permute-done.9 = bf16[48,3072]{1,0:T(8,128)(2,1)S(1)} collective-permute-done((bf16[48,3072]{1,0:T(8,128)(2,1)}, bf16[48,3072]{1,0:T(8,128)(2,1)S(1)}, u32[]{:S(2)}, u32[]{:S(2)}) %collective-permute-start.9) | collective-permute-done | bytes 294944 | tf_op jit(solution)/shard_map/ppermute | solution.py:45
  35.8 4.6 %collective-permute-done.3 = bf16[24,3072]{1,0:T(8,128)(2,1)S(1)} collective-permute-done((bf16[24,3072]{1,0:T(8,128)(2,1)S(1)}, bf16[24,3072]{1,0:T(8,128)(2,1)S(1)}, u32[]{:S(2)}, u32[]{:S(2)}) %collective-permute-start.3) | collective-permute-done | bytes 147488 | tf_op jit(solution)/shard_map/ppermute | solution.py:45
  42.6 4.6 %collective-permute-done.6.refs_5_ = bf16[48,3072]{1,0:T(8,128)(2,1)S(1)} collective-permute-done((bf16[48,3072]{1,0:T(8,128)(2,1)S(1)}, bf16[48,3072]{1,0:T(8,128)(2,1)S(1)}, u32[]{:S(2)}, u32[]{:S(2)}) %collective-permute-start.6) | collective-permute-done | bytes 294944 | tf_op jit(solution)/shard_map/ppermute | solution.py:40
  47.8 2.5 %collective-permute-start.20 = (bf16[48,3072]{1,0:T(8,128)(2,1)}, bf16[48,3072]{1,0:T(8,128)(2,1)S(1)}, u32[]{:S(2)}, u32[]{:S(2)}) collective-permute-start(bf16[48,3072]{1,0:T(8,128)(2,1)} %get-tuple-element.62), channel_id=1, source_target_pairs={{0,6},{1,7},{2,4},{3,5},{4,2},{5,3},{6,0},{7,1},{8,14},{9,15},{10,... | collective-permute-start | bytes 884744 | tf_op jit(solution)/shard_map/ppermute | solution.py:45
  50.3 3.6 %collective-permute-done.11 = bf16[48,3072]{1,0:T(8,128)(2,1)S(1)} collective-permute-done((bf16[48,3072]{1,0:T(8,128)(2,1)S(1)}, bf16[48,3072]{1,0:T(8,128)(2,1)S(1)}, u32[]{:S(2)}, u32[]{:S(2)}) %collective-permute-start.11) | collective-permute-done | bytes 294944 | tf_op jit(solution)/shard_map/ppermute | solution.py:45
  54.7 2.5 %collective-permute-start.19 = (bf16[48,3072]{1,0:T(8,128)(2,1)}, bf16[48,3072]{1,0:T(8,128)(2,1)S(1)}, u32[]{:S(2)}, u32[]{:S(2)}) collective-permute-start(bf16[48,3072]{1,0:T(8,128)(2,1)} %get-tuple-element.60), channel_id=1, source_target_pairs={{0,4},{1,5},{2,6},{3,7},{4,0},{5,1},{6,2},{7,3},{8,12},{9,13},{10,... | collective-permute-start | bytes 884744 | tf_op jit(solution)/shard_map/ppermute | solution.py:45
  59.4 8.4 %forward.2 = (bf16[384,512]{1,0:T(8,128)(2,1)}, f32[384,512]{1,0:T(8,128)}, f32[96,3072]{1,0:T(8,128)}, f32[96,3072]{1,0:T(8,128)}, bf16[192,3072]{1,0:T(8,128)(2,1)}) custom-call(bf16[48,3072]{1,0:T(8,128)(2,1)} %copy-done.16, bf16[48,3072]{1,0:T(8,128)(2,1)} %copy-done.17, bf16[48,3072]{1,0:T(8,128)(2,1)} %copy-done.19, bf16[48,3072]{1,0:T(8,128)(2,1)} %copy-done.23, ...), custom_call_target="tpu_custom_call" | custom-call | flops 2415919104 | bytes 13369344 | tf_op jit(solution)/shard_map/forward/pallas_call | solution.py:158
  68.4 4.6 %collective-permute-done.19 = bf16[48,3072]{1,0:T(8,128)(2,1)S(1)} collective-permute-done((bf16[48,3072]{1,0:T(8,128)(2,1)}, bf16[48,3072]{1,0:T(8,128)(2,1)S(1)}, u32[]{:S(2)}, u32[]{:S(2)}) %collective-permute-start.19) | collective-permute-done | bytes 294944 | tf_op jit(solution)/shard_map/ppermute | solution.py:45
  76.6 6.4 %collective-permute-done.16 = bf16[48,3072]{1,0:T(8,128)(2,1)S(1)} collective-permute-done((bf16[48,3072]{1,0:T(8,128)(2,1)S(1)}, bf16[48,3072]{1,0:T(8,128)(2,1)S(1)}, u32[]{:S(2)}, u32[]{:S(2)}) %collective-permute-start.16) | collective-permute-done | bytes 294944 | tf_op jit(solution)/shard_map/ppermute | solution.py:45
  83.1 8.4 %forward.3 = (bf16[384,512]{1,0:T(8,128)(2,1)}, f32[384,512]{1,0:T(8,128)}, f32[96,3072]{1,0:T(8,128)}, f32[96,3072]{1,0:T(8,128)}, bf16[192,3072]{1,0:T(8,128)(2,1)}) custom-call(bf16[96,3072]{1,0:T(8,128)(2,1)} %copy-done.13, bf16[96,3072]{1,0:T(8,128)(2,1)} %collective-permute-done.12.refs_1_.refs_9_, ...), custom_call_target="tpu_custom_call" | custom-call | flops 2415919104 | bytes 13369344 | tf_op jit(solution)/shard_map/forward/pallas_call | solution.py:158
  97.8 5.4 %collective-permute-done.30.refs_1_ = bf16[48,3072]{1,0:T(8,128)(2,1)S(1)} collective-permute-done((bf16[48,3072]{1,0:T(8,128)(2,1)S(1)}, bf16[48,3072]{1,0:T(8,128)(2,1)S(1)}, u32[]{:S(2)}, u32[]{:S(2)}) %collective-permute-start.30) | collective-permute-done | bytes 294944 | tf_op jit(solution)/shard_map/ppermute | solution.py:45
  103.2 7.4 %collective-permute-done.25.e2.refs_2_ = bf16[96,3072]{1,0:T(8,128)(2,1)S(1)} collective-permute-done((bf16[96,3072]{1,0:T(8,128)(2,1)S(1)}, bf16[96,3072]{1,0:T(8,128)(2,1)S(1)}, u32[]{:S(2)}, u32[]{:S(2)}) %collective-permute-start.25) | collective-permute-done | bytes 589856 | tf_op jit(solution)/shard_map/ppermute | solution.py:40
  110.6 11.6 %collective-permute-done.23 = bf16[96,3072]{1,0:T(8,128)(2,1)S(1)} collective-permute-done((bf16[96,3072]{1,0:T(8,128)(2,1)S(1)}, bf16[96,3072]{1,0:T(8,128)(2,1)S(1)}, u32[]{:S(2)}, u32[]{:S(2)}) %collective-permute-start.23) | collective-permute-done | bytes 589856 | tf_op jit(solution)/shard_map/ppermute | solution.py:40
  127.3 9.6 %collective-permute-done.28.e2.refs_6_ = bf16[96,3072]{1,0:T(8,128)(2,1)S(1)} collective-permute-done((bf16[96,3072]{1,0:T(8,128)(2,1)S(1)}, bf16[96,3072]{1,0:T(8,128)(2,1)S(1)}, u32[]{:S(2)}, u32[]{:S(2)}) %collective-permute-start.28) | collective-permute-done | bytes 589856 | tf_op jit(solution)/shard_map/ppermute | solution.py:40
  138.6 4.7 %back.2.refs_12_ = bf16[384,512]{1,0:T(8,128)(2,1)} custom-call(bf16[96,3072]{1,0:T(8,128)(2,1)} %copy-done, bf16[96,3072]{1,0:T(8,128)(2,1)} %copy-done.10, bf16[96,3072]{1,0:T(8,128)(2,1)} %copy-done.9, bf16[96,3072]{1,0:T(8,128)(2,1)} %copy-done.11, bf16[3072,512]{1,0:T(8,128)(2,1)} %bitcast.4, f32[384,512]{1,0:T(8,128)} %get-tuple-element.69.slope), custom_call_target="tpu_custom_call" | custom-call | flops 1207959552 | bytes 5505024 | tf_op jit(solution)/shard_map/back/pallas_call | solution.py:213
  144.9 9.0 %collective-permute-done.31.refs_2_ = bf16[48,3072]{1,0:T(8,128)(2,1)S(1)} collective-permute-done((bf16[48,3072]{1,0:T(8,128)(2,1)}, bf16[48,3072]{1,0:T(8,128)(2,1)S(1)}, u32[]{:S(2)}, u32[]{:S(2)}) %collective-permute-start.31) | collective-permute-done | bytes 294944 | tf_op jit(solution)/shard_map/ppermute | solution.py:45
  153.9 4.7 %back.3.refs_13_ = bf16[384,512]{1,0:T(8,128)(2,1)} custom-call(bf16[96,3072]{1,0:T(8,128)(2,1)} %copy-done.1, bf16[96,3072]{1,0:T(8,128)(2,1)} %collective-permute-done.27.e1.refs_5_, bf16[96,3072]{1,0:T(8,128)(2,1)} %copy-done.12, bf16[96,3072]{1,0:T(8,128)(2,1)} %collective-permute-done.29.e3.refs_7_, bf16[3072,512]{1,0:T(8,128)(2,1)} %bitcast.5, ...), custom_call_target="tpu_custom_call" | custom-call | flops 1207959552 | bytes 5505024 | tf_op jit(solution)/shard_map/back/pallas_call | solution.py:213
  160.2 6.8 %grad_enc.1 = bf16[1,3072,512]{2,1,0:T(8,128)(2,1)} custom-call(bf16[48,3072]{1,0:T(8,128)(2,1)} %copy-done.16, bf16[48,3072]{1,0:T(8,128)(2,1)} %copy-done.17, bf16[48,3072]{1,0:T(8,128)(2,1)} %copy-done.19, bf16[48,3072]{1,0:T(8,128)(2,1)} %copy-done.23, bf16[48,3072]{1,0:T(8,128)(2,1)} %copy-done.20, bf16[48,3072]{1,0:T(8,128)(2,1)} %copy-done.21, ...), custom_call_target="tpu_custom_call" | custom-call | flops 2415919104 | bytes 7864320 | tf_op jit(solution)/shard_map/grad_enc/pallas_call | solution.py:241
  167.0 6.8 %grad_dec.1 = bf16[1,3072,512]{2,1,0:T(8,128)(2,1)} custom-call(bf16[96,3072]{1,0:T(8,128)(2,1)} %copy-done, bf16[96,3072]{1,0:T(8,128)(2,1)} %copy-done.10, bf16[96,3072]{1,0:T(8,128)(2,1)} %copy-done.9, bf16[96,3072]{1,0:T(8,128)(2,1)} %copy-done.11, bf16[96,3072]{1,0:T(8,128)(2,1)} %copy-done.1, bf16[96,3072]{1,0:T(8,128)(2,1)} %collective-permute-done.27.e1.refs_5_, ...), custom_call_target="tpu_custom_call" | custom-call | flops 2415919104 | bytes 7864320 | tf_op jit(solution)/shard_map/grad_dec/pallas_call | solution.py:241
  174.6 3.1 %collect.1 = bf16[128,3072]{1,0:T(8,128)(2,1)} custom-call(bf16[128,192]{1,0:T(8,128)(2,1)} %get-tuple-element.72.placing, bf16[48,3072]{1,0:T(8,128)(2,1)} %get-tuple-element.82.refs_0_, bf16[48,3072]{1,0:T(8,128)(2,1)} %copy-done.6, bf16[48,3072]{1,0:T(8,128)(2,1)} %copy-done.8, bf16[48,3072]{1,0:T(8,128)(2,1)} %copy-done.7, bf16[48,3072]{1,0:T(8,128)(2,1)} %copy-done.14, ...), custom_call_target="tpu_custom_call" | custom-call | flops 226492416 | bytes 3145728 | tf_op jit(solution)/shard_map/collect/pallas_call | solution.py:275
  (136 shorter events, 33.3 us)
Async XLA Ops:
  9.9 14.1 %collective-permute-start.1 = (bf16[48,3072]{1,0:T(8,128)(2,1)}, bf16[48,3072]{1,0:T(8,128)(2,1)S(1)}, u32[]{:S(2)}, u32[]{:S(2)}) collective-permute-start(bf16[48,3072]{1,0:T(8,128)(2,1)} %get-tuple-element.41), channel_id=1, source_target_pairs={{0,2},{1,3},{2,0},{3,1},{4,6},{5,7},{6,4},{7,5},{8,10},{9,11},{10,... | collective-permute-start | bytes 884744 | tf_op jit(solution)/shard_map/ppermute | solution.py:45
  11.5 23.7 %collective-permute-start.9 = (bf16[48,3072]{1,0:T(8,128)(2,1)}, bf16[48,3072]{1,0:T(8,128)(2,1)S(1)}, u32[]{:S(2)}, u32[]{:S(2)}) collective-permute-start(bf16[48,3072]{1,0:T(8,128)(2,1)} %get-tuple-element.43), channel_id=1, source_target_pairs={{0,4},{1,5},{2,6},{3,7},{4,0},{5,1},{6,2},{7,3},{8,12},{9,13},{10,... | collective-permute-start | bytes 884744 | tf_op jit(solution)/shard_map/ppermute | solution.py:45
  14.0 21.7 %collective-permute-start.10 = (bf16[48,3072]{1,0:T(8,128)(2,1)}, bf16[48,3072]{1,0:T(8,128)(2,1)S(1)}, u32[]{:S(2)}, u32[]{:S(2)}) collective-permute-start(bf16[48,3072]{1,0:T(8,128)(2,1)} %get-tuple-element.44), channel_id=1, source_target_pairs={{0,6},{1,7},{2,4},{3,5},{4,2},{5,3},{6,0},{7,1},{8,14},{9,15},{10,... | collective-permute-start | bytes 884744 | tf_op jit(solution)/shard_map/ppermute | solution.py:45
  14.3 39.8 %collective-permute-start.4 = (bf16[48,3072]{1,0:T(8,128)(2,1)S(1)}, bf16[48,3072]{1,0:T(8,128)(2,1)S(1)}, u32[]{:S(2)}, u32[]{:S(2)}) collective-permute-start(bf16[48,3072]{1,0:T(8,128)(2,1)S(1)} %pad_maximum_fusion.1.refs_0_), channel_id=1, source_target_pairs={{0,8},{8,0},{16,24},{24,16},{1,9},{9,1},{17,25},{25,17},{2,10},{10... | collective-permute-start | bytes 884744 | tf_op jit(solution)/shard_map/ppermute | solution.py:40
  14.4 20.8 %collective-permute-start.2 = (bf16[48,3072]{1,0:T(8,128)(2,1)S(1)}, bf16[48,3072]{1,0:T(8,128)(2,1)S(1)}, u32[]{:S(2)}, u32[]{:S(2)}) collective-permute-start(bf16[48,3072]{1,0:T(8,128)(2,1)S(1)} %pad_maximum_fusion.1.refs_0_), channel_id=1, source_target_pairs={{0,16},{8,24},{16,0},{24,8},{1,17},{9,25},{17,1},{25,9},{2,18},{10... | collective-permute-start | bytes 884744 | tf_op jit(solution)/shard_map/ppermute | solution.py:40
  42.1 15.1 %collective-permute-start.5 = (bf16[48,3072]{1,0:T(8,128)(2,1)S(1)}, bf16[48,3072]{1,0:T(8,128)(2,1)S(1)}, u32[]{:S(2)}, u32[]{:S(2)}) collective-permute-start(bf16[48,3072]{1,0:T(8,128)(2,1)S(1)} %pad_maximum_fusion.2.refs_1_), channel_id=1, source_target_pairs={{0,8},{8,0},{16,24},{24,16},{1,9},{9,1},{17,25},{25,17},{2,10},{10... | collective-permute-start | bytes 884744 | tf_op jit(solution)/shard_map/ppermute | solution.py:40
  47.8 20.1 %collective-permute-start.20 = (bf16[48,3072]{1,0:T(8,128)(2,1)}, bf16[48,3072]{1,0:T(8,128)(2,1)S(1)}, u32[]{:S(2)}, u32[]{:S(2)}) collective-permute-start(bf16[48,3072]{1,0:T(8,128)(2,1)} %get-tuple-element.62), channel_id=1, source_target_pairs={{0,6},{1,7},{2,4},{3,5},{4,2},{5,3},{6,0},{7,1},{8,14},{9,15},{10,... | collective-permute-start | bytes 884744 | tf_op jit(solution)/shard_map/ppermute | solution.py:45
  54.1 14.3 %collective-permute-start.15 = (bf16[48,3072]{1,0:T(8,128)(2,1)}, bf16[48,3072]{1,0:T(8,128)(2,1)S(1)}, u32[]{:S(2)}, u32[]{:S(2)}) collective-permute-start(bf16[48,3072]{1,0:T(8,128)(2,1)} %get-tuple-element.49), channel_id=1, source_target_pairs={{0,2},{1,3},{2,0},{3,1},{4,6},{5,7},{6,4},{7,5},{8,10},{9,11},{10,... | collective-permute-start | bytes 884744 | tf_op jit(solution)/shard_map/ppermute | solution.py:45
  54.7 18.2 %collective-permute-start.19 = (bf16[48,3072]{1,0:T(8,128)(2,1)}, bf16[48,3072]{1,0:T(8,128)(2,1)S(1)}, u32[]{:S(2)}, u32[]{:S(2)}) collective-permute-start(bf16[48,3072]{1,0:T(8,128)(2,1)} %get-tuple-element.60), channel_id=1, source_target_pairs={{0,4},{1,5},{2,6},{3,7},{4,0},{5,1},{6,2},{7,3},{8,12},{9,13},{10,... | collective-permute-start | bytes 884744 | tf_op jit(solution)/shard_map/ppermute | solution.py:45
  57.2 17.9 %collective-permute-start.13 = (bf16[96,3072]{1,0:T(8,128)(2,1)S(1)}, bf16[96,3072]{1,0:T(8,128)(2,1)}, u32[]{:S(2)}, u32[]{:S(2)}) collective-permute-start(bf16[96,3072]{1,0:T(8,128)(2,1)S(1)} %pad_maximum_fusion.refs_0_.refs_8_), channel_id=1, source_target_pairs={{0,16},{8,24},{16,0},{24,8},{1,17},{9,25},{17,1},{25,9},{2,18},{10... | collective-permute-start | bytes 1769480 | tf_op jit(solution)/shard_map/ppermute | solution.py:40
  58.7 24.4 %collective-permute-start.12 = (bf16[96,3072]{1,0:T(8,128)(2,1)S(1)}, bf16[96,3072]{1,0:T(8,128)(2,1)}, u32[]{:S(2)}, u32[]{:S(2)}) collective-permute-start(bf16[96,3072]{1,0:T(8,128)(2,1)S(1)} %pad_maximum_fusion.refs_0_.refs_8_), channel_id=1, source_target_pairs={{0,8},{8,0},{16,24},{24,16},{1,9},{9,1},{17,25},{25,17},{2,10},{10... | collective-permute-start | bytes 1769480 | tf_op jit(solution)/shard_map/ppermute | solution.py:40
  74.6 22.0 %collective-permute-start.21 = (bf16[48,3072]{1,0:T(8,128)(2,1)S(1)}, bf16[48,3072]{1,0:T(8,128)(2,1)}, u32[]{:S(2)}, u32[]{:S(2)}) collective-permute-start(bf16[48,3072]{1,0:T(8,128)(2,1)S(1)} %pad_maximum_fusion.5), channel_id=1, source_target_pairs={{0,1},{1,0},{2,3},{3,2},{4,5},{5,4},{6,7},{7,6},{8,9},{9,8},{10,11... | collective-permute-start | bytes 884744 | tf_op jit(solution)/shard_map/ppermute | solution.py:45
  76.1 16.0 %collective-permute-start.18 = (bf16[96,3072]{1,0:T(8,128)(2,1)}, bf16[96,3072]{1,0:T(8,128)(2,1)}, u32[]{:S(2)}, u32[]{:S(2)}) collective-permute-start(bf16[96,3072]{1,0:T(8,128)(2,1)} %add_convert_fusion.3), channel_id=1, source_target_pairs={{0,16},{8,24},{16,0},{24,8},{1,17},{9,25},{17,1},{25,9},{2,18},{10... | collective-permute-start | bytes 1769480 | tf_op jit(solution)/shard_map/ppermute | solution.py:40
  94.4 16.2 %collective-permute-start.25 = (bf16[96,3072]{1,0:T(8,128)(2,1)S(1)}, bf16[96,3072]{1,0:T(8,128)(2,1)S(1)}, u32[]{:S(2)}, u32[]{:S(2)}) collective-permute-start(bf16[96,3072]{1,0:T(8,128)(2,1)S(1)} %get-tuple-element.68.e0.refs_0_), channel_id=1, source_target_pairs={{0,16},{8,24},{16,0},{24,8},{1,17},{9,25},{17,1},{25,9},{2,18},{10... | collective-permute-start | bytes 1769480 | tf_op jit(solution)/shard_map/ppermute | solution.py:40
  95.4 26.8 %collective-permute-start.23 = (bf16[96,3072]{1,0:T(8,128)(2,1)S(1)}, bf16[96,3072]{1,0:T(8,128)(2,1)S(1)}, u32[]{:S(2)}, u32[]{:S(2)}) collective-permute-start(bf16[96,3072]{1,0:T(8,128)(2,1)S(1)} %add_convert_fusion.1), channel_id=1, source_target_pairs={{0,16},{8,24},{16,0},{24,8},{1,17},{9,25},{17,1},{25,9},{2,18},{10... | collective-permute-start | bytes 1769480 | tf_op jit(solution)/shard_map/ppermute | solution.py:40
  97.7 28.9 %collective-permute-start.24 = (bf16[96,3072]{1,0:T(8,128)(2,1)S(1)}, bf16[96,3072]{1,0:T(8,128)(2,1)S(1)}, u32[]{:S(2)}, u32[]{:S(2)}) collective-permute-start(bf16[96,3072]{1,0:T(8,128)(2,1)S(1)} %get-tuple-element.68.e0.refs_0_), channel_id=1, source_target_pairs={{0,8},{8,0},{16,24},{24,16},{1,9},{9,1},{17,25},{25,17},{2,10},{10... | collective-permute-start | bytes 1769480 | tf_op jit(solution)/shard_map/ppermute | solution.py:40
  110.6 27.2 %collective-permute-start.26 = (bf16[96,3072]{1,0:T(8,128)(2,1)S(1)}, bf16[96,3072]{1,0:T(8,128)(2,1)S(1)}, u32[]{:S(2)}, u32[]{:S(2)}) collective-permute-start(bf16[96,3072]{1,0:T(8,128)(2,1)S(1)} %collective-permute-done.25.e2.refs_2_), channel_id=1, source_target_pairs={{0,8},{8,0},{16,24},{24,16},{1,9},{9,1},{17,25},{25,17},{2,10},{10... | collective-permute-start | bytes 1769480 | tf_op jit(solution)/shard_map/ppermute | solution.py:40
  122.6 14.3 %collective-permute-start.28 = (bf16[96,3072]{1,0:T(8,128)(2,1)S(1)}, bf16[96,3072]{1,0:T(8,128)(2,1)S(1)}, u32[]{:S(2)}, u32[]{:S(2)}) collective-permute-start(bf16[96,3072]{1,0:T(8,128)(2,1)S(1)} %get-tuple-element.70.e0.refs_4_), channel_id=1, source_target_pairs={{0,16},{8,24},{16,0},{24,8},{1,17},{9,25},{17,1},{25,9},{2,18},{10... | collective-permute-start | bytes 1769480 | tf_op jit(solution)/shard_map/ppermute | solution.py:40
  123.2 30.7 %collective-permute-start.27 = (bf16[96,3072]{1,0:T(8,128)(2,1)S(1)}, bf16[96,3072]{1,0:T(8,128)(2,1)}, u32[]{:S(2)}, u32[]{:S(2)}) collective-permute-start(bf16[96,3072]{1,0:T(8,128)(2,1)S(1)} %get-tuple-element.70.e0.refs_4_), channel_id=1, source_target_pairs={{0,8},{8,0},{16,24},{24,16},{1,9},{9,1},{17,25},{25,17},{2,10},{10... | collective-permute-start | bytes 1769480 | tf_op jit(solution)/shard_map/ppermute | solution.py:40
  124.1 20.8 %collective-permute-start.32 = (bf16[48,3072]{1,0:T(8,128)(2,1)}, bf16[48,3072]{1,0:T(8,128)(2,1)S(1)}, u32[]{:S(2)}, u32[]{:S(2)}) collective-permute-start(bf16[48,3072]{1,0:T(8,128)(2,1)} %get-tuple-element.79), channel_id=1, source_target_pairs={{0,6},{1,7},{2,4},{3,5},{4,2},{5,3},{6,0},{7,1},{8,14},{9,15},{10,... | collective-permute-start | bytes 884744 | tf_op jit(solution)/shard_map/ppermute | solution.py:45
  126.6 27.3 %collective-permute-start.31 = (bf16[48,3072]{1,0:T(8,128)(2,1)}, bf16[48,3072]{1,0:T(8,128)(2,1)S(1)}, u32[]{:S(2)}, u32[]{:S(2)}) collective-permute-start(bf16[48,3072]{1,0:T(8,128)(2,1)} %get-tuple-element.80), channel_id=1, source_target_pairs={{0,4},{1,5},{2,6},{3,7},{4,0},{5,1},{6,2},{7,3},{8,12},{9,13},{10,... | collective-permute-start | bytes 884744 | tf_op jit(solution)/shard_map/ppermute | solution.py:45
  137.0 17.0 %collective-permute-start.29 = (bf16[96,3072]{1,0:T(8,128)(2,1)S(1)}, bf16[96,3072]{1,0:T(8,128)(2,1)}, u32[]{:S(2)}, u32[]{:S(2)}) collective-permute-start(bf16[96,3072]{1,0:T(8,128)(2,1)S(1)} %collective-permute-done.28.e2.refs_6_), channel_id=1, source_target_pairs={{0,8},{8,0},{16,24},{24,16},{1,9},{9,1},{17,25},{25,17},{2,10},{10... | collective-permute-start | bytes 1769480 | tf_op jit(solution)/shard_map/ppermute | solution.py:40
  143.3 30.5 %collective-permute-start.33 = (bf16[48,3072]{1,0:T(8,128)(2,1)}, bf16[48,3072]{1,0:T(8,128)(2,1)S(1)}, u32[]{:S(2)}, u32[]{:S(2)}) collective-permute-start(bf16[48,3072]{1,0:T(8,128)(2,1)} %pad_maximum_fusion.6), channel_id=1, source_target_pairs={{0,1},{1,0},{2,3},{3,2},{4,5},{5,4},{6,7},{7,6},{8,9},{9,8},{10,11... | collective-permute-start | bytes 884744 | tf_op jit(solution)/shard_map/ppermute | solution.py:45
  158.7 15.1 %collective-permute-start.34 = (bf16[48,3072]{1,0:T(8,128)(2,1)S(1)}, bf16[48,3072]{1,0:T(8,128)(2,1)S(1)}, u32[]{:S(2)}, u32[]{:S(2)}) collective-permute-start(bf16[48,3072]{1,0:T(8,128)(2,1)S(1)} %pad_maximum_fusion.7), channel_id=1, source_target_pairs={{0,1},{1,0},{2,3},{3,2},{4,5},{5,4},{6,7},{7,6},{8,9},{9,8},{10,11... | collective-permute-start | bytes 884744 | tf_op jit(solution)/shard_map/ppermute | solution.py:45
  (37 other events, 343.6 us)

commit v2 on v1

v2 whole, which is shorter than its diff:
```python
import functools

import jax
import jax.numpy as jnp
from jax import lax
from jax.experimental import pallas as pl
from jax.experimental.pallas import tpu as pltpu
from jax.sharding import PartitionSpec as P

error_scale = 0.03125
absent_mark = 1024.0
GROUPS = 2
f32 = jnp.float32
bf16 = jnp.bfloat16
VMEM_LIMIT = 60 * 1024 * 1024
WEIGH = 10


def dot(a, b, on_a, on_b):
    return lax.dot_general(a, b, (((on_a,), (on_b,)), ((), ())), preferred_element_type=f32)


def call(kernel, name, out_shape, grid, in_specs, out_specs, scratch, flops, moved):
    return pl.pallas_call(
        kernel,
        name=name,
        out_shape=out_shape,
        grid=grid,
        in_specs=in_specs,
        out_specs=out_specs,
        scratch_shapes=scratch,
        cost_estimate=pl.CostEstimate(flops=WEIGH * flops, bytes_accessed=WEIGH * moved, transcendentals=0),
        compiler_params=pltpu.CompilerParams(
            vmem_limit_bytes=VMEM_LIMIT, dimension_semantics=("arbitrary",) * len(grid)
        ),
    )


def swap(v, distance):
    n = lax.axis_size("dp")
    return lax.ppermute(v, "dp", [(i, i ^ distance) for i in range(n)])


def pass_on(v, distance):
    n = lax.axis_size("expert")
    return lax.ppermute(v, "expert", [(i, i ^ distance) for i in range(n)])


def after(v, *first):
    return lax.optimization_barrier((v,) + first)[0]


def gate(values, *first):
    return list(lax.optimization_barrier(tuple(values) + first)[: len(values)])


def slot_row(route_row, capacity, pairs):
    tokens = route_row.shape[1]
    distance = route_row ^ lax.axis_index("expert")
    one_hot = (lax.broadcasted_iota(jnp.int32, (2 * pairs, tokens), 0) == distance).astype(f32)
    earlier = (
        lax.broadcasted_iota(jnp.int32, (tokens, tokens), 0)
        < lax.broadcasted_iota(jnp.int32, (tokens, tokens), 1)
    ).astype(bf16)
    before = dot(one_hot.astype(bf16), earlier, 1, 0)
    rank = jnp.sum(before * one_hot, axis=0, keepdims=True).astype(jnp.int32)
    return ((distance & 1) * pairs + (distance >> 1)) * capacity + rank


def store_parts(rows, outs):
    start = 0
    for out in outs:
        out[...] = rows[start : start + out.shape[0]].astype(bf16)
        start += out.shape[0]


def place_kernel(capacity, pairs, routes_ref, tokens_ref, by_slot_ref, *outs):
    slots, tokens = by_slot_ref.shape
    slot = slot_row(routes_ref[...], capacity, pairs)
    by_slot = (lax.broadcasted_iota(jnp.int32, (slots, tokens), 0) == slot).astype(f32).astype(bf16)
    by_slot_ref[...] = by_slot
    store_parts(dot(by_slot, tokens_ref[...], 1, 0), outs)


def place_target_kernel(by_slot_ref, target_ref, *outs):
    by_slot = by_slot_ref[...]
    mark = (1.0 - jnp.sum(by_slot.astype(f32), axis=1, keepdims=True)) * absent_mark
    store_parts(dot(by_slot, target_ref[...], 1, 0) + mark, outs)


def place(name, kernel, first, values, slots, pairs, with_slots):
    per_dev, features = values.shape
    capacity = slots // (2 * pairs)
    sizes = [capacity] * pairs if capacity % 8 == 0 else [slots // 2]
    sizes = sizes + [slots // 2]
    steps = 2
    cols = lambda rows: pl.BlockSpec((rows, features // steps), lambda i: (0, i))
    whole = lambda *shape: pl.BlockSpec(shape, lambda i: (0, 0))
    outs = call(
        kernel,
        name,
        [jax.ShapeDtypeStruct((slots, per_dev), bf16)] * with_slots
        + [jax.ShapeDtypeStruct((size, features), bf16) for size in sizes],
        (steps,),
        [whole(*first.shape), cols(per_dev)],
        [whole(slots, per_dev)] * with_slots + [cols(size) for size in sizes],
        [],
        2 * slots * per_dev * features,
        2 * (per_dev + slots) * features,
    )(first, values)
    direct, via = outs[with_slots:-1], outs[-1]
    if len(direct) == 1:
        direct = [direct[0][capacity * k : capacity * (k + 1)] for k in range(pairs)]
    return outs[0], list(direct), via


def forward_kernel(steps, count, *refs):
    blocks = refs[:count]
    thr, enc, dec, act_ref, slope_ref, near_ref, far_ref, send_near_ref, send_far_ref, pre = refs[count:]
    i = pl.program_id(0)
    size = act_ref.shape[0] // 4

    @pl.when(i < steps)
    def _():
        x = jnp.concatenate([b[...] for b in blocks], axis=0)
        part = dot(x, enc[...], 1, 0)

        @pl.when(i == 0)
        def _():
            pre[...] = part

        @pl.when(i > 0)
        def _():
            pre[...] += part

    @pl.when(i == steps - 1)
    def _():
        latent = pre[...] - 0.25 * thr[...].astype(f32)
        squash = jax.nn.sigmoid(4.0 * latent)
        act_ref[...] = (latent * squash).astype(bf16)
        slope_ref[...] = squash + 4.0 * latent * squash * (1.0 - squash)

    @pl.when(i >= steps)
    def _():
        part = dot(act_ref[...], dec[...], 1, 1)
        near_ref[...] = part[:size]
        send_near_ref[...] = part[size : 2 * size].astype(bf16)
        far_ref[...] = part[2 * size : 3 * size]
        send_far_ref[...] = part[3 * size :].astype(bf16)


def forward(blocks, thresholds, enc, dec):
    count = len(blocks)
    features = blocks[0].shape[1]
    size = sum(b.shape[0] for b in blocks) // 4
    latents = enc.shape[1]
    steps = 2
    wide = features // steps
    early = lambda i: jnp.minimum(i, steps - 1)
    late = lambda i: jnp.maximum(i - steps, 0)
    fixed = lambda *shape: pl.BlockSpec(shape, lambda i: (0, 0))
    col_out = lambda rows: pl.BlockSpec((rows, wide), lambda i: (0, late(i)))
    return call(
        functools.partial(forward_kernel, steps, count),
        "forward",
        [
            jax.ShapeDtypeStruct((4 * size, latents), bf16),
            jax.ShapeDtypeStruct((4 * size, latents), f32),
            jax.ShapeDtypeStruct((size, features), f32),
            jax.ShapeDtypeStruct((size, features), f32),
            jax.ShapeDtypeStruct((size, features), bf16),
            jax.ShapeDtypeStruct((size, features), bf16),
        ],
        (2 * steps,),
        [pl.BlockSpec((b.shape[0], wide), lambda i: (0, early(i))) for b in blocks]
        + [
            fixed(1, latents),
            pl.BlockSpec((wide, latents), lambda i: (early(i), 0)),
            pl.BlockSpec((wide, latents), lambda i: (late(i), 0)),
        ],
        [fixed(4 * size, latents), fixed(4 * size, latents), *[col_out(size)] * 4],
        [pltpu.VMEM((4 * size, latents), f32)],
        2 * 2 * 4 * size * features * latents,
        4 * features * latents + 24 * size * features,
    )(*blocks, thresholds, enc, dec)


def make_error(near, got, across, wanted):
    recon = (near + got.astype(f32) + across.astype(f32)).astype(bf16)
    goal = wanted.astype(f32)
    error = (recon.astype(f32) - goal) * error_scale
    return recon, jnp.where(goal < 0.5 * absent_mark, error, 0.0).astype(bf16)


def back_kernel(steps, e0, e1, e2, e3, dec, slope, out_ref, total):
    i = pl.program_id(0)
    e = jnp.concatenate([e0[...], e1[...], e2[...], e3[...]], axis=0)
    part = dot(e, dec[...], 1, 0)

    @pl.when(i == 0)
    def _():
        total[...] = part

    @pl.when(i > 0)
    def _():
        total[...] += part

    @pl.when(i == steps - 1)
    def _():
        out_ref[...] = (total[...] * slope[...]).astype(bf16)


def back(errors, dec, slope):
    size, features = errors[0].shape
    latents = dec.shape[1]
    steps = 2
    wide = features // steps
    fixed = pl.BlockSpec((4 * size, latents), lambda i: (0, 0))
    return call(
        functools.partial(back_kernel, steps),
        "back",
        jax.ShapeDtypeStruct((4 * size, latents), bf16),
        (steps,),
        [pl.BlockSpec((size, wide), lambda i: (0, i))] * 4
        + [pl.BlockSpec((wide, latents), lambda i: (i, 0)), fixed],
        fixed,
        [pltpu.VMEM((4 * size, latents), f32)],
        2 * 4 * size * features * latents,
        2 * features * latents + 8 * size * features,
    )(*errors, dec, slope)


def weight_grad_kernel(count, *refs):
    blocks = refs[:count]
    sides = refs[count : count + GROUPS]
    out_ref = refs[-1]
    left = jnp.concatenate([b[...] for b in blocks], axis=0)
    right = jnp.concatenate([s[...] for s in sides], axis=0)
    out_ref[0] = dot(left, right, 0, 0).astype(bf16)


def weight_grad(name, blocks, sides):
    features = blocks[0].shape[1]
    size = sum(b.shape[0] for b in blocks)
    latents = sides[0].shape[1]
    wide = features // 3
    return call(
        functools.partial(weight_grad_kernel, len(blocks)),
        name,
        jax.ShapeDtypeStruct((1, features, latents), bf16),
        (features // wide,),
        [pl.BlockSpec((b.shape[0], wide), lambda i: (0, i)) for b in blocks]
        + [pl.BlockSpec(s.shape, lambda i: (0, 0)) for s in sides],
        pl.BlockSpec((1, wide, latents), lambda i: (0, i, 0)),
        [],
        2 * size * features * latents,
        2 * features * latents + 2 * size * features,
    )(*blocks, *sides)


def collect_kernel(by_slot, direct, via, out):
    out[...] = dot(by_slot[...], jnp.concatenate([direct[...], via[...]], axis=0), 0, 0).astype(bf16)


def collect(by_slot, direct, via):
    slots, tokens = by_slot.shape
    features = direct.shape[1]
    steps = 2
    cols = lambda rows: pl.BlockSpec((rows, features // steps), lambda i: (0, i))
    return call(
        collect_kernel,
        "collect",
        jax.ShapeDtypeStruct((tokens, features), bf16),
        (steps,),
        [pl.BlockSpec((slots, tokens), lambda i: (0, 0)), cols(slots // 2), cols(slots // 2)],
        cols(tokens),
        [],
        2 * slots * tokens * features,
        2 * (slots + tokens) * features,
    )(by_slot, direct, via)


def local(tokens, target, routes, thresholds, enc_weight, dec_weight):
    experts = lax.axis_size("expert")
    half = lax.axis_size("dp") // 2
    per_dev, features = tokens.shape
    capacity = 3 * per_dev // (2 * experts)
    enc = enc_weight[0]
    dec = dec_weight[0]
    pairs = experts // 2
    slots = experts * capacity
    by_slot, direct, via = place(
        "place",
        functools.partial(place_kernel, capacity, pairs),
        routes.reshape(1, per_dev),
        tokens,
        slots,
        pairs,
        True,
    )
    _, goal_direct, goal_via = place(
        "place_target", place_target_kernel, by_slot, target, slots, pairs, False
    )

    def spread(parts):
        return [parts[0]] + [pass_on(parts[k], 2 * k) for k in range(1, pairs)]

    def cut(v):
        return [v[capacity * k : capacity * (k + 1)] for k in range(pairs)]

    def join(arrays):
        return jnp.concatenate(arrays, axis=0)

    def encode(blocks):
        return forward(blocks, thresholds, enc, dec)

    def total(far, got):
        return (far + got.astype(f32)).astype(bf16)

    out_direct = spread(direct)
    out_via = pass_on(via, 1)
    *out_direct, out_via, goal_via = gate(out_direct + [out_via, goal_via])
    mine0 = join(out_direct)
    out_via = spread(cut(out_via))
    far0 = swap(mine0, half)
    goal_via = pass_on(goal_via, 1)
    *out_via, mine0, far0, goal_via = gate(out_via + [mine0, far0, goal_via])
    goal_direct = gate(goal_direct, far0)
    mine1 = join(out_via)
    far1 = swap(mine1, half)
    goal_direct = spread(goal_direct)
    blocks0 = [mine0, swap(mine0, 1), far0, swap(far0, 1)]
    act0, slope0, keep0, other0, send_near0, send_far0 = encode(blocks0)
    *goal_direct, mine1, far1, send_near0, send_far0, goal_via = gate(
        goal_direct + [mine1, far1, send_near0, send_far0, goal_via]
    )
    across0 = swap(total(other0, swap(send_far0, 1)), half)
    goal_via = spread(cut(goal_via))
    blocks1 = [mine1, swap(mine1, 1), far1, swap(far1, 1)]
    act1, slope1, keep1, other1, send_near1, send_far1 = encode(blocks1)
    *goal_via, across0, send_near0, send_near1, send_far1 = gate(
        goal_via + [across0, send_near0, send_near1, send_far1]
    )
    across1 = swap(total(other1, swap(send_far1, 1)), half)
    recon0, error0 = make_error(keep0, swap(send_near0, 1), across0, join(goal_direct))
    home0 = spread(cut(recon0))
    *home0, across1, error0, send_near1 = gate(home0 + [across1, error0, send_near1])
    efar0 = swap(error0, half)
    recon1, error1 = make_error(keep1, swap(send_near1, 1), across1, join(goal_via))
    home1 = spread(cut(recon1))
    *home1, error0, efar0, error1 = gate(home1 + [error0, efar0, error1])
    efar1, enear1 = swap(error1, half), swap(error1, 1)
    home1 = pass_on(join(home1), 1)
    errors0 = [error0, swap(error0, 1), efar0, swap(efar0, 1)]
    back0 = back(errors0, dec, slope0)
    home1, efar1, enear1, back0 = gate([home1, efar1, enear1, back0])
    errors1 = [error1, enear1, efar1, swap(efar1, 1)]
    back1 = back(errors1, dec, slope1)
    grad_dec = weight_grad("grad_dec", errors0 + errors1, [act0, act1])
    grad_enc = weight_grad("grad_enc", blocks0 + blocks1, [back0, back1])
    recon = collect(by_slot, join(home0), home1)
    return recon, grad_enc, grad_dec


def solution(mesh):
    in_specs = (
        P(("dp", "expert"), None),
        P(("dp", "expert"), None),
        P(("dp", "expert"), None),
        P("expert", "dp"),
        P("expert", None, "dp"),
        P("expert", None, "dp"),
    )
    out_specs = (P(("dp", "expert"), None), P("expert", None, "dp"), P("expert", None, "dp"))
    return jax.shard_map(local, mesh=mesh, in_specs=in_specs, out_specs=out_specs, check_vma=False)
```

time: 178 us -> 161 us (0.904)
  waiting for transfers between devices: 87 us -> 67.2 us
  starting transfers between devices: 31 us -> 39.4 us
  local copies, waits for them, and re-layouts: 7.32 us -> 2.81 us
    ppermute x16 -> x21, waiting for transfers between devices: 53.2 us -> 39.6 us  [pass_on(): return lax.ppermute(v, 'expert', [(i, i ^ distance) for i in range(n)])]
    ppermute x16 -> x21, starting transfers between devices: 22.6 us -> 31.3 us  [pass_on(): return lax.ppermute(v, 'expert', [(i, i ^ distance) for i in range(n)])]
    ppermute x19 -> x18, waiting for transfers between devices: 33.8 us -> 27.6 us  [swap(): return lax.ppermute(v, 'dp', [(i, i ^ distance) for i in range(n)])]
    slice x18 -> x4, local copies, waits for them, and re-layouts: 3.89 us -> 0.16 us  [cut(): return [v[capacity * k:capacity * (k + 1)] for k in range(pairs)]]
    pallas_call x2 -> x3, Pallas kernels: 6.94 us -> 7.51 us  [the longest x2 5.11 us: place(): call(kernel, name, [jax.ShapeDtypeStruct((slots, per_dev), bf16)] * with_...]
    ppermute x19 -> x18, starting transfers between devices: 8.43 us -> 8.07 us  [swap(): return lax.ppermute(v, 'dp', [(i, i ^ distance) for i in range(n)])]
  transfers between devices with their start and end apart: 35 -> 39, of which waited for: 14 -> 17; matrix products, arithmetic and copies ran while one was open for 4% -> 2% of each run, Pallas kernels for 22% -> 16%
where the time goes in v2:
time: 161 us
  waiting for transfers between devices  67.2 us (42%)
  Pallas kernels  47 us (29%)
  starting transfers between devices  39.4 us (24%)
  other arithmetic  3.31 us (2%)
  local copies, waits for them, and re-layouts  2.81 us (2%)
    ppermute x21, waiting for transfers between devices, pass_on(): return lax.ppermute(v, 'expert', [(i, i ^ distance) for i in range(n)])  39.6 us
    ppermute x21, starting transfers between devices, pass_on(): return lax.ppermute(v, 'expert', [(i, i ^ distance) for i in range(n)])  31.3 us
    ppermute x18, waiting for transfers between devices, swap(): return lax.ppermute(v, 'dp', [(i, i ^ distance) for i in range(n)])  27.6 us
    pallas_call x2, Pallas kernels, forward(): call(functools.partial(forward_kernel, steps, count), 'forward', [jax.Sha...  16.7 us
    pallas_call x2, Pallas kernels, weight_grad(): call(functools.partial(weight_grad_kernel, len(blocks)), name, jax.ShapeD...  13.5 us
    pallas_call x2, Pallas kernels, back(): call(functools.partial(back_kernel, steps), 'back', jax.ShapeDtypeStruct(...  9.34 us
    ppermute x18, starting transfers between devices, swap(): return lax.ppermute(v, 'dp', [(i, i ^ distance) for i in range(n)])  8.07 us
    pallas_call x2, Pallas kernels, place(): call(kernel, name, [jax.ShapeDtypeStruct((slots, per_dev), bf16)] * with_...  5.11 us
  transfers between devices with their start and end apart: 39, of which 17 were waited for; matrix products, arithmetic and copies ran while one was open for 2% of the time, Pallas kernels for 16%

profile of v2, /device:TPU:0, one launch (start us, length us, event | category | flops | bytes accessed | tf_op | source)
XLA Modules:
  0.0 160.8 jit_solution(7314395421533858693)
XLA Ops:
  0.6 2.7 %place.1 = (bf16[192,128]{1,0:T(8,128)(2,1)}, bf16[24,3072]{1,0:T(8,128)(2,1)}, bf16[24,3072]{1,0:T(8,128)(2,1)}, bf16[24,3072]{1,0:T(8,128)(2,1)}, bf16[24,3072]{1,0:T(8,128)(2,1)}, /*index=5*/bf16[96,3072]{1,0:T(8,128)(2,1)}) custom-call(s32[1,128]{1,0:T(1,128)} %bitcast.9, bf16[128,3072]{1,0:T(8,128)(2,1)} %tokens_ref.1), custom_call_target="tpu_custom_call" | custom-call | flops 1509949440 | bytes 19660800 | tf_op jit(solution)/shard_map/place/pallas_call | solution.py:99
  3.3 3.0 %collective-permute-start.3 = (bf16[96,3072]{1,0:T(8,128)(2,1)}, bf16[96,3072]{1,0:T(8,128)(2,1)S(1)}, u32[]{:S(2)}, u32[]{:S(2)}) collective-permute-start(bf16[96,3072]{1,0:T(8,128)(2,1)} %get-tuple-element.83), channel_id=1, source_target_pairs={{0,1},{1,0},{2,3},{3,2},{4,5},{5,4},{6,7},{7,6},{8,9},{9,8},{10,11... | collective-permute-start | bytes 1769480 | tf_op jit(solution)/shard_map/ppermute | solution.py:46
  7.8 2.6 %collective-permute-start.1 = (bf16[24,3072]{1,0:T(8,128)(2,1)}, bf16[24,3072]{1,0:T(8,128)(2,1)S(1)}, u32[]{:S(2)}, u32[]{:S(2)}) collective-permute-start(bf16[24,3072]{1,0:T(8,128)(2,1)} %get-tuple-element.81), channel_id=1, source_target_pairs={{0,4},{1,5},{2,6},{3,7},{4,0},{5,1},{6,2},{7,3},{8,12},{9,13},{10,... | collective-permute-start | bytes 442376 | tf_op jit(solution)/shard_map/ppermute | solution.py:46
  13.6 8.3 %collective-permute-done.1 = bf16[24,3072]{1,0:T(8,128)(2,1)S(1)} collective-permute-done((bf16[24,3072]{1,0:T(8,128)(2,1)}, bf16[24,3072]{1,0:T(8,128)(2,1)S(1)}, u32[]{:S(2)}, u32[]{:S(2)}) %collective-permute-start.1) | collective-permute-done | bytes 147488 | tf_op jit(solution)/shard_map/ppermute | solution.py:46
  24.2 2.7 %collective-permute-start.6 = (bf16[24,3072]{1,0:T(8,128)(2,1)S(1)}, bf16[24,3072]{1,0:T(8,128)(2,1)S(1)}, u32[]{:S(2)}, u32[]{:S(2)}) collective-permute-start(bf16[24,3072]{1,0:T(8,128)(2,1)S(1)} %get-tuple-element.169), channel_id=1, source_target_pairs={{0,6},{1,7},{2,4},{3,5},{4,2},{5,3},{6,0},{7,1},{8,14},{9,15},{10,... | collective-permute-start | bytes 442376 | tf_op jit(solution)/shard_map/ppermute | solution.py:46
  28.6 4.1 %collective-permute-done.6 = bf16[24,3072]{1,0:T(8,128)(2,1)S(1)} collective-permute-done((bf16[24,3072]{1,0:T(8,128)(2,1)S(1)}, bf16[24,3072]{1,0:T(8,128)(2,1)S(1)}, u32[]{:S(2)}, u32[]{:S(2)}) %collective-permute-start.6) | collective-permute-done | bytes 147488 | tf_op jit(solution)/shard_map/ppermute | solution.py:46
  32.8 6.0 %collective-permute-done.5 = bf16[24,3072]{1,0:T(8,128)(2,1)S(1)} collective-permute-done((bf16[24,3072]{1,0:T(8,128)(2,1)S(1)}, bf16[24,3072]{1,0:T(8,128)(2,1)S(1)}, u32[]{:S(2)}, u32[]{:S(2)}) %collective-permute-start.5) | collective-permute-done | bytes 147488 | tf_op jit(solution)/shard_map/ppermute | solution.py:46
  39.1 3.4 %collective-permute-start.12 = (bf16[24,3072]{1,0:T(8,128)(2,1)S(1)}, bf16[24,3072]{1,0:T(8,128)(2,1)S(1)}, u32[]{:S(2)}, u32[]{:S(2)}) collective-permute-start(bf16[24,3072]{1,0:T(8,128)(2,1)S(1)} %copy-done.21), channel_id=1, source_target_pairs={{0,4},{1,5},{2,6},{3,7},{4,0},{5,1},{6,2},{7,3},{8,12},{9,13},{10,... | collective-permute-start | bytes 442376 | tf_op jit(solution)/shard_map/ppermute | solution.py:46
  46.8 8.3 %forward.2 = (bf16[384,512]{1,0:T(8,128)(2,1)}, f32[384,512]{1,0:T(8,128)}, f32[96,3072]{1,0:T(8,128)}, f32[96,3072]{1,0:T(8,128)}, bf16[96,3072]{1,0:T(8,128)(2,1)}, /*index=5*/bf16[96,3072]{1,0:T(8,128)(2,1)}) custom-call(bf16[96,3072]{1,0:T(8,128)(2,1)} %copy-done.8, bf16[96,3072]{1,0:T(8,128)(2,1)} %copy-done.11, bf16[96,3072]{1,0:T(8,128)(2,1)} %copy-done.9, ...), custom_call_target="tpu_custom_call" | custom-call | flops 24159191040 | bytes 133693440 | tf_op jit(solution)/shard_map/forward/pallas_call | solution.py:163
  55.1 5.7 %collective-permute-done.14.refs_2_.refs_6_ = bf16[96,3072]{1,0:T(8,128)(2,1)S(1)} collective-permute-done((bf16[96,3072]{1,0:T(8,128)(2,1)S(1)}, bf16[96,3072]{1,0:T(8,128)(2,1)S(1)}, u32[]{:S(2)}, u32[]{:S(2)}) %collective-permute-start.14) | collective-permute-done | bytes 589856 | tf_op jit(solution)/shard_map/ppermute | solution.py:41
  60.9 2.9 %collective-permute-start.17 = (bf16[24,3072]{1,0:T(8,128)(2,1)S(1)}, bf16[24,3072]{1,0:T(8,128)(2,1)S(1)}, u32[]{:S(2)}, u32[]{:S(2)}) collective-permute-start(bf16[24,3072]{1,0:T(8,128)(2,1)S(1)} %get-tuple-element.165), channel_id=1, source_target_pairs={{0,6},{1,7},{2,4},{3,5},{4,2},{5,3},{6,0},{7,1},{8,14},{9,15},{10,... | collective-permute-start | bytes 442376 | tf_op jit(solution)/shard_map/ppermute | solution.py:46
  68.3 8.4 %forward.3 = (bf16[384,512]{1,0:T(8,128)(2,1)}, f32[384,512]{1,0:T(8,128)}, f32[96,3072]{1,0:T(8,128)}, f32[96,3072]{1,0:T(8,128)}, bf16[96,3072]{1,0:T(8,128)(2,1)}, /*index=5*/bf16[96,3072]{1,0:T(8,128)(2,1)}) custom-call(bf16[96,3072]{1,0:T(8,128)(2,1)} %copy-done.7, bf16[96,3072]{1,0:T(8,128)(2,1)} %collective-permute-done.20.refs_1_.refs_5_, ...), custom_call_target="tpu_custom_call" | custom-call | flops 24159191040 | bytes 133693440 | tf_op jit(solution)/shard_map/forward/pallas_call | solution.py:163
  76.8 6.1 %collective-permute-done.19 = bf16[96,3072]{1,0:T(8,128)(2,1)S(1)} collective-permute-done((bf16[96,3072]{1,0:T(8,128)(2,1)S(1)}, bf16[96,3072]{1,0:T(8,128)(2,1)S(1)}, u32[]{:S(2)}, u32[]{:S(2)}) %collective-permute-start.19) | collective-permute-done | bytes 589856 | tf_op jit(solution)/shard_map/ppermute | solution.py:41
  83.4 2.5 %collective-permute-done.26 = bf16[96,3072]{1,0:T(8,128)(2,1)S(1)} collective-permute-done((bf16[96,3072]{1,0:T(8,128)(2,1)}, bf16[96,3072]{1,0:T(8,128)(2,1)S(1)}, u32[]{:S(2)}, u32[]{:S(2)}) %collective-permute-start.26) | collective-permute-done | bytes 589856 | tf_op jit(solution)/shard_map/ppermute | solution.py:41
  88.4 3.0 %collective-permute-start.25 = (bf16[24,3072]{1,0:T(8,128)(2,1)S(1)}, bf16[24,3072]{1,0:T(8,128)(2,1)S(1)}, u32[]{:S(2)}, u32[]{:S(2)}) collective-permute-start(bf16[24,3072]{1,0:T(8,128)(2,1)S(1)} %get-tuple-element.161), channel_id=1, source_target_pairs={{0,6},{1,7},{2,4},{3,5},{4,2},{5,3},{6,0},{7,1},{8,14},{9,15},{10,... | collective-permute-start | bytes 442376 | tf_op jit(solution)/shard_map/ppermute | solution.py:46
  92.9 4.2 %collective-permute-done.25 = bf16[24,3072]{1,0:T(8,128)(2,1)S(1)} collective-permute-done((bf16[24,3072]{1,0:T(8,128)(2,1)S(1)}, bf16[24,3072]{1,0:T(8,128)(2,1)S(1)}, u32[]{:S(2)}, u32[]{:S(2)}) %collective-permute-start.25) | collective-permute-done | bytes 147488 | tf_op jit(solution)/shard_map/ppermute | solution.py:46
  97.1 6.5 %collective-permute-done.24 = bf16[24,3072]{1,0:T(8,128)(2,1)S(1)} collective-permute-done((bf16[24,3072]{1,0:T(8,128)(2,1)S(1)}, bf16[24,3072]{1,0:T(8,128)(2,1)S(1)}, u32[]{:S(2)}, u32[]{:S(2)}) %collective-permute-start.24) | collective-permute-done | bytes 147488 | tf_op jit(solution)/shard_map/ppermute | solution.py:46
  106.1 2.5 %collective-permute-start.31 = (bf16[24,3072]{1,0:T(8,128)(2,1)S(1)}, bf16[24,3072]{1,0:T(8,128)(2,1)S(1)}, u32[]{:S(2)}, u32[]{:S(2)}) collective-permute-start(bf16[24,3072]{1,0:T(8,128)(2,1)S(1)} %get-tuple-element.157), channel_id=1, source_target_pairs={{0,6},{1,7},{2,4},{3,5},{4,2},{5,3},{6,0},{7,1},{8,14},{9,15},{10,... | collective-permute-start | bytes 442376 | tf_op jit(solution)/shard_map/ppermute | solution.py:46
  110.6 8.8 %collective-permute-done.32.e2.refs_2_ = bf16[96,3072]{1,0:T(8,128)(2,1)S(1)} collective-permute-done((bf16[96,3072]{1,0:T(8,128)(2,1)S(1)}, bf16[96,3072]{1,0:T(8,128)(2,1)S(1)}, u32[]{:S(2)}, u32[]{:S(2)}) %collective-permute-start.32) | collective-permute-done | bytes 589856 | tf_op jit(solution)/shard_map/ppermute | solution.py:41
  125.3 4.7 %back.2.refs_8_ = bf16[384,512]{1,0:T(8,128)(2,1)} custom-call(bf16[96,3072]{1,0:T(8,128)(2,1)} %copy-done.3, bf16[96,3072]{1,0:T(8,128)(2,1)} %copy-done.17, bf16[96,3072]{1,0:T(8,128)(2,1)} %copy-done.13, bf16[96,3072]{1,0:T(8,128)(2,1)} %copy-done.18, bf16[3072,512]{1,0:T(8,128)(2,1)} %bitcast.7, f32[384,512]{1,0:T(8,128)} %get-tuple-element.145.slope), custom_call_target="tpu_custom_call" | custom-call | flops 12079595520 | bytes 55050240 | tf_op jit(solution)/shard_map/back/pallas_call | solution.py:219
  130.0 8.5 %collective-permute-done.33.via = bf16[96,3072]{1,0:T(8,128)(2,1)} collective-permute-done((bf16[96,3072]{1,0:T(8,128)(2,1)S(1)}, bf16[96,3072]{1,0:T(8,128)(2,1)}, u32[]{:S(2)}, u32[]{:S(2)}) %collective-permute-start.33) | collective-permute-done | bytes 589856 | tf_op jit(solution)/shard_map/ppermute | solution.py:46
  142.6 4.7 %back.3.refs_9_ = bf16[384,512]{1,0:T(8,128)(2,1)} custom-call(bf16[96,3072]{1,0:T(8,128)(2,1)} %copy-done.4, bf16[96,3072]{1,0:T(8,128)(2,1)} %collective-permute-done.35.e1.refs_5_, bf16[96,3072]{1,0:T(8,128)(2,1)} %collective-permute-done.34.e2.refs_6_, bf16[96,3072]{1,0:T(8,128)(2,1)} %copy-done.19, bf16[3072,512]{1,0:T(8,128)(2,1)} %bitcast.8, ...), custom_call_target="tpu_custom_call" | custom-call | flops 12079595520 | bytes 55050240 | tf_op jit(solution)/shard_map/back/pallas_call | solution.py:219
  147.2 6.8 %grad_dec.1 = bf16[1,3072,512]{2,1,0:T(8,128)(2,1)} custom-call(bf16[96,3072]{1,0:T(8,128)(2,1)} %copy-done.3, bf16[96,3072]{1,0:T(8,128)(2,1)} %copy-done.17, bf16[96,3072]{1,0:T(8,128)(2,1)} %copy-done.13, bf16[96,3072]{1,0:T(8,128)(2,1)} %copy-done.18, bf16[96,3072]{1,0:T(8,128)(2,1)} %copy-done.4, bf16[96,3072]{1,0:T(8,128)(2,1)} %collective-permute-done.35.e1.refs_5_, ...), custom_call_target="tpu_custom_call" | custom-call | flops 24159191040 | bytes 78643200 | tf_op jit(solution)/shard_map/grad_dec/pallas_call | solution.py:247
  154.0 6.8 %grad_enc.1 = bf16[1,3072,512]{2,1,0:T(8,128)(2,1)} custom-call(bf16[96,3072]{1,0:T(8,128)(2,1)} %copy-done.8, bf16[96,3072]{1,0:T(8,128)(2,1)} %copy-done.11, bf16[96,3072]{1,0:T(8,128)(2,1)} %copy-done.9, bf16[96,3072]{1,0:T(8,128)(2,1)} %copy-done.10, bf16[96,3072]{1,0:T(8,128)(2,1)} %copy-done.7, ...), custom_call_target="tpu_custom_call" | custom-call | flops 24159191040 | bytes 78643200 | tf_op jit(solution)/shard_map/grad_enc/pallas_call | solution.py:247
  (127 shorter events, 36.7 us)
Async XLA Ops:
  3.3 18.6 %collective-permute-start.3 = (bf16[96,3072]{1,0:T(8,128)(2,1)}, bf16[96,3072]{1,0:T(8,128)(2,1)S(1)}, u32[]{:S(2)}, u32[]{:S(2)}) collective-permute-start(bf16[96,3072]{1,0:T(8,128)(2,1)} %get-tuple-element.83), channel_id=1, source_target_pairs={{0,1},{1,0},{2,3},{3,2},{4,5},{5,4},{6,7},{7,6},{8,9},{9,8},{10,11... | collective-permute-start | bytes 1769480 | tf_op jit(solution)/shard_map/ppermute | solution.py:46
  7.8 14.1 %collective-permute-start.1 = (bf16[24,3072]{1,0:T(8,128)(2,1)}, bf16[24,3072]{1,0:T(8,128)(2,1)S(1)}, u32[]{:S(2)}, u32[]{:S(2)}) collective-permute-start(bf16[24,3072]{1,0:T(8,128)(2,1)} %get-tuple-element.81), channel_id=1, source_target_pairs={{0,4},{1,5},{2,6},{3,7},{4,0},{5,1},{6,2},{7,3},{8,12},{9,13},{10,... | collective-permute-start | bytes 442376 | tf_op jit(solution)/shard_map/ppermute | solution.py:46
  10.4 11.5 %collective-permute-start.2 = (bf16[24,3072]{1,0:T(8,128)(2,1)}, bf16[24,3072]{1,0:T(8,128)(2,1)S(1)}, u32[]{:S(2)}, u32[]{:S(2)}) collective-permute-start(bf16[24,3072]{1,0:T(8,128)(2,1)} %get-tuple-element.82), channel_id=1, source_target_pairs={{0,6},{1,7},{2,4},{3,5},{4,2},{5,3},{6,0},{7,1},{8,14},{9,15},{10,... | collective-permute-start | bytes 442376 | tf_op jit(solution)/shard_map/ppermute | solution.py:46
  22.1 16.8 %collective-permute-start.7 = (bf16[96,3072]{1,0:T(8,128)(2,1)S(1)}, bf16[96,3072]{1,0:T(8,128)(2,1)S(1)}, u32[]{:S(2)}, u32[]{:S(2)}) collective-permute-start(bf16[96,3072]{1,0:T(8,128)(2,1)S(1)} %constant_dynamic-update-slice_fusion.refs_0_), channel_id=1, source_target_pairs={{0,16},{8,24},{16,0},{24,8},{1,17},{9,25},{17,1},{25,9},{2,18},{10... | collective-permute-start | bytes 1769480 | tf_op jit(solution)/shard_map/ppermute | solution.py:41
  23.6 15.2 %collective-permute-start.8 = (bf16[96,3072]{1,0:T(8,128)(2,1)S(1)}, bf16[96,3072]{1,0:T(8,128)(2,1)S(1)}, u32[]{:S(2)}, u32[]{:S(2)}) collective-permute-start(bf16[96,3072]{1,0:T(8,128)(2,1)S(1)} %copy-done.16), channel_id=1, source_target_pairs={{0,1},{1,0},{2,3},{3,2},{4,5},{5,4},{6,7},{7,6},{8,9},{9,8},{10,11... | collective-permute-start | bytes 1769480 | tf_op jit(solution)/shard_map/ppermute | solution.py:46
  26.9 11.9 %collective-permute-start.5 = (bf16[24,3072]{1,0:T(8,128)(2,1)S(1)}, bf16[24,3072]{1,0:T(8,128)(2,1)S(1)}, u32[]{:S(2)}, u32[]{:S(2)}) collective-permute-start(bf16[24,3072]{1,0:T(8,128)(2,1)S(1)} %get-tuple-element.170), channel_id=1, source_target_pairs={{0,4},{1,5},{2,6},{3,7},{4,0},{5,1},{6,2},{7,3},{8,12},{9,13},{10,... | collective-permute-start | bytes 442376 | tf_op jit(solution)/shard_map/ppermute | solution.py:46
  38.9 16.2 %collective-permute-start.11 = (bf16[24,3072]{1,0:T(8,128)(2,1)S(1)}, bf16[24,3072]{1,0:T(8,128)(2,1)S(1)}, u32[]{:S(2)}, u32[]{:S(2)}) collective-permute-start(bf16[24,3072]{1,0:T(8,128)(2,1)S(1)} %copy-done.22), channel_id=1, source_target_pairs={{0,2},{1,3},{2,0},{3,1},{4,6},{5,7},{6,4},{7,5},{8,10},{9,11},{10,... | collective-permute-start | bytes 442376 | tf_op jit(solution)/shard_map/ppermute | solution.py:46
  39.1 16.1 %collective-permute-start.12 = (bf16[24,3072]{1,0:T(8,128)(2,1)S(1)}, bf16[24,3072]{1,0:T(8,128)(2,1)S(1)}, u32[]{:S(2)}, u32[]{:S(2)}) collective-permute-start(bf16[24,3072]{1,0:T(8,128)(2,1)S(1)} %copy-done.21), channel_id=1, source_target_pairs={{0,4},{1,5},{2,6},{3,7},{4,0},{5,1},{6,2},{7,3},{8,12},{9,13},{10,... | collective-permute-start | bytes 442376 | tf_op jit(solution)/shard_map/ppermute | solution.py:46
  42.4 12.7 %collective-permute-start.13 = (bf16[24,3072]{1,0:T(8,128)(2,1)S(1)}, bf16[24,3072]{1,0:T(8,128)(2,1)S(1)}, u32[]{:S(2)}, u32[]{:S(2)}) collective-permute-start(bf16[24,3072]{1,0:T(8,128)(2,1)S(1)} %copy-done.20), channel_id=1, source_target_pairs={{0,6},{1,7},{2,4},{3,5},{4,2},{5,3},{6,0},{7,1},{8,14},{9,15},{10,... | collective-permute-start | bytes 442376 | tf_op jit(solution)/shard_map/ppermute | solution.py:46
  45.5 15.4 %collective-permute-start.14 = (bf16[96,3072]{1,0:T(8,128)(2,1)S(1)}, bf16[96,3072]{1,0:T(8,128)(2,1)S(1)}, u32[]{:S(2)}, u32[]{:S(2)}) collective-permute-start(bf16[96,3072]{1,0:T(8,128)(2,1)S(1)} %constant_dynamic-update-slice_fusion.4.refs_0_.refs_4_), channel_id=1, source_target_pairs={{0,16},{8,24},{16,0},{24,8},{1,17},{9,25},{17,1},{25,9},{2,18},{10... | collective-permute-start | bytes 1769480 | tf_op jit(solution)/shard_map/ppermute | solution.py:41
  60.9 15.8 %collective-permute-start.17 = (bf16[24,3072]{1,0:T(8,128)(2,1)S(1)}, bf16[24,3072]{1,0:T(8,128)(2,1)S(1)}, u32[]{:S(2)}, u32[]{:S(2)}) collective-permute-start(bf16[24,3072]{1,0:T(8,128)(2,1)S(1)} %get-tuple-element.165), channel_id=1, source_target_pairs={{0,6},{1,7},{2,4},{3,5},{4,2},{5,3},{6,0},{7,1},{8,14},{9,15},{10,... | collective-permute-start | bytes 442376 | tf_op jit(solution)/shard_map/ppermute | solution.py:46
  63.8 12.9 %collective-permute-start.16 = (bf16[24,3072]{1,0:T(8,128)(2,1)S(1)}, bf16[24,3072]{1,0:T(8,128)(2,1)S(1)}, u32[]{:S(2)}, u32[]{:S(2)}) collective-permute-start(bf16[24,3072]{1,0:T(8,128)(2,1)S(1)} %get-tuple-element.166), channel_id=1, source_target_pairs={{0,4},{1,5},{2,6},{3,7},{4,0},{5,1},{6,2},{7,3},{8,12},{9,13},{10,... | collective-permute-start | bytes 442376 | tf_op jit(solution)/shard_map/ppermute | solution.py:46
  63.8 12.9 %collective-permute-start.15 = (bf16[24,3072]{1,0:T(8,128)(2,1)S(1)}, bf16[24,3072]{1,0:T(8,128)(2,1)S(1)}, u32[]{:S(2)}, u32[]{:S(2)}) collective-permute-start(bf16[24,3072]{1,0:T(8,128)(2,1)S(1)} %get-tuple-element.167), channel_id=1, source_target_pairs={{0,2},{1,3},{2,0},{3,1},{4,6},{5,7},{6,4},{7,5},{8,10},{9,11},{10,... | collective-permute-start | bytes 442376 | tf_op jit(solution)/shard_map/ppermute | solution.py:46
  67.5 15.4 %collective-permute-start.19 = (bf16[96,3072]{1,0:T(8,128)(2,1)S(1)}, bf16[96,3072]{1,0:T(8,128)(2,1)S(1)}, u32[]{:S(2)}, u32[]{:S(2)}) collective-permute-start(bf16[96,3072]{1,0:T(8,128)(2,1)S(1)} %add_convert_fusion.3), channel_id=1, source_target_pairs={{0,16},{8,24},{16,0},{24,8},{1,17},{9,25},{17,1},{25,9},{2,18},{10... | collective-permute-start | bytes 1769480 | tf_op jit(solution)/shard_map/ppermute | solution.py:41
  87.3 16.2 %collective-permute-start.27 = (bf16[96,3072]{1,0:T(8,128)(2,1)S(1)}, bf16[96,3072]{1,0:T(8,128)(2,1)S(1)}, u32[]{:S(2)}, u32[]{:S(2)}) collective-permute-start(bf16[96,3072]{1,0:T(8,128)(2,1)S(1)} %add_convert_fusion.1), channel_id=1, source_target_pairs={{0,16},{8,24},{16,0},{24,8},{1,17},{9,25},{17,1},{25,9},{2,18},{10... | collective-permute-start | bytes 1769480 | tf_op jit(solution)/shard_map/ppermute | solution.py:41
  91.4 12.2 %collective-permute-start.24 = (bf16[24,3072]{1,0:T(8,128)(2,1)S(1)}, bf16[24,3072]{1,0:T(8,128)(2,1)S(1)}, u32[]{:S(2)}, u32[]{:S(2)}) collective-permute-start(bf16[24,3072]{1,0:T(8,128)(2,1)S(1)} %get-tuple-element.162), channel_id=1, source_target_pairs={{0,4},{1,5},{2,6},{3,7},{4,0},{5,1},{6,2},{7,3},{8,12},{9,13},{10,... | collective-permute-start | bytes 442376 | tf_op jit(solution)/shard_map/ppermute | solution.py:46
  91.4 12.2 %collective-permute-start.23 = (bf16[24,3072]{1,0:T(8,128)(2,1)S(1)}, bf16[24,3072]{1,0:T(8,128)(2,1)S(1)}, u32[]{:S(2)}, u32[]{:S(2)}) collective-permute-start(bf16[24,3072]{1,0:T(8,128)(2,1)S(1)} %get-tuple-element.163), channel_id=1, source_target_pairs={{0,2},{1,3},{2,0},{3,1},{4,6},{5,7},{6,4},{7,5},{8,10},{9,11},{10,... | collective-permute-start | bytes 442376 | tf_op jit(solution)/shard_map/ppermute | solution.py:46
  103.7 15.7 %collective-permute-start.32 = (bf16[96,3072]{1,0:T(8,128)(2,1)S(1)}, bf16[96,3072]{1,0:T(8,128)(2,1)S(1)}, u32[]{:S(2)}, u32[]{:S(2)}) collective-permute-start(bf16[96,3072]{1,0:T(8,128)(2,1)S(1)} %get-tuple-element.143.e0.refs_0_), channel_id=1, source_target_pairs={{0,16},{8,24},{16,0},{24,8},{1,17},{9,25},{17,1},{25,9},{2,18},{10... | collective-permute-start | bytes 1769480 | tf_op jit(solution)/shard_map/ppermute | solution.py:41
  106.1 13.3 %collective-permute-start.31 = (bf16[24,3072]{1,0:T(8,128)(2,1)S(1)}, bf16[24,3072]{1,0:T(8,128)(2,1)S(1)}, u32[]{:S(2)}, u32[]{:S(2)}) collective-permute-start(bf16[24,3072]{1,0:T(8,128)(2,1)S(1)} %get-tuple-element.157), channel_id=1, source_target_pairs={{0,6},{1,7},{2,4},{3,5},{4,2},{5,3},{6,0},{7,1},{8,14},{9,15},{10,... | collective-permute-start | bytes 442376 | tf_op jit(solution)/shard_map/ppermute | solution.py:46
  108.6 12.2 %collective-permute-start.30 = (bf16[24,3072]{1,0:T(8,128)(2,1)S(1)}, bf16[24,3072]{1,0:T(8,128)(2,1)S(1)}, u32[]{:S(2)}, u32[]{:S(2)}) collective-permute-start(bf16[24,3072]{1,0:T(8,128)(2,1)S(1)} %get-tuple-element.158), channel_id=1, source_target_pairs={{0,4},{1,5},{2,6},{3,7},{4,0},{5,1},{6,2},{7,3},{8,12},{9,13},{10,... | collective-permute-start | bytes 442376 | tf_op jit(solution)/shard_map/ppermute | solution.py:46
  108.6 12.2 %collective-permute-start.29 = (bf16[24,3072]{1,0:T(8,128)(2,1)S(1)}, bf16[24,3072]{1,0:T(8,128)(2,1)S(1)}, u32[]{:S(2)}, u32[]{:S(2)}) collective-permute-start(bf16[24,3072]{1,0:T(8,128)(2,1)S(1)} %get-tuple-element.159), channel_id=1, source_target_pairs={{0,2},{1,3},{2,0},{3,1},{4,6},{5,7},{6,4},{7,5},{8,10},{9,11},{10,... | collective-permute-start | bytes 442376 | tf_op jit(solution)/shard_map/ppermute | solution.py:46
  121.3 17.2 %collective-permute-start.35 = (bf16[96,3072]{1,0:T(8,128)(2,1)S(1)}, bf16[96,3072]{1,0:T(8,128)(2,1)}, u32[]{:S(2)}, u32[]{:S(2)}) collective-permute-start(bf16[96,3072]{1,0:T(8,128)(2,1)S(1)} %get-tuple-element.142.e0.refs_4_), channel_id=1, source_target_pairs={{0,8},{8,0},{16,24},{24,16},{1,9},{9,1},{17,25},{25,17},{2,10},{10... | collective-permute-start | bytes 1769480 | tf_op jit(solution)/shard_map/ppermute | solution.py:41
  121.4 17.1 %collective-permute-start.34 = (bf16[96,3072]{1,0:T(8,128)(2,1)S(1)}, bf16[96,3072]{1,0:T(8,128)(2,1)}, u32[]{:S(2)}, u32[]{:S(2)}) collective-permute-start(bf16[96,3072]{1,0:T(8,128)(2,1)S(1)} %get-tuple-element.142.e0.refs_4_), channel_id=1, source_target_pairs={{0,16},{8,24},{16,0},{24,8},{1,17},{9,25},{17,1},{25,9},{2,18},{10... | collective-permute-start | bytes 1769480 | tf_op jit(solution)/shard_map/ppermute | solution.py:41
  122.9 15.6 %collective-permute-start.33 = (bf16[96,3072]{1,0:T(8,128)(2,1)S(1)}, bf16[96,3072]{1,0:T(8,128)(2,1)}, u32[]{:S(2)}, u32[]{:S(2)}) collective-permute-start(bf16[96,3072]{1,0:T(8,128)(2,1)S(1)} %pad_maximum_fusion.1), channel_id=1, source_target_pairs={{0,1},{1,0},{2,3},{3,2},{4,5},{5,4},{6,7},{7,6},{8,9},{9,8},{10,11... | collective-permute-start | bytes 1769480 | tf_op jit(solution)/shard_map/ppermute | solution.py:46
  (38 other events, 331.0 us)

commit v3 on v2

v3 whole, which is shorter than its diff:
```python
import functools

import jax
import jax.numpy as jnp
from jax import lax
from jax.experimental import pallas as pl
from jax.experimental.pallas import tpu as pltpu
from jax.sharding import PartitionSpec as P

error_scale = 0.03125
absent_mark = 1024.0
GROUPS = 2
f32 = jnp.float32
bf16 = jnp.bfloat16
VMEM_LIMIT = 36 * 1024 * 1024
WEIGH = 10


def dot(a, b, on_a, on_b):
    return lax.dot_general(a, b, (((on_a,), (on_b,)), ((), ())), preferred_element_type=f32)


def call(kernel, name, out_shape, grid, in_specs, out_specs, scratch, flops, moved):
    return pl.pallas_call(
        kernel,
        name=name,
        out_shape=out_shape,
        grid=grid,
        in_specs=in_specs,
        out_specs=out_specs,
        scratch_shapes=scratch,
        cost_estimate=pl.CostEstimate(flops=WEIGH * flops, bytes_accessed=WEIGH * moved, transcendentals=0),
        compiler_params=pltpu.CompilerParams(
            vmem_limit_bytes=VMEM_LIMIT, dimension_semantics=("arbitrary",) * len(grid) or None
        ),
    )


def swap(v, distance):
    n = lax.axis_size("dp")
    return lax.ppermute(v, "dp", [(i, i ^ distance) for i in range(n)])


def pass_on(v, distance):
    n = lax.axis_size("expert")
    return lax.ppermute(v, "expert", [(i, i ^ distance) for i in range(n)])


def after(v, *first):
    return lax.optimization_barrier((v,) + first)[0]


def gate(values, *first):
    return list(lax.optimization_barrier(tuple(values) + first)[: len(values)])


def slot_row(route_row, capacity, pairs):
    tokens = route_row.shape[1]
    distance = route_row ^ lax.axis_index("expert")
    one_hot = (lax.broadcasted_iota(jnp.int32, (2 * pairs, tokens), 0) == distance).astype(f32)
    earlier = (
        lax.broadcasted_iota(jnp.int32, (tokens, tokens), 0)
        < lax.broadcasted_iota(jnp.int32, (tokens, tokens), 1)
    ).astype(bf16)
    before = dot(one_hot.astype(bf16), earlier, 1, 0)
    rank = jnp.sum(before * one_hot, axis=0, keepdims=True).astype(jnp.int32)
    return ((distance & 1) * pairs + (distance >> 1)) * capacity + rank


def store_parts(rows, outs):
    start = 0
    for out in outs:
        out[...] = rows[start : start + out.shape[0]].astype(bf16)
        start += out.shape[0]


def place_kernel(capacity, pairs, routes_ref, tokens_ref, by_slot_ref, *outs):
    slots, tokens = by_slot_ref.shape
    slot = slot_row(routes_ref[...], capacity, pairs)
    by_slot = (lax.broadcasted_iota(jnp.int32, (slots, tokens), 0) == slot).astype(f32).astype(bf16)
    by_slot_ref[...] = by_slot
    store_parts(dot(by_slot, tokens_ref[...], 1, 0), outs)


def place_target_kernel(by_slot_ref, target_ref, *outs):
    by_slot = by_slot_ref[...]
    mark = (1.0 - jnp.sum(by_slot.astype(f32), axis=1, keepdims=True)) * absent_mark
    store_parts(dot(by_slot, target_ref[...], 1, 0) + mark, outs)


def place(name, kernel, first, values, slots, pairs, with_slots):
    per_dev, features = values.shape
    capacity = slots // (2 * pairs)
    sizes = [capacity] * pairs if capacity % 8 == 0 else [slots // 2]
    sizes = sizes + [slots // 2]
    steps = 2
    cols = lambda rows: pl.BlockSpec((rows, features // steps), lambda i: (0, i))
    whole = lambda *shape: pl.BlockSpec(shape, lambda i: (0, 0))
    outs = call(
        kernel,
        name,
        [jax.ShapeDtypeStruct((slots, per_dev), bf16)] * with_slots
        + [jax.ShapeDtypeStruct((size, features), bf16) for size in sizes],
        (steps,),
        [whole(*first.shape), cols(per_dev)],
        [whole(slots, per_dev)] * with_slots + [cols(size) for size in sizes],
        [],
        2 * slots * per_dev * features,
        2 * (per_dev + slots) * features,
    )(first, values)
    direct, via = outs[with_slots:-1], outs[-1]
    if len(direct) == 1:
        direct = [direct[0][capacity * k : capacity * (k + 1)] for k in range(pairs)]
    return outs[0], list(direct), via


def clamp_parts(latent):
    squash = jax.nn.sigmoid(4.0 * latent)
    return (latent * squash).astype(bf16), squash + 4.0 * latent * squash * (1.0 - squash)


def forward_kernel(
    steps, mine, far, shift, shift_o, enc, enc_o, dec, dec_o, rows, pre, pre_o, keep, out, act, act_o
):
    i = pl.program_id(0)
    size = mine.shape[0]

    @pl.when(i < steps)
    def _():
        x = jnp.concatenate([mine[...], far[...]], axis=0)
        rows[...] = x
        part, part_o = dot(x, enc[...], 1, 0), dot(x, enc_o[...], 1, 0)

        @pl.when(i == 0)
        def _():
            pre[...] = part - shift[...]
            pre_o[...] = part_o - shift_o[...]

        @pl.when(i > 0)
        def _():
            pre[...] += part
            pre_o[...] += part_o

    @pl.when(i == steps - 1)
    def _():
        act[...] = clamp_parts(pre[...])[0]
        act_o[...] = clamp_parts(pre_o[...])[0]

    @pl.when(i >= steps)
    def _():
        part = dot(act[...], dec[...], 1, 1) + dot(act_o[...], dec_o[...], 1, 1)
        keep[...] = part[:size]
        out[...] = part[size:].astype(bf16)


def forward(mine, far, shifts, encs, decs):
    size, features = mine.shape
    latents = encs[0].shape[1]
    steps = 2
    wide = features // steps
    early = lambda i: jnp.minimum(i, steps - 1)
    late = lambda i: jnp.maximum(i - steps, 0)
    col_in = lambda rows: pl.BlockSpec((rows, wide), lambda i: (0, early(i)))
    fixed = lambda *shape: pl.BlockSpec(shape, lambda i: (0, 0))
    col_out = pl.BlockSpec((size, wide), lambda i: (0, late(i)))
    enc_in = pl.BlockSpec((wide, latents), lambda i: (early(i), 0))
    dec_in = pl.BlockSpec((wide, latents), lambda i: (late(i), 0))
    return call(
        functools.partial(forward_kernel, steps),
        "forward",
        [
            jax.ShapeDtypeStruct((2 * size, features), bf16),
            jax.ShapeDtypeStruct((2 * size, latents), f32),
            jax.ShapeDtypeStruct((2 * size, latents), f32),
            jax.ShapeDtypeStruct((size, features), f32),
            jax.ShapeDtypeStruct((size, features), bf16),
        ],
        (2 * steps,),
        [col_in(size)] * 2 + [fixed(1, latents)] * 2 + [enc_in] * 2 + [dec_in] * 2,
        [col_in(2 * size), fixed(2 * size, latents), fixed(2 * size, latents), col_out, col_out],
        [pltpu.VMEM((2 * size, latents), bf16)] * 2,
        2 * 2 * 4 * size * features * latents,
        8 * features * latents + 14 * size * features,
    )(mine, far, *shifts, *encs, *decs)


def make_error(keep, across, wanted):
    recon = (keep + across.astype(f32)).astype(bf16)
    goal = wanted.astype(f32)
    error = (recon.astype(f32) - goal) * error_scale
    return recon, jnp.where(goal < 0.5 * absent_mark, error, 0.0).astype(bf16)


def gradients_kernel(tiles, summed, *refs):
    errors, rows = refs[:4], refs[4:6]
    act, slope, dec = refs[6:9]
    before = refs[9:11] if summed else ()
    out_enc, out_dec = refs[9 + len(before) : 11 + len(before)]
    e_all, x_all, act_all, slope_all, dec_all, was, out_buf, sems, out_sems = refs[11 + len(before) :]
    features = errors[0].shape[1]
    cut = features // 2
    wide = features // tiles
    started = []

    def fetch(source, target):
        copy = pltpu.make_async_copy(source, target, sems.at[len(started)])
        copy.start()
        started.append(copy)
        return copy

    def fetch_rows(refs, target, columns):
        size = refs[0].shape[0]
        return [
            fetch(r.at[:, columns], target.at[pl.ds(size * j, size), columns]) for j, r in enumerate(refs)
        ]

    first = []
    for columns in (pl.ds(0, cut), pl.ds(cut, cut)):
        first.append(fetch_rows(errors, e_all, columns) + [fetch(dec.at[columns, :], dec_all.at[columns, :])])
    first[1].append(fetch(slope, slope_all))
    second = [fetch(act, act_all)]
    second += [fetch(before[1].at[0], was.at[1])] if summed else []
    third = fetch_rows(rows, x_all, pl.ds(0, features))
    third += [fetch(before[0].at[0], was.at[0])] if summed else []

    total = None
    for columns, copies in zip((slice(0, cut), slice(cut, features)), first):
        for copy in copies:
            copy.wait()
        part = dot(e_all[:, columns], dec_all[columns, :], 1, 0)
        total = part if total is None else total + part
    pre = (total * slope_all[...]).astype(bf16)

    pending = {}
    for n, (left, out, copies) in enumerate(((x_all, out_enc, third), (e_all, out_dec, second))[::-1]):
        for copy in copies:
            copy.wait()
        right = act_all[...] if n == 0 else pre
        for i in range(tiles):
            slot = (n * tiles + i) % 3
            if slot in pending:
                pending.pop(slot).wait()
            here = slice(i * wide, (i + 1) * wide)
            part = dot(left[:, here], right, 0, 0)
            if summed:
                part = part + was[1 - n, here, :].astype(f32)
            out_buf[slot] = part.astype(bf16)
            pending[slot] = pltpu.make_async_copy(
                out_buf.at[slot], out.at[0, pl.ds(i * wide, wide), :], out_sems.at[slot]
            )
            pending[slot].start()
    for copy in pending.values():
        copy.wait()


def gradients(errors, rows, act, slope, dec, before):
    size, features = errors[0].shape
    latents = dec.shape[1]
    tiles = 3
    summed = len(before) > 0
    anywhere = pl.BlockSpec(memory_space=pl.ANY)
    was = (2, features, latents) if summed else (2, 16, 128)
    return call(
        functools.partial(gradients_kernel, tiles, summed),
        "gradients_sum" if summed else "gradients",
        [jax.ShapeDtypeStruct((1, features, latents), bf16)] * 2,
        (),
        [anywhere] * (9 + len(before)),
        [anywhere] * 2,
        [
            pltpu.VMEM((4 * size, features), bf16),
            pltpu.VMEM((4 * size, features), bf16),
            pltpu.VMEM((4 * size, latents), bf16),
            pltpu.VMEM((4 * size, latents), f32),
            pltpu.VMEM((features, latents), bf16),
            pltpu.VMEM(was, bf16),
            pltpu.VMEM((3, features // tiles, latents), bf16),
            pltpu.SemaphoreType.DMA((16,)),
            pltpu.SemaphoreType.DMA((3,)),
        ],
        2 * 12 * size * features * latents,
        6 * features * latents + 32 * size * features,
    )(*errors, *rows, act, slope, dec, *before)


def collect_kernel(by_slot, direct, via, out):
    out[...] = dot(by_slot[...], jnp.concatenate([direct[...], via[...]], axis=0), 0, 0).astype(bf16)


def collect(by_slot, direct, via):
    slots, tokens = by_slot.shape
    features = direct.shape[1]
    steps = 2
    cols = lambda rows: pl.BlockSpec((rows, features // steps), lambda i: (0, i))
    return call(
        collect_kernel,
        "collect",
        jax.ShapeDtypeStruct((tokens, features), bf16),
        (steps,),
        [pl.BlockSpec((slots, tokens), lambda i: (0, 0)), cols(slots // 2), cols(slots // 2)],
        cols(tokens),
        [],
        2 * slots * tokens * features,
        2 * (slots + tokens) * features,
    )(by_slot, direct, via)


def local(tokens, target, routes, thresholds, enc_weight, dec_weight):
    experts = lax.axis_size("expert")
    half = lax.axis_size("dp") // 2
    per_dev, features = tokens.shape
    capacity = 3 * per_dev // (2 * experts)
    enc = enc_weight[0]
    dec = dec_weight[0]
    pairs = experts // 2
    slots = experts * capacity
    by_slot, direct, via = place(
        "place",
        functools.partial(place_kernel, capacity, pairs),
        routes.reshape(1, per_dev),
        tokens,
        slots,
        pairs,
        True,
    )
    _, goal_direct, goal_via = place(
        "place_target", place_target_kernel, by_slot, target, slots, pairs, False
    )

    def spread(parts, step=0):
        return [pass_on(v, 2 * k + step) if 2 * k + step else v for k, v in enumerate(parts)]

    def cut(v):
        return [v[capacity * k : capacity * (k + 1)] for k in range(pairs)]

    def join(arrays):
        return jnp.concatenate(arrays, axis=0)

    shift = 0.25 * thresholds.astype(f32)
    shift_o = swap(shift, 1)

    def gradient_side(pre, got):
        return clamp_parts(jnp.concatenate([pre, got], axis=0))

    out_direct = spread(direct)
    out_via = pass_on(via, 1)
    enc_o = swap(enc, 1)
    *out_direct, out_via, goal_via, shift_o, enc_o = gate(out_direct + [out_via, goal_via, shift_o, enc_o])
    mine0 = join(out_direct)
    out_via = spread(cut(out_via))
    far0 = swap(mine0, half)
    dec_o = swap(after(dec, enc_o), 1)
    *out_via, mine0, far0, goal_via, dec_o = gate(out_via + [mine0, far0, goal_via, dec_o])
    goal_direct = gate(goal_direct, dec_o)
    shifts, encs, decs = (shift, shift_o), (enc, enc_o), (dec, dec_o)
    mine1 = join(out_via)
    far1 = swap(mine1, half)
    goal_direct = spread(goal_direct)
    goal_via = pass_on(goal_via, 1)
    rows0, pre0, pre_o0, keep0, sum0 = forward(mine0, far0, shifts, encs, decs)
    *goal_direct, mine1, far1, keep0, sum0, goal_via, pre_o0 = gate(
        goal_direct + [mine1, far1, keep0, sum0, goal_via, pre_o0]
    )
    across0 = swap(sum0, half)
    got0 = swap(pre_o0, 1)
    goal_via = spread(cut(after(goal_via, got0)))
    rows1, pre1, pre_o1, keep1, sum1 = forward(mine1, far1, shifts, encs, decs)
    *goal_via, across0, sum1, got0, pre_o1, rows0 = gate(goal_via + [across0, sum1, got0, pre_o1, rows0])
    across1 = swap(sum1, half)
    recon0, error0 = make_error(keep0, across0, join(goal_direct))
    home0 = spread(cut(recon0))
    got1 = swap(pre_o1, 1)
    act0, slope0 = gradient_side(pre0, got0)
    *home0, across1, error0, got1, slope0 = gate(home0 + [across1, error0, got1, slope0])
    efar0 = swap(error0, half)
    recon1, error1 = make_error(keep1, across1, join(goal_via))
    home_via = cut(recon1)
    home1 = [pass_on(home_via[k], 2 * k + 1) for k in range(1, pairs)]
    act1, slope1 = gradient_side(pre1, got1)
    *home1, home_via[0], error0, efar0, error1, slope1, rows0, rows1 = gate(
        home1 + [home_via[0], error0, efar0, error1, slope1, rows0, rows1]
    )
    efar1 = swap(error1, half)
    home1 = [pass_on(home_via[0], 1)] + home1
    errors0 = [error0, efar0, swap(error0, 1), swap(efar0, 1)]
    before = gradients(errors0, [rows0, swap(rows0, 1)], act0, slope0, dec, ())
    core1 = swap(after(rows1, errors0[3]), 1)
    enear1 = swap(after(error1, errors0[3]), 1)
    homes = gate([join(home0), join(home1)], before[0])
    recon = collect(by_slot, *homes)
    efar1, enear1, recon, core1, *before = gate([efar1, enear1, recon, core1, *before])
    errors1 = [error1, efar1, enear1, swap(efar1, 1)]
    grad_enc, grad_dec = gradients(errors1, [rows1, core1], act1, slope1, dec, before)
    return recon, grad_enc, grad_dec


def solution(mesh):
    in_specs = (
        P(("dp", "expert"), None),
        P(("dp", "expert"), None),
        P(("dp", "expert"), None),
        P("expert", "dp"),
        P("expert", None, "dp"),
        P("expert", None, "dp"),
    )
    out_specs = (P(("dp", "expert"), None), P("expert", None, "dp"), P("expert", None, "dp"))
    return jax.shard_map(local, mesh=mesh, in_specs=in_specs, out_specs=out_specs, check_vma=False)
```

time: 161 us -> 138 us (0.86)
  Pallas kernels: 47 us -> 29.4 us
  waiting for transfers between devices: 67.2 us -> 62.9 us
  other arithmetic: 3.31 us -> 1.4 us
    ppermute x18 -> x17, waiting for transfers between devices: 27.6 us -> 7.44 us  [swap(): return lax.ppermute(v, 'dp', [(i, i ^ distance) for i in range(n)])]
    ppermute x21, waiting for transfers between devices: 39.6 us -> 55.5 us  [pass_on(): return lax.ppermute(v, 'expert', [(i, i ^ distance) for i in range(n)])]
    pallas_call x6 -> x4, Pallas kernels: 39.5 us -> 26.1 us  [the longest x2 16.6 us: gradients(): call(functools.partial(gradients_kernel, tiles, summed), 'gradients_sum'...]
    pallas_call x2, Pallas kernels: 5.11 us -> 1.84 us  [place(): call(kernel, name, [jax.ShapeDtypeStruct((slots, per_dev), bf16)] * with_...]
    ppermute x18 -> x17, starting transfers between devices: 8.07 us -> 8.82 us  [swap(): return lax.ppermute(v, 'dp', [(i, i ^ distance) for i in range(n)])]
  transfers between devices with their start and end apart: 39 -> 38, of which waited for: 17 -> 16; matrix products, arithmetic and copies ran while one was open for 2% -> 1% of each run, Pallas kernels for 16% -> 15%
where the time goes in v3:
time: 138 us
  waiting for transfers between devices  62.9 us (46%)
  starting transfers between devices  40.8 us (30%)
  Pallas kernels  29.4 us (21%)
  local copies, waits for them, and re-layouts  2.18 us (2%)
  other arithmetic  1.4 us (1%)
    ppermute x21, waiting for transfers between devices, pass_on(): return lax.ppermute(v, 'expert', [(i, i ^ distance) for i in range(n)])  55.5 us
    ppermute x21, starting transfers between devices, pass_on(): return lax.ppermute(v, 'expert', [(i, i ^ distance) for i in range(n)])  32 us
    pallas_call x2, Pallas kernels, gradients(): call(functools.partial(gradients_kernel, tiles, summed), 'gradients_sum'...  16.6 us
    pallas_call x2, Pallas kernels, forward(): call(functools.partial(forward_kernel, steps), 'forward', [jax.ShapeDtype...  9.54 us
    ppermute x17, starting transfers between devices, swap(): return lax.ppermute(v, 'dp', [(i, i ^ distance) for i in range(n)])  8.82 us
    ppermute x17, waiting for transfers between devices, swap(): return lax.ppermute(v, 'dp', [(i, i ^ distance) for i in range(n)])  7.44 us
  transfers between devices with their start and end apart: 38, of which 16 were waited for; matrix products, arithmetic and copies ran while one was open for 1% of the time, Pallas kernels for 15%

profile of v3, /device:TPU:0, one launch (start us, length us, event | category | flops | bytes accessed | tf_op | source)
XLA Modules:
  0.0 137.8 jit_solution(10784767488710306746)
XLA Ops:
  4.0 2.6 %collective-permute-start.3 = (bf16[96,3072]{1,0:T(8,128)(2,1)S(1)}, bf16[96,3072]{1,0:T(8,128)(2,1)S(1)}, u32[]{:S(2)}, u32[]{:S(2)}) collective-permute-start(bf16[96,3072]{1,0:T(8,128)(2,1)S(1)} %get-tuple-element.106), channel_id=1, source_target_pairs={{0,1},{1,0},{2,3},{3,2},{4,5},{5,4},{6,7},{7,6},{8,9},{9,8},{10,11... | collective-permute-start | bytes 1769480 | tf_op jit(solution)/shard_map/ppermute | solution.py:46
  8.4 2.6 %collective-permute-start.1 = (bf16[24,3072]{1,0:T(8,128)(2,1)S(1)}, bf16[24,3072]{1,0:T(8,128)(2,1)S(1)}, u32[]{:S(2)}, u32[]{:S(2)}) collective-permute-start(bf16[24,3072]{1,0:T(8,128)(2,1)S(1)} %get-tuple-element.104), channel_id=1, source_target_pairs={{0,4},{1,5},{2,6},{3,7},{4,0},{5,1},{6,2},{7,3},{8,12},{9,13},{10,... | collective-permute-start | bytes 442376 | tf_op jit(solution)/shard_map/ppermute | solution.py:46
  12.2 3.2 %collective-permute-done = bf16[24,3072]{1,0:T(8,128)(2,1)S(1)} collective-permute-done((bf16[24,3072]{1,0:T(8,128)(2,1)S(1)}, bf16[24,3072]{1,0:T(8,128)(2,1)S(1)}, u32[]{:S(2)}, u32[]{:S(2)}) %collective-permute-start) | collective-permute-done | bytes 147488 | tf_op jit(solution)/shard_map/ppermute | solution.py:46
  15.4 6.9 %collective-permute-done.1 = bf16[24,3072]{1,0:T(8,128)(2,1)S(1)} collective-permute-done((bf16[24,3072]{1,0:T(8,128)(2,1)S(1)}, bf16[24,3072]{1,0:T(8,128)(2,1)S(1)}, u32[]{:S(2)}, u32[]{:S(2)}) %collective-permute-start.1) | collective-permute-done | bytes 147488 | tf_op jit(solution)/shard_map/ppermute | solution.py:46
  24.2 2.5 %collective-permute-start.8 = (bf16[24,3072]{1,0:T(8,128)(2,1)S(1)}, bf16[24,3072]{1,0:T(8,128)(2,1)S(1)}, u32[]{:S(2)}, u32[]{:S(2)}) collective-permute-start(bf16[24,3072]{1,0:T(8,128)(2,1)S(1)} %get-tuple-element.211), channel_id=1, source_target_pairs={{0,6},{1,7},{2,4},{3,5},{4,2},{5,3},{6,0},{7,1},{8,14},{9,15},{10,... | collective-permute-start | bytes 442376 | tf_op jit(solution)/shard_map/ppermute | solution.py:46
  28.6 4.0 %collective-permute-done.8 = bf16[24,3072]{1,0:T(8,128)(2,1)S(1)} collective-permute-done((bf16[24,3072]{1,0:T(8,128)(2,1)S(1)}, bf16[24,3072]{1,0:T(8,128)(2,1)S(1)}, u32[]{:S(2)}, u32[]{:S(2)}) %collective-permute-start.8) | collective-permute-done | bytes 147488 | tf_op jit(solution)/shard_map/ppermute | solution.py:46
  32.6 8.9 %collective-permute-done.7 = bf16[24,3072]{1,0:T(8,128)(2,1)S(1)} collective-permute-done((bf16[24,3072]{1,0:T(8,128)(2,1)S(1)}, bf16[24,3072]{1,0:T(8,128)(2,1)S(1)}, u32[]{:S(2)}, u32[]{:S(2)}) %collective-permute-start.7) | collective-permute-done | bytes 147488 | tf_op jit(solution)/shard_map/ppermute | solution.py:46
  41.6 3.0 %collective-permute-start.12 = (bf16[24,3072]{1,0:T(8,128)(2,1)S(1)}, bf16[24,3072]{1,0:T(8,128)(2,1)S(1)}, u32[]{:S(2)}, u32[]{:S(2)}) collective-permute-start(bf16[24,3072]{1,0:T(8,128)(2,1)S(1)} %get-tuple-element.119), channel_id=1, source_target_pairs={{0,4},{1,5},{2,6},{3,7},{4,0},{5,1},{6,2},{7,3},{8,12},{9,13},{10,... | collective-permute-start | bytes 442376 | tf_op jit(solution)/shard_map/ppermute | solution.py:46
  47.1 4.8 %forward.2 = (bf16[192,3072]{1,0:T(8,128)(2,1)S(1)}, f32[192,512]{1,0:T(8,128)S(1)}, f32[192,512]{1,0:T(8,128)S(1)}, f32[96,3072]{1,0:T(8,128)S(1)}, bf16[96,3072]{1,0:T(8,128)(2,1)S(1)}) custom-call(bf16[96,3072]{1,0:T(8,128)(2,1)S(1)} %constant_dynamic-update-slice_fusion.mine, bf16[96,3072]{1,0:T(8,128)(2,1)S(1)} %collective-permute-done.9.far, ...), custom_call_target="tpu_custom_call" | custom-call | flops 24159191040 | bytes 167116800 | tf_op jit(solution)/shard_map/forward/pallas_call | solution.py:168
  51.9 3.7 %collective-permute-done.12 = bf16[24,3072]{1,0:T(8,128)(2,1)S(1)} collective-permute-done((bf16[24,3072]{1,0:T(8,128)(2,1)S(1)}, bf16[24,3072]{1,0:T(8,128)(2,1)S(1)}, u32[]{:S(2)}, u32[]{:S(2)}) %collective-permute-start.12) | collective-permute-done | bytes 147488 | tf_op jit(solution)/shard_map/ppermute | solution.py:46
  55.6 4.9 %collective-permute-done.14.far = bf16[96,3072]{1,0:T(8,128)(2,1)S(1)} collective-permute-done((bf16[96,3072]{1,0:T(8,128)(2,1)S(1)}, bf16[96,3072]{1,0:T(8,128)(2,1)S(1)}, u32[]{:S(2)}, u32[]{:S(2)}) %collective-permute-start.14) | collective-permute-done | bytes 589856 | tf_op jit(solution)/shard_map/ppermute | solution.py:41
  62.5 2.5 %collective-permute-start.19 = (bf16[24,3072]{1,0:T(8,128)(2,1)S(1)}, bf16[24,3072]{1,0:T(8,128)(2,1)S(1)}, u32[]{:S(2)}, u32[]{:S(2)}) collective-permute-start(bf16[24,3072]{1,0:T(8,128)(2,1)S(1)} %get-tuple-element.207), channel_id=1, source_target_pairs={{0,6},{1,7},{2,4},{3,5},{4,2},{5,3},{6,0},{7,1},{8,14},{9,15},{10,... | collective-permute-start | bytes 442376 | tf_op jit(solution)/shard_map/ppermute | solution.py:46
  67.0 4.8 %forward.3 = (bf16[192,3072]{1,0:T(8,128)(2,1)S(1)}, f32[192,512]{1,0:T(8,128)S(1)}, f32[192,512]{1,0:T(8,128)S(1)}, f32[96,3072]{1,0:T(8,128)S(1)}, bf16[96,3072]{1,0:T(8,128)(2,1)S(1)}) custom-call(bf16[96,3072]{1,0:T(8,128)(2,1)S(1)} %constant_dynamic-update-slice_fusion.4.mine, bf16[96,3072]{1,0:T(8,128)(2,1)S(1)} %collective-permute-done.14.far, ...), custom_call_target="tpu_custom_call" | custom-call | flops 24159191040 | bytes 167116800 | tf_op jit(solution)/shard_map/forward/pallas_call | solution.py:168
  71.8 5.1 %collective-permute-done.18 = bf16[24,3072]{1,0:T(8,128)(2,1)S(1)} collective-permute-done((bf16[24,3072]{1,0:T(8,128)(2,1)S(1)}, bf16[24,3072]{1,0:T(8,128)(2,1)S(1)}, u32[]{:S(2)}, u32[]{:S(2)}) %collective-permute-start.18) | collective-permute-done | bytes 147488 | tf_op jit(solution)/shard_map/ppermute | solution.py:46
  78.9 2.5 %collective-permute-start.23 = (bf16[24,3072]{1,0:T(8,128)(2,1)S(1)}, bf16[24,3072]{1,0:T(8,128)(2,1)S(1)}, u32[]{:S(2)}, u32[]{:S(2)}) collective-permute-start(bf16[24,3072]{1,0:T(8,128)(2,1)S(1)} %get-tuple-element.203), channel_id=1, source_target_pairs={{0,6},{1,7},{2,4},{3,5},{4,2},{5,3},{6,0},{7,1},{8,14},{9,15},{10,... | collective-permute-start | bytes 442376 | tf_op jit(solution)/shard_map/ppermute | solution.py:46
  83.7 3.9 %collective-permute-done.23 = bf16[24,3072]{1,0:T(8,128)(2,1)S(1)} collective-permute-done((bf16[24,3072]{1,0:T(8,128)(2,1)S(1)}, bf16[24,3072]{1,0:T(8,128)(2,1)S(1)}, u32[]{:S(2)}, u32[]{:S(2)}) %collective-permute-start.23) | collective-permute-done | bytes 147488 | tf_op jit(solution)/shard_map/ppermute | solution.py:46
  87.6 6.7 %collective-permute-done.22 = bf16[24,3072]{1,0:T(8,128)(2,1)S(1)} collective-permute-done((bf16[24,3072]{1,0:T(8,128)(2,1)S(1)}, bf16[24,3072]{1,0:T(8,128)(2,1)S(1)}, u32[]{:S(2)}, u32[]{:S(2)}) %collective-permute-start.22) | collective-permute-done | bytes 147488 | tf_op jit(solution)/shard_map/ppermute | solution.py:46
  95.2 2.1 %collective-permute-start.28 = (bf16[24,3072]{1,0:T(8,128)(2,1)S(1)}, bf16[24,3072]{1,0:T(8,128)(2,1)S(1)}, u32[]{:S(2)}, u32[]{:S(2)}) collective-permute-start(bf16[24,3072]{1,0:T(8,128)(2,1)S(1)} %get-tuple-element.200), channel_id=1, source_target_pairs={{0,7},{1,6},{2,5},{3,4},{4,3},{5,2},{6,1},{7,0},{8,15},{9,14},{10,... | collective-permute-start | bytes 442376 | tf_op jit(solution)/shard_map/ppermute | solution.py:46
  97.4 3.4 %collective-permute-start.26 = (bf16[24,3072]{1,0:T(8,128)(2,1)S(1)}, bf16[24,3072]{1,0:T(8,128)(2,1)S(1)}, u32[]{:S(2)}, u32[]{:S(2)}) collective-permute-start(bf16[24,3072]{1,0:T(8,128)(2,1)S(1)} %get-tuple-element.202), channel_id=1, source_target_pairs={{0,3},{1,2},{2,1},{3,0},{4,7},{5,6},{6,5},{7,4},{8,11},{9,10},{10,... | collective-permute-start | bytes 442376 | tf_op jit(solution)/shard_map/ppermute | solution.py:46
  101.2 3.6 %collective-permute-done.28 = bf16[24,3072]{1,0:T(8,128)(2,1)S(1)} collective-permute-done((bf16[24,3072]{1,0:T(8,128)(2,1)S(1)}, bf16[24,3072]{1,0:T(8,128)(2,1)S(1)}, u32[]{:S(2)}, u32[]{:S(2)}) %collective-permute-start.28) | collective-permute-done | bytes 147488 | tf_op jit(solution)/shard_map/ppermute | solution.py:46
  104.8 5.5 %collective-permute-done.27 = bf16[24,3072]{1,0:T(8,128)(2,1)S(1)} collective-permute-done((bf16[24,3072]{1,0:T(8,128)(2,1)S(1)}, bf16[24,3072]{1,0:T(8,128)(2,1)S(1)}, u32[]{:S(2)}, u32[]{:S(2)}) %collective-permute-start.27) | collective-permute-done | bytes 147488 | tf_op jit(solution)/shard_map/ppermute | solution.py:46
  112.8 3.8 %collective-permute-done.33 = bf16[24,3072]{1,0:T(8,128)(2,1)S(1)} collective-permute-done((bf16[24,3072]{1,0:T(8,128)(2,1)S(1)}, bf16[24,3072]{1,0:T(8,128)(2,1)S(1)}, u32[]{:S(2)}, u32[]{:S(2)}) %collective-permute-start.33) | collective-permute-done | bytes 147488 | tf_op jit(solution)/shard_map/ppermute | solution.py:46
  117.2 8.1 %gradients.1 = (bf16[1,3072,512]{2,1,0:T(8,128)(2,1)S(1)}, bf16[1,3072,512]{2,1,0:T(8,128)(2,1)S(1)}) custom-call(bf16[96,3072]{1,0:T(8,128)(2,1)S(1)} %get-tuple-element.173.refs_0_, bf16[96,3072]{1,0:T(8,128)(2,1)S(1)} %collective-permute-done.29.refs_1_, bf16[96,3072]{1,0:T(8,128)(2,1)S(1)} %collective-permute-done.34.refs_2_, ...), custom_call_target="tpu_custom_call" | custom-call | flops 36238786560 | bytes 188743680 | tf_op jit(solution)/shard_map/gradients/pallas_call | solution.py:263
  129.2 8.5 %gradients_sum.1 = (bf16[1,3072,512]{2,1,0:T(8,128)(2,1)}, bf16[1,3072,512]{2,1,0:T(8,128)(2,1)}) custom-call(bf16[96,3072]{1,0:T(8,128)(2,1)S(1)} %get-tuple-element.164.refs_0_, bf16[96,3072]{1,0:T(8,128)(2,1)S(1)} %collective-permute-done.30.refs_1_, bf16[96,3072]{1,0:T(8,128)(2,1)S(1)} %collective-permute-done.32.refs_2_, ...), custom_call_target="tpu_custom_call" | custom-call | flops 36238786560 | bytes 188743680 | tf_op jit(solution)/shard_map/gradients_sum/pallas_call | solution.py:263
  (98 shorter events, 29.2 us)
Async XLA Ops:
  0.6 21.8 %collective-permute-start.5 = (bf16[3072,512]{1,0:T(8,128)(2,1)}, bf16[3072,512]{1,0:T(8,128)(2,1)S(1)}, u32[]{:S(2)}, u32[]{:S(2)}) collective-permute-start(bf16[3072,512]{1,0:T(8,128)(2,1)} %bitcast.3), channel_id=1, source_target_pairs={{0,8},{8,0},{16,24},{24,16},{1,9},{9,1},{17,25},{25,17},{2,10},{10... | collective-permute-start | bytes 9437192 | tf_op jit(solution)/shard_map/ppermute | solution.py:41
  4.0 18.4 %collective-permute-start.3 = (bf16[96,3072]{1,0:T(8,128)(2,1)S(1)}, bf16[96,3072]{1,0:T(8,128)(2,1)S(1)}, u32[]{:S(2)}, u32[]{:S(2)}) collective-permute-start(bf16[96,3072]{1,0:T(8,128)(2,1)S(1)} %get-tuple-element.106), channel_id=1, source_target_pairs={{0,1},{1,0},{2,3},{3,2},{4,5},{5,4},{6,7},{7,6},{8,9},{9,8},{10,11... | collective-permute-start | bytes 1769480 | tf_op jit(solution)/shard_map/ppermute | solution.py:46
  8.4 14.0 %collective-permute-start.1 = (bf16[24,3072]{1,0:T(8,128)(2,1)S(1)}, bf16[24,3072]{1,0:T(8,128)(2,1)S(1)}, u32[]{:S(2)}, u32[]{:S(2)}) collective-permute-start(bf16[24,3072]{1,0:T(8,128)(2,1)S(1)} %get-tuple-element.104), channel_id=1, source_target_pairs={{0,4},{1,5},{2,6},{3,7},{4,0},{5,1},{6,2},{7,3},{8,12},{9,13},{10,... | collective-permute-start | bytes 442376 | tf_op jit(solution)/shard_map/ppermute | solution.py:46
  11.0 11.4 %collective-permute-start.2 = (bf16[24,3072]{1,0:T(8,128)(2,1)S(1)}, bf16[24,3072]{1,0:T(8,128)(2,1)S(1)}, u32[]{:S(2)}, u32[]{:S(2)}) collective-permute-start(bf16[24,3072]{1,0:T(8,128)(2,1)S(1)} %get-tuple-element.105), channel_id=1, source_target_pairs={{0,6},{1,7},{2,4},{3,5},{4,2},{5,3},{6,0},{7,1},{8,14},{9,15},{10,... | collective-permute-start | bytes 442376 | tf_op jit(solution)/shard_map/ppermute | solution.py:46
  22.4 19.1 %collective-permute-start.10 = (bf16[3072,512]{1,0:T(8,128)(2,1)S(1)}, bf16[3072,512]{1,0:T(8,128)(2,1)S(1)}, u32[]{:S(2)}, u32[]{:S(2)}) collective-permute-start(bf16[3072,512]{1,0:T(8,128)(2,1)S(1)} %bitcast.6), channel_id=1, source_target_pairs={{0,8},{8,0},{16,24},{24,16},{1,9},{9,1},{17,25},{25,17},{2,10},{10... | collective-permute-start | bytes 9437192 | tf_op jit(solution)/shard_map/ppermute | solution.py:41
  22.6 18.9 %collective-permute-start.9 = (bf16[96,3072]{1,0:T(8,128)(2,1)S(1)}, bf16[96,3072]{1,0:T(8,128)(2,1)S(1)}, u32[]{:S(2)}, u32[]{:S(2)}) collective-permute-start(bf16[96,3072]{1,0:T(8,128)(2,1)S(1)} %constant_dynamic-update-slice_fusion.mine), channel_id=1, source_target_pairs={{0,16},{8,24},{16,0},{24,8},{1,17},{9,25},{17,1},{25,9},{2,18},{10... | collective-permute-start | bytes 1769480 | tf_op jit(solution)/shard_map/ppermute | solution.py:41
  26.7 14.8 %collective-permute-start.7 = (bf16[24,3072]{1,0:T(8,128)(2,1)S(1)}, bf16[24,3072]{1,0:T(8,128)(2,1)S(1)}, u32[]{:S(2)}, u32[]{:S(2)}) collective-permute-start(bf16[24,3072]{1,0:T(8,128)(2,1)S(1)} %get-tuple-element.212), channel_id=1, source_target_pairs={{0,4},{1,5},{2,6},{3,7},{4,0},{5,1},{6,2},{7,3},{8,12},{9,13},{10,... | collective-permute-start | bytes 442376 | tf_op jit(solution)/shard_map/ppermute | solution.py:46
  28.5 13.0 %collective-permute-start.6 = (bf16[24,3072]{1,0:T(8,128)(2,1)S(1)}, bf16[24,3072]{1,0:T(8,128)(2,1)S(1)}, u32[]{:S(2)}, u32[]{:S(2)}) collective-permute-start(bf16[24,3072]{1,0:T(8,128)(2,1)S(1)} %get-tuple-element.213), channel_id=1, source_target_pairs={{0,2},{1,3},{2,0},{3,1},{4,6},{5,7},{6,4},{7,5},{8,10},{9,11},{10,... | collective-permute-start | bytes 442376 | tf_op jit(solution)/shard_map/ppermute | solution.py:46
  41.6 14.1 %collective-permute-start.12 = (bf16[24,3072]{1,0:T(8,128)(2,1)S(1)}, bf16[24,3072]{1,0:T(8,128)(2,1)S(1)}, u32[]{:S(2)}, u32[]{:S(2)}) collective-permute-start(bf16[24,3072]{1,0:T(8,128)(2,1)S(1)} %get-tuple-element.119), channel_id=1, source_target_pairs={{0,4},{1,5},{2,6},{3,7},{4,0},{5,1},{6,2},{7,3},{8,12},{9,13},{10,... | collective-permute-start | bytes 442376 | tf_op jit(solution)/shard_map/ppermute | solution.py:46
  44.6 11.1 %collective-permute-start.13 = (bf16[24,3072]{1,0:T(8,128)(2,1)S(1)}, bf16[24,3072]{1,0:T(8,128)(2,1)S(1)}, u32[]{:S(2)}, u32[]{:S(2)}) collective-permute-start(bf16[24,3072]{1,0:T(8,128)(2,1)S(1)} %get-tuple-element.120), channel_id=1, source_target_pairs={{0,6},{1,7},{2,4},{3,5},{4,2},{5,3},{6,0},{7,1},{8,14},{9,15},{10,... | collective-permute-start | bytes 442376 | tf_op jit(solution)/shard_map/ppermute | solution.py:46
  46.0 14.5 %collective-permute-start.14 = (bf16[96,3072]{1,0:T(8,128)(2,1)S(1)}, bf16[96,3072]{1,0:T(8,128)(2,1)S(1)}, u32[]{:S(2)}, u32[]{:S(2)}) collective-permute-start(bf16[96,3072]{1,0:T(8,128)(2,1)S(1)} %constant_dynamic-update-slice_fusion.4.mine), channel_id=1, source_target_pairs={{0,16},{8,24},{16,0},{24,8},{1,17},{9,25},{17,1},{25,9},{2,18},{10... | collective-permute-start | bytes 1769480 | tf_op jit(solution)/shard_map/ppermute | solution.py:41
  46.6 14.2 %collective-permute-start.15 = (bf16[96,3072]{1,0:T(8,128)(2,1)S(1)}, bf16[96,3072]{1,0:T(8,128)(2,1)S(1)}, u32[]{:S(2)}, u32[]{:S(2)}) collective-permute-start(bf16[96,3072]{1,0:T(8,128)(2,1)S(1)} %get-tuple-element.130), channel_id=1, source_target_pairs={{0,1},{1,0},{2,3},{3,2},{4,5},{5,4},{6,7},{7,6},{8,9},{9,8},{10,11... | collective-permute-start | bytes 1769480 | tf_op jit(solution)/shard_map/ppermute | solution.py:46
  60.8 16.1 %collective-permute-start.20 = (bf16[96,3072]{1,0:T(8,128)(2,1)S(1)}, bf16[96,3072]{1,0:T(8,128)(2,1)S(1)}, u32[]{:S(2)}, u32[]{:S(2)}) collective-permute-start(bf16[96,3072]{1,0:T(8,128)(2,1)S(1)} %get-tuple-element.139), channel_id=1, source_target_pairs={{0,16},{8,24},{16,0},{24,8},{1,17},{9,25},{17,1},{25,9},{2,18},{10... | collective-permute-start | bytes 1769480 | tf_op jit(solution)/shard_map/ppermute | solution.py:41
  65.1 11.8 %collective-permute-start.18 = (bf16[24,3072]{1,0:T(8,128)(2,1)S(1)}, bf16[24,3072]{1,0:T(8,128)(2,1)S(1)}, u32[]{:S(2)}, u32[]{:S(2)}) collective-permute-start(bf16[24,3072]{1,0:T(8,128)(2,1)S(1)} %get-tuple-element.208), channel_id=1, source_target_pairs={{0,4},{1,5},{2,6},{3,7},{4,0},{5,1},{6,2},{7,3},{8,12},{9,13},{10,... | collective-permute-start | bytes 442376 | tf_op jit(solution)/shard_map/ppermute | solution.py:46
  65.1 11.8 %collective-permute-start.17 = (bf16[24,3072]{1,0:T(8,128)(2,1)S(1)}, bf16[24,3072]{1,0:T(8,128)(2,1)S(1)}, u32[]{:S(2)}, u32[]{:S(2)}) collective-permute-start(bf16[24,3072]{1,0:T(8,128)(2,1)S(1)} %get-tuple-element.209), channel_id=1, source_target_pairs={{0,2},{1,3},{2,0},{3,1},{4,6},{5,7},{6,4},{7,5},{8,10},{9,11},{10,... | collective-permute-start | bytes 442376 | tf_op jit(solution)/shard_map/ppermute | solution.py:46
  76.9 17.3 %collective-permute-start.25 = (f32[192,512]{1,0:T(8,128)S(1)}, f32[192,512]{1,0:T(8,128)S(1)}, u32[]{:S(2)}, u32[]{:S(2)}) collective-permute-start(f32[192,512]{1,0:T(8,128)S(1)} %get-tuple-element.149), channel_id=1, source_target_pairs={{0,8},{8,0},{16,24},{24,16},{1,9},{9,1},{17,25},{25,17},{2,10},{10... | collective-permute-start | bytes 1179656 | tf_op jit(solution)/shard_map/ppermute | solution.py:41
  76.9 17.3 %collective-permute-start.24 = (bf16[96,3072]{1,0:T(8,128)(2,1)S(1)}, bf16[96,3072]{1,0:T(8,128)(2,1)S(1)}, u32[]{:S(2)}, u32[]{:S(2)}) collective-permute-start(bf16[96,3072]{1,0:T(8,128)(2,1)S(1)} %get-tuple-element.144), channel_id=1, source_target_pairs={{0,16},{8,24},{16,0},{24,8},{1,17},{9,25},{17,1},{25,9},{2,18},{10... | collective-permute-start | bytes 1769480 | tf_op jit(solution)/shard_map/ppermute | solution.py:41
  81.4 12.9 %collective-permute-start.22 = (bf16[24,3072]{1,0:T(8,128)(2,1)S(1)}, bf16[24,3072]{1,0:T(8,128)(2,1)S(1)}, u32[]{:S(2)}, u32[]{:S(2)}) collective-permute-start(bf16[24,3072]{1,0:T(8,128)(2,1)S(1)} %get-tuple-element.204), channel_id=1, source_target_pairs={{0,4},{1,5},{2,6},{3,7},{4,0},{5,1},{6,2},{7,3},{8,12},{9,13},{10,... | collective-permute-start | bytes 442376 | tf_op jit(solution)/shard_map/ppermute | solution.py:46
  81.4 12.9 %collective-permute-start.21 = (bf16[24,3072]{1,0:T(8,128)(2,1)S(1)}, bf16[24,3072]{1,0:T(8,128)(2,1)S(1)}, u32[]{:S(2)}, u32[]{:S(2)}) collective-permute-start(bf16[24,3072]{1,0:T(8,128)(2,1)S(1)} %get-tuple-element.205), channel_id=1, source_target_pairs={{0,2},{1,3},{2,0},{3,1},{4,6},{5,7},{6,4},{7,5},{8,10},{9,11},{10,... | collective-permute-start | bytes 442376 | tf_op jit(solution)/shard_map/ppermute | solution.py:46
  94.2 16.0 %collective-permute-start.29 = (bf16[96,3072]{1,0:T(8,128)(2,1)S(1)}, bf16[96,3072]{1,0:T(8,128)(2,1)S(1)}, u32[]{:S(2)}, u32[]{:S(2)}) collective-permute-start(bf16[96,3072]{1,0:T(8,128)(2,1)S(1)} %get-tuple-element.173.refs_0_), channel_id=1, source_target_pairs={{0,16},{8,24},{16,0},{24,8},{1,17},{9,25},{17,1},{25,9},{2,18},{10... | collective-permute-start | bytes 1769480 | tf_op jit(solution)/shard_map/ppermute | solution.py:41
  97.3 12.9 %collective-permute-start.27 = (bf16[24,3072]{1,0:T(8,128)(2,1)S(1)}, bf16[24,3072]{1,0:T(8,128)(2,1)S(1)}, u32[]{:S(2)}, u32[]{:S(2)}) collective-permute-start(bf16[24,3072]{1,0:T(8,128)(2,1)S(1)} %get-tuple-element.201), channel_id=1, source_target_pairs={{0,5},{1,4},{2,7},{3,6},{4,1},{5,0},{6,3},{7,2},{8,13},{9,12},{10,... | collective-permute-start | bytes 442376 | tf_op jit(solution)/shard_map/ppermute | solution.py:46
  97.4 12.8 %collective-permute-start.26 = (bf16[24,3072]{1,0:T(8,128)(2,1)S(1)}, bf16[24,3072]{1,0:T(8,128)(2,1)S(1)}, u32[]{:S(2)}, u32[]{:S(2)}) collective-permute-start(bf16[24,3072]{1,0:T(8,128)(2,1)S(1)} %get-tuple-element.202), channel_id=1, source_target_pairs={{0,3},{1,2},{2,1},{3,0},{4,7},{5,6},{6,5},{7,4},{8,11},{9,10},{10,... | collective-permute-start | bytes 442376 | tf_op jit(solution)/shard_map/ppermute | solution.py:46
  111.8 15.5 %collective-permute-start.30 = (bf16[96,3072]{1,0:T(8,128)(2,1)S(1)}, bf16[96,3072]{1,0:T(8,128)(2,1)S(1)}, u32[]{:S(2)}, u32[]{:S(2)}) collective-permute-start(bf16[96,3072]{1,0:T(8,128)(2,1)S(1)} %get-tuple-element.164.refs_0_), channel_id=1, source_target_pairs={{0,16},{8,24},{16,0},{24,8},{1,17},{9,25},{17,1},{25,9},{2,18},{10... | collective-permute-start | bytes 1769480 | tf_op jit(solution)/shard_map/ppermute | solution.py:41
  116.6 10.6 %collective-permute-start.32 = (bf16[96,3072]{1,0:T(8,128)(2,1)S(1)}, bf16[96,3072]{1,0:T(8,128)(2,1)S(1)}, u32[]{:S(2)}, u32[]{:S(2)}) collective-permute-start(bf16[96,3072]{1,0:T(8,128)(2,1)S(1)} %get-tuple-element.164.refs_0_), channel_id=1, source_target_pairs={{0,8},{8,0},{16,24},{24,16},{1,9},{9,1},{17,25},{25,17},{2,10},{10... | collective-permute-start | bytes 1769480 | tf_op jit(solution)/shard_map/ppermute | solution.py:41
  (22 other events, 212.9 us)

commit v4 on v3

v4 whole, which is shorter than its diff:
```python
import functools

import jax
import jax.numpy as jnp
from jax import lax
from jax.experimental import pallas as pl
from jax.experimental.pallas import tpu as pltpu
from jax.sharding import PartitionSpec as P

error_scale = 0.03125
absent_mark = 1024.0
GROUPS = 2
f32 = jnp.float32
bf16 = jnp.bfloat16
VMEM_LIMIT = 36 * 1024 * 1024
WEIGH = 10


def dot(a, b, on_a, on_b):
    return lax.dot_general(a, b, (((on_a,), (on_b,)), ((), ())), preferred_element_type=f32)


def call(kernel, name, out_shape, grid, in_specs, out_specs, scratch, flops, moved):
    return pl.pallas_call(
        kernel,
        name=name,
        out_shape=out_shape,
        grid=grid,
        in_specs=in_specs,
        out_specs=out_specs,
        scratch_shapes=scratch,
        cost_estimate=pl.CostEstimate(flops=WEIGH * flops, bytes_accessed=WEIGH * moved, transcendentals=0),
        compiler_params=pltpu.CompilerParams(
            vmem_limit_bytes=VMEM_LIMIT, dimension_semantics=("arbitrary",) * len(grid) or None
        ),
    )


def swap(v, distance):
    n = lax.axis_size("dp")
    return lax.ppermute(v, "dp", [(i, i ^ distance) for i in range(n)])


def pass_on(v, distance):
    n = lax.axis_size("expert")
    return lax.ppermute(v, "expert", [(i, i ^ distance) for i in range(n)])


def after(v, *first):
    return lax.optimization_barrier((v,) + first)[0]


def gate(values, *first):
    return list(lax.optimization_barrier(tuple(values) + first)[: len(values)])


def slot_row(route_row, capacity, pairs):
    tokens = route_row.shape[1]
    distance = route_row ^ lax.axis_index("expert")
    one_hot = (lax.broadcasted_iota(jnp.int32, (2 * pairs, tokens), 0) == distance).astype(f32)
    earlier = (
        lax.broadcasted_iota(jnp.int32, (tokens, tokens), 0)
        < lax.broadcasted_iota(jnp.int32, (tokens, tokens), 1)
    ).astype(bf16)
    before = dot(one_hot.astype(bf16), earlier, 1, 0)
    rank = jnp.sum(before * one_hot, axis=0, keepdims=True).astype(jnp.int32)
    return ((distance & 1) * pairs + (pairs - (distance >> 1)) % pairs) * capacity + rank


def store_parts(rows, outs):
    start = 0
    for out in outs:
        out[...] = rows[start : start + out.shape[0]].astype(bf16)
        start += out.shape[0]


def place_kernel(capacity, pairs, routes_ref, tokens_ref, by_slot_ref, *outs):
    slots, tokens = by_slot_ref.shape
    slot = slot_row(routes_ref[...], capacity, pairs)
    by_slot = (lax.broadcasted_iota(jnp.int32, (slots, tokens), 0) == slot).astype(f32).astype(bf16)
    by_slot_ref[...] = by_slot
    store_parts(dot(by_slot, tokens_ref[...], 1, 0), outs)


def place_target_kernel(by_slot_ref, target_ref, *outs):
    by_slot = by_slot_ref[...]
    mark = (1.0 - jnp.sum(by_slot.astype(f32), axis=1, keepdims=True)) * absent_mark
    store_parts(dot(by_slot, target_ref[...], 1, 0) + mark, outs)


def place(name, kernel, first, values, sizes, with_slots):
    per_dev, features = values.shape
    slots = sum(sizes)
    wanted = sizes
    if any(size % 8 for size in sizes):
        sizes = [slots]
    steps = 2
    cols = lambda rows: pl.BlockSpec((rows, features // steps), lambda i: (0, i))
    whole = lambda *shape: pl.BlockSpec(shape, lambda i: (0, 0))
    outs = call(
        kernel,
        name,
        [jax.ShapeDtypeStruct((slots, per_dev), bf16)] * with_slots
        + [jax.ShapeDtypeStruct((size, features), bf16) for size in sizes],
        (steps,),
        [whole(*first.shape), cols(per_dev)],
        [whole(slots, per_dev)] * with_slots + [cols(size) for size in sizes],
        [],
        2 * slots * per_dev * features,
        2 * (per_dev + slots) * features,
    )(first, values)
    parts = list(outs[with_slots:])
    if len(parts) < len(wanted):
        starts = [sum(wanted[:j]) for j in range(len(wanted))]
        parts = [parts[0][start : start + size] for start, size in zip(starts, wanted)]
    return outs[0], parts


def clamp_parts(latent):
    squash = jax.nn.sigmoid(4.0 * latent)
    return (latent * squash).astype(bf16), squash + 4.0 * latent * squash * (1.0 - squash)


def forward_kernel(
    steps, mine, far, shift, shift_o, enc, enc_o, dec, dec_o, pre, pre_o, keep, out, act, act_o
):
    i = pl.program_id(0)
    size = mine.shape[0]

    @pl.when(i < steps)
    def _():
        x = jnp.concatenate([mine[...], far[...]], axis=0)
        part, part_o = dot(x, enc[...], 1, 0), dot(x, enc_o[...], 1, 0)

        @pl.when(i == 0)
        def _():
            pre[...] = part - shift[...]
            pre_o[...] = part_o - shift_o[...]

        @pl.when(i > 0)
        def _():
            pre[...] += part
            pre_o[...] += part_o

    @pl.when(i == steps - 1)
    def _():
        act[...] = clamp_parts(pre[...])[0]
        act_o[...] = clamp_parts(pre_o[...])[0]

    @pl.when(i >= steps)
    def _():
        part = dot(act[...], dec[...], 1, 1) + dot(act_o[...], dec_o[...], 1, 1)
        keep[...] = part[:size]
        out[...] = part[size:].astype(bf16)


def forward(mine, far, shifts, encs, decs):
    size, features = mine.shape
    latents = encs[0].shape[1]
    steps = 2
    wide = features // steps
    early = lambda i: jnp.minimum(i, steps - 1)
    late = lambda i: jnp.maximum(i - steps, 0)
    col_in = lambda rows: pl.BlockSpec((rows, wide), lambda i: (0, early(i)))
    fixed = lambda *shape: pl.BlockSpec(shape, lambda i: (0, 0))
    col_out = pl.BlockSpec((size, wide), lambda i: (0, late(i)))
    enc_in = pl.BlockSpec((wide, latents), lambda i: (early(i), 0))
    dec_in = pl.BlockSpec((wide, latents), lambda i: (late(i), 0))
    return call(
        functools.partial(forward_kernel, steps),
        "forward",
        [
            jax.ShapeDtypeStruct((2 * size, latents), f32),
            jax.ShapeDtypeStruct((2 * size, latents), f32),
            jax.ShapeDtypeStruct((size, features), f32),
            jax.ShapeDtypeStruct((size, features), bf16),
        ],
        (2 * steps,),
        [col_in(size)] * 2 + [fixed(1, latents)] * 2 + [enc_in] * 2 + [dec_in] * 2,
        [fixed(2 * size, latents), fixed(2 * size, latents), col_out, col_out],
        [pltpu.VMEM((2 * size, latents), bf16)] * 2,
        2 * 2 * 4 * size * features * latents,
        8 * features * latents + 14 * size * features,
    )(mine, far, *shifts, *encs, *decs)


def make_error(keep, across, wanted):
    recon = (keep + across.astype(f32)).astype(bf16)
    goal = wanted.astype(f32)
    error = (recon.astype(f32) - goal) * error_scale
    return recon, jnp.where(goal < 0.5 * absent_mark, error, 0.0).astype(bf16)


def gradients_kernel(tiles, count, *refs):
    errors, rows = refs[:count], refs[count : 2 * count]
    half = count // 2
    acts, slopes = refs[2 * count : 2 * count + half], refs[2 * count + half : 3 * count]
    dec, *rest = refs[3 * count :]
    summed = len(rest) > 4
    before, rest = (rest[:2], rest[2:]) if summed else ((), rest)
    act = jnp.concatenate([a[...] for a in acts], axis=0)
    slope = jnp.concatenate([s[...] for s in slopes], axis=0)
    out_enc, out_dec, out_buf, out_sems = rest
    features = errors[0].shape[1]
    wide = features // tiles
    cuts = [slice(i * wide, (i + 1) * wide) for i in range(tiles)]
    stack = lambda refs, cut: jnp.concatenate([r[:, cut] for r in refs], axis=0)

    pending = {}

    def put(n, i, left, right, out, was):
        slot = (n * tiles + i) % 3
        if slot in pending:
            pending.pop(slot).wait()
        part = dot(left, right, 0, 0)
        if summed:
            part = part + was[0, cuts[i], :].astype(f32)
        out_buf[slot] = part.astype(bf16)
        pending[slot] = pltpu.make_async_copy(
            out_buf.at[slot], out.at[0, pl.ds(i * wide, wide), :], out_sems.at[slot]
        )
        pending[slot].start()

    total = None
    for i, cut in enumerate(cuts):
        left = stack(errors, cut)
        part = dot(left, dec[cut, :], 1, 0)
        total = part if total is None else total + part
        put(0, i, left, act, out_dec, before[1] if summed else None)
    pre = (total * slope).astype(bf16)
    for i, cut in enumerate(cuts):
        put(1, i, stack(rows, cut), pre, out_enc, before[0] if summed else None)
    for copy in pending.values():
        copy.wait()


def gradients(errors, rows, acts, slopes, dec, before):
    size, features = errors[0].shape
    latents = dec.shape[1]
    tiles = 3
    count = len(errors)
    summed = len(before) > 0
    return call(
        functools.partial(gradients_kernel, tiles, count),
        "gradients_sum" if summed else "gradients",
        [jax.ShapeDtypeStruct((1, features, latents), bf16)] * 2,
        (),
        [pl.BlockSpec(memory_space=pltpu.VMEM)] * (3 * count + 1 + len(before)),
        [pl.BlockSpec(memory_space=pl.ANY)] * 2,
        [
            pltpu.VMEM((3, features // tiles, latents), bf16),
            pltpu.SemaphoreType.DMA((3,)),
        ],
        2 * 3 * count * size * features * latents,
        6 * features * latents + 4 * count * size * features,
    )(*errors, *rows, *acts, *slopes, dec, *before)


def collect_kernel(by_slot, direct, via, out):
    out[...] = dot(by_slot[...], jnp.concatenate([direct[...], via[...]], axis=0), 0, 0).astype(bf16)


def collect(by_slot, direct, via):
    slots, tokens = by_slot.shape
    features = direct.shape[1]
    steps = 2
    cols = lambda rows: pl.BlockSpec((rows, features // steps), lambda i: (0, i))
    return call(
        collect_kernel,
        "collect",
        jax.ShapeDtypeStruct((tokens, features), bf16),
        (steps,),
        [pl.BlockSpec((slots, tokens), lambda i: (0, 0)), cols(slots // 2), cols(slots // 2)],
        cols(tokens),
        [],
        2 * slots * tokens * features,
        2 * (slots + tokens) * features,
    )(by_slot, direct, via)


def local(tokens, target, routes, thresholds, enc_weight, dec_weight):
    experts = lax.axis_size("expert")
    half = lax.axis_size("dp") // 2
    per_dev, features = tokens.shape
    capacity = 3 * per_dev // (2 * experts)
    enc = enc_weight[0]
    dec = dec_weight[0]
    pairs = experts // 2
    sizes = [capacity] * pairs + [pairs * capacity]
    by_slot, parts = place(
        "place",
        functools.partial(place_kernel, capacity, pairs),
        routes.reshape(1, per_dev),
        tokens,
        sizes,
        True,
    )
    direct, via = parts[:pairs], parts[pairs]
    _, parts = place(
        "place_target",
        place_target_kernel,
        by_slot,
        target,
        sizes,
        False,
    )
    goal_direct, goal_via = parts[:pairs], parts[pairs]

    def outer(v, k, step=0):
        distance = 2 * ((pairs - k) % pairs) + step
        return pass_on(v, distance) if distance else v

    def spread(parts):
        return [outer(v, k) for k, v in enumerate(parts)]

    def cut(v):
        return [v[capacity * k : capacity * (k + 1)] for k in range(pairs)]

    def join(arrays):
        return jnp.concatenate(arrays, axis=0)

    shift = 0.25 * thresholds.astype(f32)
    shift_o = swap(shift, 1)

    def gradient_sides(pre, got):
        size = pre.shape[0] // 2
        sides = [clamp_parts(jnp.concatenate([pre[c], got[c]], axis=0)) for c in (slice(size), slice(size, None))]
        return [v for side in sides for v in side]

    out_direct = spread(direct)
    out_via = pass_on(via, 1)
    enc_o = swap(enc, 1)
    *out_direct, out_via, goal_via, shift_o, enc_o = gate(out_direct + [out_via, goal_via, shift_o, enc_o])
    mine0 = join(out_direct)
    out_via = spread(cut(out_via))
    far0 = swap(mine0, half)
    dec_o = swap(after(dec, enc_o), 1)
    *out_via, mine0, far0, goal_via, dec_o = gate(out_via + [mine0, far0, goal_via, dec_o])
    shifts, encs, decs = (shift, shift_o), (enc, enc_o), (dec, dec_o)
    mine1 = join(out_via)
    far1, cmine0 = swap(mine1, half), swap(mine0, 1)
    goal_direct = spread(gate(goal_direct, dec_o, cmine0))
    goal_via = pass_on(goal_via, 1)
    pre0, pre_o0, keep0, sum0 = forward(after(mine0, cmine0), far0, shifts, encs, decs)
    *goal_direct, mine1, far1, far0, keep0, sum0, goal_via, pre_o0 = gate(
        goal_direct + [mine1, far1, far0, keep0, sum0, goal_via, pre_o0]
    )
    across0 = swap(sum0, half)
    got0, cfar0 = swap(pre_o0, 1), swap(far0, 1)
    goal_via = spread(cut(after(goal_via, got0, cfar0)))
    pre1, pre_o1, keep1, sum1 = forward(after(mine1, got0, cfar0), far1, shifts, encs, decs)
    *goal_via, across0, sum1, got0, pre_o1 = gate(goal_via + [across0, sum1, got0, pre_o1])
    across1 = swap(sum1, half)
    recon0, error0 = make_error(keep0, across0, join(goal_direct))
    home0 = spread(cut(recon0))
    got1 = swap(pre_o1, 1)
    sides0 = gradient_sides(pre0, got0)
    *home0, across1, error0, got1, sides0[0] = gate(home0 + [across1, error0, got1, sides0[0]])
    efar0, enear0 = swap(error0, half), swap(error0, 1)
    recon1, error1 = make_error(keep1, across1, join(goal_via))
    home_via = cut(after(recon1, enear0))
    home1 = [outer(home_via[k], k, 1) for k in range(1, pairs)]
    sides1 = gradient_sides(pre1, got1)
    *home1, home_via, error0, efar0, error1, sides1[0], mine1, far1 = gate(
        home1 + [home_via[0], error0, efar0, error1, sides1[0], mine1, far1]
    )
    efar1 = swap(error1, half)
    ecross0, enear1, cmine1 = swap(efar0, 1), swap(error1, 1), swap(mine1, 1)
    home_via, far1 = gate([home_via, far1], ecross0, enear1, cmine1)
    home1 = [pass_on(home_via, 1)] + home1
    cfar1 = swap(far1, 1)
    before = gradients(
        [error0, enear0, efar0, ecross0, error1, enear1],
        [mine0, cmine0, far0, cfar0, mine1, cmine1],
        [sides0[0], sides0[2], sides1[0]],
        [sides0[1], sides0[3], sides1[1]],
        dec,
        (),
    )
    efar1, cfar1, *before = gate([efar1, cfar1, *before])
    ecross1 = swap(efar1, 1)
    homes = gate([join(home0), join(home1)], efar1)
    recon = collect(by_slot, *homes)
    grad_enc, grad_dec = gradients(
        [efar1, ecross1], [far1, cfar1], [sides1[2]], [sides1[3]], dec, before
    )
    return recon, grad_enc, grad_dec


def solution(mesh):
    in_specs = (
        P(("dp", "expert"), None),
        P(("dp", "expert"), None),
        P(("dp", "expert"), None),
        P("expert", "dp"),
        P("expert", None, "dp"),
        P("expert", None, "dp"),
    )
    out_specs = (P(("dp", "expert"), None), P("expert", None, "dp"), P("expert", None, "dp"))
    return jax.shard_map(local, mesh=mesh, in_specs=in_specs, out_specs=out_specs, check_vma=False)
```

time: 138 us -> 131 us (0.949)
  waiting for transfers between devices: 62.9 us -> 56.2 us
  Pallas kernels: 29.4 us -> 25.5 us
  local copies, waits for them, and re-layouts: 2.18 us -> 4.06 us
    ppermute x21, waiting for transfers between devices: 55.5 us -> 35.2 us  [pass_on(): return lax.ppermute(v, 'expert', [(i, i ^ distance) for i in range(n)])]
    ppermute x17 -> x19, waiting for transfers between devices: 7.44 us -> 21 us  [swap(): return lax.ppermute(v, 'dp', [(i, i ^ distance) for i in range(n)])]
    pallas_call x2, Pallas kernels: 16.6 us -> 13.1 us  [gradients(): call(functools.partial(gradients_kernel, tiles, count), 'gradients_sum' i...]
    unnamed x24 -> x22, local copies, waits for them, and re-layouts: 1.94 us -> 3.77 us
    ppermute x17 -> x19, starting transfers between devices: 8.82 us -> 9.71 us  [swap(): return lax.ppermute(v, 'dp', [(i, i ^ distance) for i in range(n)])]
  transfers between devices with their start and end apart: 38 -> 40, of which waited for: 16 -> 20; matrix products, arithmetic and copies ran while one was open for 1% -> 1% of each run, Pallas kernels for 15% -> 16%
where the time goes in v4:
time: 131 us; the launch traced here: 130 us
  waiting for transfers between devices  56.2 us (43%)
  starting transfers between devices  42.1 us (32%)
  Pallas kernels  25.5 us (19%)
  local copies, waits for them, and re-layouts  4.06 us (3%)
  other arithmetic  1.41 us (1%)
    ppermute x21, waiting for transfers between devices, pass_on(): return lax.ppermute(v, 'expert', [(i, i ^ distance) for i in range(n)])  35.2 us
    ppermute x21, starting transfers between devices, pass_on(): return lax.ppermute(v, 'expert', [(i, i ^ distance) for i in range(n)])  32.4 us
    ppermute x19, waiting for transfers between devices, swap(): return lax.ppermute(v, 'dp', [(i, i ^ distance) for i in range(n)])  21 us
    pallas_call x2, Pallas kernels, gradients(): call(functools.partial(gradients_kernel, tiles, count), 'gradients_sum' i...  13.1 us
    ppermute x19, starting transfers between devices, swap(): return lax.ppermute(v, 'dp', [(i, i ^ distance) for i in range(n)])  9.71 us
    pallas_call x2, Pallas kernels, forward(): call(functools.partial(forward_kernel, steps), 'forward', [jax.ShapeDtype...  9.17 us
    unnamed x22, local copies, waits for them, and re-layouts  3.77 us
  transfers between devices with their start and end apart: 40, of which 20 were waited for; matrix products, arithmetic and copies ran while one was open for 1% of the time, Pallas kernels for 16%

profile of v4, /device:TPU:0, one launch (start us, length us, event | category | flops | bytes accessed | tf_op | source)
XLA Modules:
  0.0 130.4 jit_solution(546790333941450403)
XLA Ops:
  4.0 2.6 %collective-permute-start.3 = (bf16[96,3072]{1,0:T(8,128)(2,1)S(1)}, bf16[96,3072]{1,0:T(8,128)(2,1)S(1)}, u32[]{:S(2)}, u32[]{:S(2)}) collective-permute-start(bf16[96,3072]{1,0:T(8,128)(2,1)S(1)} %get-tuple-element.105), channel_id=1, source_target_pairs={{0,1},{1,0},{2,3},{3,2},{4,5},{5,4},{6,7},{7,6},{8,9},{9,8},{10,11... | collective-permute-start | bytes 1769480 | tf_op jit(solution)/shard_map/ppermute | solution.py:46
  6.8 3.6 %collective-permute-start = (bf16[24,3072]{1,0:T(8,128)(2,1)S(1)}, bf16[24,3072]{1,0:T(8,128)(2,1)S(1)}, u32[]{:S(2)}, u32[]{:S(2)}) collective-permute-start(bf16[24,3072]{1,0:T(8,128)(2,1)S(1)} %get-tuple-element.102), channel_id=1, source_target_pairs={{0,6},{1,7},{2,4},{3,5},{4,2},{5,3},{6,0},{7,1},{8,14},{9,15},{10,... | collective-permute-start | bytes 442376 | tf_op jit(solution)/shard_map/ppermute | solution.py:46
  12.0 3.4 %collective-permute-done = bf16[24,3072]{1,0:T(8,128)(2,1)S(1)} collective-permute-done((bf16[24,3072]{1,0:T(8,128)(2,1)S(1)}, bf16[24,3072]{1,0:T(8,128)(2,1)S(1)}, u32[]{:S(2)}, u32[]{:S(2)}) %collective-permute-start) | collective-permute-done | bytes 147488 | tf_op jit(solution)/shard_map/ppermute | solution.py:46
  15.4 8.0 %collective-permute-done.1 = bf16[24,3072]{1,0:T(8,128)(2,1)S(1)} collective-permute-done((bf16[24,3072]{1,0:T(8,128)(2,1)S(1)}, bf16[24,3072]{1,0:T(8,128)(2,1)S(1)}, u32[]{:S(2)}, u32[]{:S(2)}) %collective-permute-start.1) | collective-permute-done | bytes 147488 | tf_op jit(solution)/shard_map/ppermute | solution.py:46
  25.2 2.5 %collective-permute-start.6 = (bf16[24,3072]{1,0:T(8,128)(2,1)S(1)}, bf16[24,3072]{1,0:T(8,128)(2,1)S(1)}, u32[]{:S(2)}, u32[]{:S(2)}) collective-permute-start(bf16[24,3072]{1,0:T(8,128)(2,1)S(1)} %get-tuple-element.207), channel_id=1, source_target_pairs={{0,6},{1,7},{2,4},{3,5},{4,2},{5,3},{6,0},{7,1},{8,14},{9,15},{10,... | collective-permute-start | bytes 442376 | tf_op jit(solution)/shard_map/ppermute | solution.py:46
  29.6 4.2 %collective-permute-done.6 = bf16[24,3072]{1,0:T(8,128)(2,1)S(1)} collective-permute-done((bf16[24,3072]{1,0:T(8,128)(2,1)S(1)}, bf16[24,3072]{1,0:T(8,128)(2,1)S(1)}, u32[]{:S(2)}, u32[]{:S(2)}) %collective-permute-start.6) | collective-permute-done | bytes 147488 | tf_op jit(solution)/shard_map/ppermute | solution.py:46
  33.9 5.9 %collective-permute-done.7 = bf16[24,3072]{1,0:T(8,128)(2,1)S(1)} collective-permute-done((bf16[24,3072]{1,0:T(8,128)(2,1)S(1)}, bf16[24,3072]{1,0:T(8,128)(2,1)S(1)}, u32[]{:S(2)}, u32[]{:S(2)}) %collective-permute-start.7) | collective-permute-done | bytes 147488 | tf_op jit(solution)/shard_map/ppermute | solution.py:46
  41.9 2.1 %collective-permute-start.12 = (bf16[24,3072]{1,0:T(8,128)(2,1)S(1)}, bf16[24,3072]{1,0:T(8,128)(2,1)S(1)}, u32[]{:S(2)}, u32[]{:S(2)}) collective-permute-start(bf16[24,3072]{1,0:T(8,128)(2,1)S(1)} %get-tuple-element.118), channel_id=1, source_target_pairs={{0,6},{1,7},{2,4},{3,5},{4,2},{5,3},{6,0},{7,1},{8,14},{9,15},{10,... | collective-permute-start | bytes 442376 | tf_op jit(solution)/shard_map/ppermute | solution.py:46
  44.0 2.3 %collective-permute-start.14 = (bf16[24,3072]{1,0:T(8,128)(2,1)S(1)}, bf16[24,3072]{1,0:T(8,128)(2,1)S(1)}, u32[]{:S(2)}, u32[]{:S(2)}) collective-permute-start(bf16[24,3072]{1,0:T(8,128)(2,1)S(1)} %get-tuple-element.120), channel_id=1, source_target_pairs={{0,2},{1,3},{2,0},{3,1},{4,6},{5,7},{6,4},{7,5},{8,10},{9,11},{10,... | collective-permute-start | bytes 442376 | tf_op jit(solution)/shard_map/ppermute | solution.py:46
  46.2 4.6 %forward.2 = (f32[192,512]{1,0:T(8,128)S(1)}, f32[192,512]{1,0:T(8,128)S(1)}, f32[96,3072]{1,0:T(8,128)S(1)}, bf16[96,3072]{1,0:T(8,128)(2,1)S(1)}) custom-call(bf16[96,3072]{1,0:T(8,128)(2,1)S(1)} %constant_dynamic-update-slice_fusion.mine.refs_6_, bf16[96,3072]{1,0:T(8,128)(2,1)S(1)} %collective-permute-done.9.far.refs_8_, ...), custom_call_target="tpu_custom_call" | custom-call | flops 24159191040 | bytes 167116800 | tf_op jit(solution)/shard_map/forward/pallas_call | solution.py:169
  50.8 4.9 %collective-permute-done.15.far.refs_2_ = bf16[96,3072]{1,0:T(8,128)(2,1)S(1)} collective-permute-done((bf16[96,3072]{1,0:T(8,128)(2,1)S(1)}, bf16[96,3072]{1,0:T(8,128)(2,1)S(1)}, u32[]{:S(2)}, u32[]{:S(2)}) %collective-permute-start.15) | collective-permute-done | bytes 589856 | tf_op jit(solution)/shard_map/ppermute | solution.py:41
  59.5 2.2 %collective-permute-start.19 = (bf16[24,3072]{1,0:T(8,128)(2,1)S(1)}, bf16[24,3072]{1,0:T(8,128)(2,1)S(1)}, u32[]{:S(2)}, u32[]{:S(2)}) collective-permute-start(bf16[24,3072]{1,0:T(8,128)(2,1)S(1)} %get-tuple-element.203), channel_id=1, source_target_pairs={{0,6},{1,7},{2,4},{3,5},{4,2},{5,3},{6,0},{7,1},{8,14},{9,15},{10,... | collective-permute-start | bytes 442376 | tf_op jit(solution)/shard_map/ppermute | solution.py:46
  61.7 2.3 %collective-permute-start.21 = (bf16[24,3072]{1,0:T(8,128)(2,1)S(1)}, bf16[24,3072]{1,0:T(8,128)(2,1)S(1)}, u32[]{:S(2)}, u32[]{:S(2)}) collective-permute-start(bf16[24,3072]{1,0:T(8,128)(2,1)S(1)} %get-tuple-element.201), channel_id=1, source_target_pairs={{0,2},{1,3},{2,0},{3,1},{4,6},{5,7},{6,4},{7,5},{8,10},{9,11},{10,... | collective-permute-start | bytes 442376 | tf_op jit(solution)/shard_map/ppermute | solution.py:46
  65.9 4.6 %forward.3 = (f32[192,512]{1,0:T(8,128)S(1)}, f32[192,512]{1,0:T(8,128)S(1)}, f32[96,3072]{1,0:T(8,128)S(1)}, bf16[96,3072]{1,0:T(8,128)(2,1)S(1)}) custom-call(bf16[96,3072]{1,0:T(8,128)(2,1)S(1)} %constant_dynamic-update-slice_fusion.4.mine.refs_10_, bf16[96,3072]{1,0:T(8,128)(2,1)S(1)} %collective-permute-done.15.far.refs_2_, ...), custom_call_target="tpu_custom_call" | custom-call | flops 24159191040 | bytes 167116800 | tf_op jit(solution)/shard_map/forward/pallas_call | solution.py:169
  70.5 2.3 %collective-permute-done.22 = bf16[96,3072]{1,0:T(8,128)(2,1)S(1)} collective-permute-done((bf16[96,3072]{1,0:T(8,128)(2,1)S(1)}, bf16[96,3072]{1,0:T(8,128)(2,1)S(1)}, u32[]{:S(2)}, u32[]{:S(2)}) %collective-permute-start.22) | collective-permute-done | bytes 589856 | tf_op jit(solution)/shard_map/ppermute | solution.py:41
  77.1 3.0 %collective-permute-start.25 = (bf16[24,3072]{1,0:T(8,128)(2,1)S(1)}, bf16[24,3072]{1,0:T(8,128)(2,1)S(1)}, u32[]{:S(2)}, u32[]{:S(2)}) collective-permute-start(bf16[24,3072]{1,0:T(8,128)(2,1)S(1)} %get-tuple-element.197), channel_id=1, source_target_pairs={{0,2},{1,3},{2,0},{3,1},{4,6},{5,7},{6,4},{7,5},{8,10},{9,11},{10,... | collective-permute-start | bytes 442376 | tf_op jit(solution)/shard_map/ppermute | solution.py:46
  80.3 4.0 %collective-permute-done.23 = bf16[24,3072]{1,0:T(8,128)(2,1)S(1)} collective-permute-done((bf16[24,3072]{1,0:T(8,128)(2,1)S(1)}, bf16[24,3072]{1,0:T(8,128)(2,1)S(1)}, u32[]{:S(2)}, u32[]{:S(2)}) %collective-permute-start.23) | collective-permute-done | bytes 147488 | tf_op jit(solution)/shard_map/ppermute | solution.py:46
  84.3 5.9 %collective-permute-done.24 = bf16[24,3072]{1,0:T(8,128)(2,1)S(1)} collective-permute-done((bf16[24,3072]{1,0:T(8,128)(2,1)S(1)}, bf16[24,3072]{1,0:T(8,128)(2,1)S(1)}, u32[]{:S(2)}, u32[]{:S(2)}) %collective-permute-start.24) | collective-permute-done | bytes 147488 | tf_op jit(solution)/shard_map/ppermute | solution.py:46
  92.3 2.6 %collective-permute-start.29 = (bf16[24,3072]{1,0:T(8,128)(2,1)S(1)}, bf16[24,3072]{1,0:T(8,128)(2,1)S(1)}, u32[]{:S(2)}, u32[]{:S(2)}) collective-permute-start(bf16[24,3072]{1,0:T(8,128)(2,1)S(1)} %get-tuple-element.196), channel_id=1, source_target_pairs={{0,7},{1,6},{2,5},{3,4},{4,3},{5,2},{6,1},{7,0},{8,15},{9,14},{10,... | collective-permute-start | bytes 442376 | tf_op jit(solution)/shard_map/ppermute | solution.py:46
  95.0 3.4 %collective-permute-start.31 = (bf16[24,3072]{1,0:T(8,128)(2,1)S(1)}, bf16[24,3072]{1,0:T(8,128)(2,1)S(1)}, u32[]{:S(2)}, u32[]{:S(2)}) collective-permute-start(bf16[24,3072]{1,0:T(8,128)(2,1)S(1)} %get-tuple-element.194), channel_id=1, source_target_pairs={{0,3},{1,2},{2,1},{3,0},{4,7},{5,6},{6,5},{7,4},{8,11},{9,10},{10,... | collective-permute-start | bytes 442376 | tf_op jit(solution)/shard_map/ppermute | solution.py:46
  98.6 7.4 %collective-permute-done.32.refs_2_ = bf16[96,3072]{1,0:T(8,128)(2,1)S(1)} collective-permute-done((bf16[96,3072]{1,0:T(8,128)(2,1)S(1)}, bf16[96,3072]{1,0:T(8,128)(2,1)S(1)}, u32[]{:S(2)}, u32[]{:S(2)}) %collective-permute-start.32) | collective-permute-done | bytes 589856 | tf_op jit(solution)/shard_map/ppermute | solution.py:41
  112.5 9.0 %gradients.1 = (bf16[1,3072,512]{2,1,0:T(8,128)(2,1)S(1)}, bf16[1,3072,512]{2,1,0:T(8,128)(2,1)S(1)}) custom-call(bf16[96,3072]{1,0:T(8,128)(2,1)S(1)} %get-tuple-element.176.refs_0_, bf16[96,3072]{1,0:T(8,128)(2,1)S(1)} %collective-permute-done.28.refs_1_, bf16[96,3072]{1,0:T(8,128)(2,1)S(1)} %collective-permute-done.32.refs_2_, ...), custom_call_target="tpu_custom_call" | custom-call | flops 54358179840 | bytes 165150720 | tf_op jit(solution)/shard_map/gradients/pallas_call | solution.py:243
  121.5 2.6 %collective-permute-done.37.refs_0_ = bf16[96,3072]{1,0:T(8,128)(2,1)S(1)} collective-permute-done((bf16[96,3072]{1,0:T(8,128)(2,1)S(1)}, bf16[96,3072]{1,0:T(8,128)(2,1)S(1)}, u32[]{:S(2)}, u32[]{:S(2)}) %collective-permute-start.37) | collective-permute-done | bytes 589856 | tf_op jit(solution)/shard_map/ppermute | solution.py:41
  126.1 4.1 %gradients_sum.1 = (bf16[1,3072,512]{2,1,0:T(8,128)(2,1)}, bf16[1,3072,512]{2,1,0:T(8,128)(2,1)}) custom-call(bf16[96,3072]{1,0:T(8,128)(2,1)S(1)} %collective-permute-done.37.refs_0_, bf16[96,3072]{1,0:T(8,128)(2,1)S(1)} %collective-permute-done.39.refs_1_, bf16[96,3072]{1,0:T(8,128)(2,1)S(1)} %collective-permute-done.15.far.refs_2_, ...), custom_call_target="tpu_custom_call" | custom-call | flops 18119393280 | bytes 117964800 | tf_op jit(solution)/shard_map/gradients_sum/pallas_call | solution.py:243
  (104 shorter events, 31.8 us)
Async XLA Ops:
  0.6 22.7 %collective-permute-start.5 = (bf16[3072,512]{1,0:T(8,128)(2,1)}, bf16[3072,512]{1,0:T(8,128)(2,1)S(1)}, u32[]{:S(2)}, u32[]{:S(2)}) collective-permute-start(bf16[3072,512]{1,0:T(8,128)(2,1)} %bitcast.3), channel_id=1, source_target_pairs={{0,8},{8,0},{16,24},{24,16},{1,9},{9,1},{17,25},{25,17},{2,10},{10... | collective-permute-start | bytes 9437192 | tf_op jit(solution)/shard_map/ppermute | solution.py:41
  4.0 19.4 %collective-permute-start.3 = (bf16[96,3072]{1,0:T(8,128)(2,1)S(1)}, bf16[96,3072]{1,0:T(8,128)(2,1)S(1)}, u32[]{:S(2)}, u32[]{:S(2)}) collective-permute-start(bf16[96,3072]{1,0:T(8,128)(2,1)S(1)} %get-tuple-element.105), channel_id=1, source_target_pairs={{0,1},{1,0},{2,3},{3,2},{4,5},{5,4},{6,7},{7,6},{8,9},{9,8},{10,11... | collective-permute-start | bytes 1769480 | tf_op jit(solution)/shard_map/ppermute | solution.py:46
  10.4 12.9 %collective-permute-start.1 = (bf16[24,3072]{1,0:T(8,128)(2,1)S(1)}, bf16[24,3072]{1,0:T(8,128)(2,1)S(1)}, u32[]{:S(2)}, u32[]{:S(2)}) collective-permute-start(bf16[24,3072]{1,0:T(8,128)(2,1)S(1)} %get-tuple-element.103), channel_id=1, source_target_pairs={{0,4},{1,5},{2,6},{3,7},{4,0},{5,1},{6,2},{7,3},{8,12},{9,13},{10,... | collective-permute-start | bytes 442376 | tf_op jit(solution)/shard_map/ppermute | solution.py:46
  10.4 12.9 %collective-permute-start.2 = (bf16[24,3072]{1,0:T(8,128)(2,1)S(1)}, bf16[24,3072]{1,0:T(8,128)(2,1)S(1)}, u32[]{:S(2)}, u32[]{:S(2)}) collective-permute-start(bf16[24,3072]{1,0:T(8,128)(2,1)S(1)} %get-tuple-element.104), channel_id=1, source_target_pairs={{0,2},{1,3},{2,0},{3,1},{4,6},{5,7},{6,4},{7,5},{8,10},{9,11},{10,... | collective-permute-start | bytes 442376 | tf_op jit(solution)/shard_map/ppermute | solution.py:46
  23.4 16.4 %collective-permute-start.10 = (bf16[3072,512]{1,0:T(8,128)(2,1)S(1)}, bf16[3072,512]{1,0:T(8,128)(2,1)S(1)}, u32[]{:S(2)}, u32[]{:S(2)}) collective-permute-start(bf16[3072,512]{1,0:T(8,128)(2,1)S(1)} %bitcast.6), channel_id=1, source_target_pairs={{0,8},{8,0},{16,24},{24,16},{1,9},{9,1},{17,25},{25,17},{2,10},{10... | collective-permute-start | bytes 9437192 | tf_op jit(solution)/shard_map/ppermute | solution.py:41
  23.6 16.2 %collective-permute-start.9 = (bf16[96,3072]{1,0:T(8,128)(2,1)S(1)}, bf16[96,3072]{1,0:T(8,128)(2,1)S(1)}, u32[]{:S(2)}, u32[]{:S(2)}) collective-permute-start(bf16[96,3072]{1,0:T(8,128)(2,1)S(1)} %constant_dynamic-update-slice_fusion.mine.refs_6_), channel_id=1, source_target_pairs={{0,16},{8,24},{16,0},{24,8},{1,17},{9,25},{17,1},{25,9},{2,18},{10... | collective-permute-start | bytes 1769480 | tf_op jit(solution)/shard_map/ppermute | solution.py:41
  39.9 15.8 %collective-permute-start.15 = (bf16[96,3072]{1,0:T(8,128)(2,1)S(1)}, bf16[96,3072]{1,0:T(8,128)(2,1)S(1)}, u32[]{:S(2)}, u32[]{:S(2)}) collective-permute-start(bf16[96,3072]{1,0:T(8,128)(2,1)S(1)} %constant_dynamic-update-slice_fusion.4.mine.refs_10_), channel_id=1, source_target_pairs={{0,16},{8,24},{16,0},{24,8},{1,17},{9,25},{17,1},{25,9},{2,18},{10... | collective-permute-start | bytes 1769480 | tf_op jit(solution)/shard_map/ppermute | solution.py:41
  41.0 15.5 %collective-permute-start.16 = (bf16[96,3072]{1,0:T(8,128)(2,1)S(1)}, bf16[96,3072]{1,0:T(8,128)(2,1)S(1)}, u32[]{:S(2)}, u32[]{:S(2)}) collective-permute-start(bf16[96,3072]{1,0:T(8,128)(2,1)S(1)} %get-tuple-element.130), channel_id=1, source_target_pairs={{0,1},{1,0},{2,3},{3,2},{4,5},{5,4},{6,7},{7,6},{8,9},{9,8},{10,11... | collective-permute-start | bytes 1769480 | tf_op jit(solution)/shard_map/ppermute | solution.py:46
  41.9 14.6 %collective-permute-start.12 = (bf16[24,3072]{1,0:T(8,128)(2,1)S(1)}, bf16[24,3072]{1,0:T(8,128)(2,1)S(1)}, u32[]{:S(2)}, u32[]{:S(2)}) collective-permute-start(bf16[24,3072]{1,0:T(8,128)(2,1)S(1)} %get-tuple-element.118), channel_id=1, source_target_pairs={{0,6},{1,7},{2,4},{3,5},{4,2},{5,3},{6,0},{7,1},{8,14},{9,15},{10,... | collective-permute-start | bytes 442376 | tf_op jit(solution)/shard_map/ppermute | solution.py:46
  44.0 12.9 %collective-permute-start.13 = (bf16[24,3072]{1,0:T(8,128)(2,1)S(1)}, bf16[24,3072]{1,0:T(8,128)(2,1)S(1)}, u32[]{:S(2)}, u32[]{:S(2)}) collective-permute-start(bf16[24,3072]{1,0:T(8,128)(2,1)S(1)} %get-tuple-element.119), channel_id=1, source_target_pairs={{0,4},{1,5},{2,6},{3,7},{4,0},{5,1},{6,2},{7,3},{8,12},{9,13},{10,... | collective-permute-start | bytes 442376 | tf_op jit(solution)/shard_map/ppermute | solution.py:46
  44.0 12.9 %collective-permute-start.14 = (bf16[24,3072]{1,0:T(8,128)(2,1)S(1)}, bf16[24,3072]{1,0:T(8,128)(2,1)S(1)}, u32[]{:S(2)}, u32[]{:S(2)}) collective-permute-start(bf16[24,3072]{1,0:T(8,128)(2,1)S(1)} %get-tuple-element.120), channel_id=1, source_target_pairs={{0,2},{1,3},{2,0},{3,1},{4,6},{5,7},{6,4},{7,5},{8,10},{9,11},{10,... | collective-permute-start | bytes 442376 | tf_op jit(solution)/shard_map/ppermute | solution.py:46
  57.4 15.3 %collective-permute-start.22 = (bf16[96,3072]{1,0:T(8,128)(2,1)S(1)}, bf16[96,3072]{1,0:T(8,128)(2,1)S(1)}, u32[]{:S(2)}, u32[]{:S(2)}) collective-permute-start(bf16[96,3072]{1,0:T(8,128)(2,1)S(1)} %get-tuple-element.137), channel_id=1, source_target_pairs={{0,16},{8,24},{16,0},{24,8},{1,17},{9,25},{17,1},{25,9},{2,18},{10... | collective-permute-start | bytes 1769480 | tf_op jit(solution)/shard_map/ppermute | solution.py:41
  59.5 13.2 %collective-permute-start.19 = (bf16[24,3072]{1,0:T(8,128)(2,1)S(1)}, bf16[24,3072]{1,0:T(8,128)(2,1)S(1)}, u32[]{:S(2)}, u32[]{:S(2)}) collective-permute-start(bf16[24,3072]{1,0:T(8,128)(2,1)S(1)} %get-tuple-element.203), channel_id=1, source_target_pairs={{0,6},{1,7},{2,4},{3,5},{4,2},{5,3},{6,0},{7,1},{8,14},{9,15},{10,... | collective-permute-start | bytes 442376 | tf_op jit(solution)/shard_map/ppermute | solution.py:46
  73.8 16.4 %collective-permute-start.26 = (bf16[96,3072]{1,0:T(8,128)(2,1)S(1)}, bf16[96,3072]{1,0:T(8,128)(2,1)S(1)}, u32[]{:S(2)}, u32[]{:S(2)}) collective-permute-start(bf16[96,3072]{1,0:T(8,128)(2,1)S(1)} %get-tuple-element.144), channel_id=1, source_target_pairs={{0,16},{8,24},{16,0},{24,8},{1,17},{9,25},{17,1},{25,9},{2,18},{10... | collective-permute-start | bytes 1769480 | tf_op jit(solution)/shard_map/ppermute | solution.py:41
  75.3 14.9 %collective-permute-start.27 = (f32[192,512]{1,0:T(8,128)S(1)}, f32[192,512]{1,0:T(8,128)S(1)}, u32[]{:S(2)}, u32[]{:S(2)}) collective-permute-start(f32[192,512]{1,0:T(8,128)S(1)} %get-tuple-element.149), channel_id=1, source_target_pairs={{0,8},{8,0},{16,24},{24,16},{1,9},{9,1},{17,25},{25,17},{2,10},{10... | collective-permute-start | bytes 1179656 | tf_op jit(solution)/shard_map/ppermute | solution.py:41
  77.1 13.1 %collective-permute-start.24 = (bf16[24,3072]{1,0:T(8,128)(2,1)S(1)}, bf16[24,3072]{1,0:T(8,128)(2,1)S(1)}, u32[]{:S(2)}, u32[]{:S(2)}) collective-permute-start(bf16[24,3072]{1,0:T(8,128)(2,1)S(1)} %get-tuple-element.198), channel_id=1, source_target_pairs={{0,4},{1,5},{2,6},{3,7},{4,0},{5,1},{6,2},{7,3},{8,12},{9,13},{10,... | collective-permute-start | bytes 442376 | tf_op jit(solution)/shard_map/ppermute | solution.py:46
  77.1 13.1 %collective-permute-start.25 = (bf16[24,3072]{1,0:T(8,128)(2,1)S(1)}, bf16[24,3072]{1,0:T(8,128)(2,1)S(1)}, u32[]{:S(2)}, u32[]{:S(2)}) collective-permute-start(bf16[24,3072]{1,0:T(8,128)(2,1)S(1)} %get-tuple-element.197), channel_id=1, source_target_pairs={{0,2},{1,3},{2,0},{3,1},{4,6},{5,7},{6,4},{7,5},{8,10},{9,11},{10,... | collective-permute-start | bytes 442376 | tf_op jit(solution)/shard_map/ppermute | solution.py:46
  90.4 15.6 %collective-permute-start.32 = (bf16[96,3072]{1,0:T(8,128)(2,1)S(1)}, bf16[96,3072]{1,0:T(8,128)(2,1)S(1)}, u32[]{:S(2)}, u32[]{:S(2)}) collective-permute-start(bf16[96,3072]{1,0:T(8,128)(2,1)S(1)} %get-tuple-element.176.refs_0_), channel_id=1, source_target_pairs={{0,16},{8,24},{16,0},{24,8},{1,17},{9,25},{17,1},{25,9},{2,18},{10... | collective-permute-start | bytes 1769480 | tf_op jit(solution)/shard_map/ppermute | solution.py:41
  92.3 13.7 %collective-permute-start.29 = (bf16[24,3072]{1,0:T(8,128)(2,1)S(1)}, bf16[24,3072]{1,0:T(8,128)(2,1)S(1)}, u32[]{:S(2)}, u32[]{:S(2)}) collective-permute-start(bf16[24,3072]{1,0:T(8,128)(2,1)S(1)} %get-tuple-element.196), channel_id=1, source_target_pairs={{0,7},{1,6},{2,5},{3,4},{4,3},{5,2},{6,1},{7,0},{8,15},{9,14},{10,... | collective-permute-start | bytes 442376 | tf_op jit(solution)/shard_map/ppermute | solution.py:46
  95.0 12.6 %collective-permute-start.30 = (bf16[24,3072]{1,0:T(8,128)(2,1)S(1)}, bf16[24,3072]{1,0:T(8,128)(2,1)S(1)}, u32[]{:S(2)}, u32[]{:S(2)}) collective-permute-start(bf16[24,3072]{1,0:T(8,128)(2,1)S(1)} %get-tuple-element.195), channel_id=1, source_target_pairs={{0,5},{1,4},{2,7},{3,6},{4,1},{5,0},{6,3},{7,2},{8,13},{9,12},{10,... | collective-permute-start | bytes 442376 | tf_op jit(solution)/shard_map/ppermute | solution.py:46
  95.0 12.6 %collective-permute-start.31 = (bf16[24,3072]{1,0:T(8,128)(2,1)S(1)}, bf16[24,3072]{1,0:T(8,128)(2,1)S(1)}, u32[]{:S(2)}, u32[]{:S(2)}) collective-permute-start(bf16[24,3072]{1,0:T(8,128)(2,1)S(1)} %get-tuple-element.194), channel_id=1, source_target_pairs={{0,3},{1,2},{2,1},{3,0},{4,7},{5,6},{6,5},{7,4},{8,11},{9,10},{10,... | collective-permute-start | bytes 442376 | tf_op jit(solution)/shard_map/ppermute | solution.py:46
  108.3 15.8 %collective-permute-start.37 = (bf16[96,3072]{1,0:T(8,128)(2,1)S(1)}, bf16[96,3072]{1,0:T(8,128)(2,1)S(1)}, u32[]{:S(2)}, u32[]{:S(2)}) collective-permute-start(bf16[96,3072]{1,0:T(8,128)(2,1)S(1)} %get-tuple-element.169.refs_4_), channel_id=1, source_target_pairs={{0,16},{8,24},{16,0},{24,8},{1,17},{9,25},{17,1},{25,9},{2,18},{10... | collective-permute-start | bytes 1769480 | tf_op jit(solution)/shard_map/ppermute | solution.py:41
  111.3 12.9 %collective-permute-start.38 = (bf16[96,3072]{1,0:T(8,128)(2,1)S(1)}, bf16[96,3072]{1,0:T(8,128)(2,1)S(1)}, u32[]{:S(2)}, u32[]{:S(2)}) collective-permute-start(bf16[96,3072]{1,0:T(8,128)(2,1)S(1)} %collective-permute-done.15.far.refs_2_), channel_id=1, source_target_pairs={{0,8},{8,0},{16,24},{24,16},{1,9},{9,1},{17,25},{25,17},{2,10},{10... | collective-permute-start | bytes 1769480 | tf_op jit(solution)/shard_map/ppermute | solution.py:41
  111.4 12.9 %collective-permute-start.36 = (bf16[24,3072]{1,0:T(8,128)(2,1)S(1)}, bf16[24,3072]{1,0:T(8,128)(2,1)S(1)}, u32[]{:S(2)}, u32[]{:S(2)}) collective-permute-start(bf16[24,3072]{1,0:T(8,128)(2,1)S(1)} %get-tuple-element.171), channel_id=1, source_target_pairs={{0,1},{1,0},{2,3},{3,2},{4,5},{5,4},{6,7},{7,6},{8,9},{9,8},{10,11... | collective-permute-start | bytes 442376 | tf_op jit(solution)/shard_map/ppermute | solution.py:46
  (24 other events, 170.8 us)

commit v5 on v4

--- a/solution.py
+++ b/solution.py
@@ -338,18 +338,18 @@
     *out_via, mine0, far0, goal_via, dec_o = gate(out_via + [mine0, far0, goal_via, dec_o])
     shifts, encs, decs = (shift, shift_o), (enc, enc_o), (dec, dec_o)
     mine1 = join(out_via)
-    far1, cmine0 = swap(mine1, half), swap(mine0, 1)
-    goal_direct = spread(gate(goal_direct, dec_o, cmine0))
+    far1 = swap(mine1, half)
+    goal_direct = spread(gate(goal_direct, dec_o))
     goal_via = pass_on(goal_via, 1)
-    pre0, pre_o0, keep0, sum0 = forward(after(mine0, cmine0), far0, shifts, encs, decs)
+    pre0, pre_o0, keep0, sum0 = forward(mine0, far0, shifts, encs, decs)
     *goal_direct, mine1, far1, far0, keep0, sum0, goal_via, pre_o0 = gate(
         goal_direct + [mine1, far1, far0, keep0, sum0, goal_via, pre_o0]
     )
     across0 = swap(sum0, half)
-    got0, cfar0 = swap(pre_o0, 1), swap(far0, 1)
-    goal_via = spread(cut(after(goal_via, got0, cfar0)))
-    pre1, pre_o1, keep1, sum1 = forward(after(mine1, got0, cfar0), far1, shifts, encs, decs)
-    *goal_via, across0, sum1, got0, pre_o1 = gate(goal_via + [across0, sum1, got0, pre_o1])
+    got0 = swap(pre_o0, 1)
+    goal_via = spread(cut(after(goal_via, got0)))
+    pre1, pre_o1, keep1, sum1 = forward(after(mine1, got0), far1, shifts, encs, decs)
+    *goal_via, across0, sum1, got0, pre_o1, mine1 = gate(goal_via + [across0, sum1, got0, pre_o1, mine1])
     across1 = swap(sum1, half)
     recon0, error0 = make_error(keep0, across0, join(goal_direct))
     home0 = spread(cut(recon0))
@@ -357,16 +357,17 @@
     sides0 = gradient_sides(pre0, got0)
     *home0, across1, error0, got1, sides0[0] = gate(home0 + [across1, error0, got1, sides0[0]])
     efar0, enear0 = swap(error0, half), swap(error0, 1)
+    cfar0, cmine0 = swap(far0, 1), swap(mine0, 1)
     recon1, error1 = make_error(keep1, across1, join(goal_via))
-    home_via = cut(after(recon1, enear0))
+    home_via = cut(recon1)
     home1 = [outer(home_via[k], k, 1) for k in range(1, pairs)]
     sides1 = gradient_sides(pre1, got1)
-    *home1, home_via, error0, efar0, error1, sides1[0], mine1, far1 = gate(
-        home1 + [home_via[0], error0, efar0, error1, sides1[0], mine1, far1]
+    *home1, home_via, error0, efar0, cfar0, cmine0, error1, sides1[0], mine1, far1 = gate(
+        home1 + [home_via[0], error0, efar0, cfar0, cmine0, error1, sides1[0], mine1, far1]
     )
     efar1 = swap(error1, half)
     ecross0, enear1, cmine1 = swap(efar0, 1), swap(error1, 1), swap(mine1, 1)
-    home_via, far1 = gate([home_via, far1], ecross0, enear1, cmine1)
+    home_via, far1 = gate([home_via, far1], ecross0, enear1)
     home1 = [pass_on(home_via, 1)] + home1
     cfar1 = swap(far1, 1)
     before = gradients(

time: 131 us -> 129 us (0.985)
  starting transfers between devices: 42.1 us -> 40.6 us
    ppermute x19, waiting for transfers between devices: 21 us -> 5.47 us  [swap(): return lax.ppermute(v, 'dp', [(i, i ^ distance) for i in range(n)])]
    ppermute x21, waiting for transfers between devices: 35.2 us -> 50.1 us  [pass_on(): return lax.ppermute(v, 'expert', [(i, i ^ distance) for i in range(n)])]
  transfers between devices with their start and end apart: 40 -> 40, of which waited for: 20 -> 17; matrix products, arithmetic and copies ran while one was open for 1% -> 1% of each run, Pallas kernels for 16% -> 17%
where the time goes in v5:
time: 129 us; the launch traced here: 128 us
  waiting for transfers between devices  55.6 us (43%)
  starting transfers between devices  40.6 us (31%)
  Pallas kernels  25.5 us (20%)
  local copies, waits for them, and re-layouts  4.06 us (3%)
  other arithmetic  1.41 us (1%)
    ppermute x21, waiting for transfers between devices, pass_on(): return lax.ppermute(v, 'expert', [(i, i ^ distance) for i in range(n)])  50.1 us
    ppermute x21, starting transfers between devices, pass_on(): return lax.ppermute(v, 'expert', [(i, i ^ distance) for i in range(n)])  31.2 us
    pallas_call x2, Pallas kernels, gradients(): call(functools.partial(gradients_kernel, tiles, count), 'gradients_sum' i...  13.1 us
    ppermute x19, starting transfers between devices, swap(): return lax.ppermute(v, 'dp', [(i, i ^ distance) for i in range(n)])  9.42 us
    pallas_call x2, Pallas kernels, forward(): call(functools.partial(forward_kernel, steps), 'forward', [jax.ShapeDtype...  9.17 us
    ppermute x19, waiting for transfers between devices, swap(): return lax.ppermute(v, 'dp', [(i, i ^ distance) for i in range(n)])  5.47 us
    unnamed x22, local copies, waits for them, and re-layouts  3.77 us
  transfers between devices with their start and end apart: 40, of which 17 were waited for; matrix products, arithmetic and copies ran while one was open for 1% of the time, Pallas kernels for 17%

profile of v5, /device:TPU:0, one launch (start us, length us, event | category | flops | bytes accessed | tf_op | source)
XLA Modules:
  0.0 128.3 jit_solution(13920325544212062224)
XLA Ops:
  4.0 2.6 %collective-permute-start.3 = (bf16[96,3072]{1,0:T(8,128)(2,1)S(1)}, bf16[96,3072]{1,0:T(8,128)(2,1)S(1)}, u32[]{:S(2)}, u32[]{:S(2)}) collective-permute-start(bf16[96,3072]{1,0:T(8,128)(2,1)S(1)} %get-tuple-element.106), channel_id=1, source_target_pairs={{0,1},{1,0},{2,3},{3,2},{4,5},{5,4},{6,7},{7,6},{8,9},{9,8},{10,11... | collective-permute-start | bytes 1769480 | tf_op jit(solution)/shard_map/ppermute | solution.py:46
  6.8 3.6 %collective-permute-start = (bf16[24,3072]{1,0:T(8,128)(2,1)S(1)}, bf16[24,3072]{1,0:T(8,128)(2,1)S(1)}, u32[]{:S(2)}, u32[]{:S(2)}) collective-permute-start(bf16[24,3072]{1,0:T(8,128)(2,1)S(1)} %get-tuple-element.103), channel_id=1, source_target_pairs={{0,6},{1,7},{2,4},{3,5},{4,2},{5,3},{6,0},{7,1},{8,14},{9,15},{10,... | collective-permute-start | bytes 442376 | tf_op jit(solution)/shard_map/ppermute | solution.py:46
  12.0 3.4 %collective-permute-done = bf16[24,3072]{1,0:T(8,128)(2,1)S(1)} collective-permute-done((bf16[24,3072]{1,0:T(8,128)(2,1)S(1)}, bf16[24,3072]{1,0:T(8,128)(2,1)S(1)}, u32[]{:S(2)}, u32[]{:S(2)}) %collective-permute-start) | collective-permute-done | bytes 147488 | tf_op jit(solution)/shard_map/ppermute | solution.py:46
  15.4 8.0 %collective-permute-done.1 = bf16[24,3072]{1,0:T(8,128)(2,1)S(1)} collective-permute-done((bf16[24,3072]{1,0:T(8,128)(2,1)S(1)}, bf16[24,3072]{1,0:T(8,128)(2,1)S(1)}, u32[]{:S(2)}, u32[]{:S(2)}) %collective-permute-start.1) | collective-permute-done | bytes 147488 | tf_op jit(solution)/shard_map/ppermute | solution.py:46
  25.2 2.5 %collective-permute-start.6 = (bf16[24,3072]{1,0:T(8,128)(2,1)S(1)}, bf16[24,3072]{1,0:T(8,128)(2,1)S(1)}, u32[]{:S(2)}, u32[]{:S(2)}) collective-permute-start(bf16[24,3072]{1,0:T(8,128)(2,1)S(1)} %get-tuple-element.209), channel_id=1, source_target_pairs={{0,6},{1,7},{2,4},{3,5},{4,2},{5,3},{6,0},{7,1},{8,14},{9,15},{10,... | collective-permute-start | bytes 442376 | tf_op jit(solution)/shard_map/ppermute | solution.py:46
  27.7 1.9 %collective-permute-start.8 = (bf16[24,3072]{1,0:T(8,128)(2,1)S(1)}, bf16[24,3072]{1,0:T(8,128)(2,1)S(1)}, u32[]{:S(2)}, u32[]{:S(2)}) collective-permute-start(bf16[24,3072]{1,0:T(8,128)(2,1)S(1)} %get-tuple-element.207), channel_id=1, source_target_pairs={{0,2},{1,3},{2,0},{3,1},{4,6},{5,7},{6,4},{7,5},{8,10},{9,11},{10,... | collective-permute-start | bytes 442376 | tf_op jit(solution)/shard_map/ppermute | solution.py:46
  29.6 4.2 %collective-permute-done.6 = bf16[24,3072]{1,0:T(8,128)(2,1)S(1)} collective-permute-done((bf16[24,3072]{1,0:T(8,128)(2,1)S(1)}, bf16[24,3072]{1,0:T(8,128)(2,1)S(1)}, u32[]{:S(2)}, u32[]{:S(2)}) %collective-permute-start.6) | collective-permute-done | bytes 147488 | tf_op jit(solution)/shard_map/ppermute | solution.py:46
  33.9 5.9 %collective-permute-done.7 = bf16[24,3072]{1,0:T(8,128)(2,1)S(1)} collective-permute-done((bf16[24,3072]{1,0:T(8,128)(2,1)S(1)}, bf16[24,3072]{1,0:T(8,128)(2,1)S(1)}, u32[]{:S(2)}, u32[]{:S(2)}) %collective-permute-start.7) | collective-permute-done | bytes 147488 | tf_op jit(solution)/shard_map/ppermute | solution.py:46
  41.5 2.5 %collective-permute-start.11 = (bf16[24,3072]{1,0:T(8,128)(2,1)S(1)}, bf16[24,3072]{1,0:T(8,128)(2,1)S(1)}, u32[]{:S(2)}, u32[]{:S(2)}) collective-permute-start(bf16[24,3072]{1,0:T(8,128)(2,1)S(1)} %get-tuple-element.118), channel_id=1, source_target_pairs={{0,6},{1,7},{2,4},{3,5},{4,2},{5,3},{6,0},{7,1},{8,14},{9,15},{10,... | collective-permute-start | bytes 442376 | tf_op jit(solution)/shard_map/ppermute | solution.py:46
  45.9 4.6 %forward.2 = (f32[192,512]{1,0:T(8,128)S(1)}, f32[192,512]{1,0:T(8,128)S(1)}, f32[96,3072]{1,0:T(8,128)S(1)}, bf16[96,3072]{1,0:T(8,128)(2,1)S(1)}) custom-call(bf16[96,3072]{1,0:T(8,128)(2,1)S(1)} %constant_dynamic-update-slice_fusion.mine.refs_6_, bf16[96,3072]{1,0:T(8,128)(2,1)S(1)} %collective-permute-done.9.far.refs_8_, ...), custom_call_target="tpu_custom_call" | custom-call | flops 24159191040 | bytes 167116800 | tf_op jit(solution)/shard_map/forward/pallas_call | solution.py:169
  50.5 5.1 %collective-permute-done.12 = bf16[24,3072]{1,0:T(8,128)(2,1)S(1)} collective-permute-done((bf16[24,3072]{1,0:T(8,128)(2,1)S(1)}, bf16[24,3072]{1,0:T(8,128)(2,1)S(1)}, u32[]{:S(2)}, u32[]{:S(2)}) %collective-permute-start.12) | collective-permute-done | bytes 147488 | tf_op jit(solution)/shard_map/ppermute | solution.py:46
  57.4 2.5 %collective-permute-start.17 = (bf16[24,3072]{1,0:T(8,128)(2,1)S(1)}, bf16[24,3072]{1,0:T(8,128)(2,1)S(1)}, u32[]{:S(2)}, u32[]{:S(2)}) collective-permute-start(bf16[24,3072]{1,0:T(8,128)(2,1)S(1)} %get-tuple-element.205), channel_id=1, source_target_pairs={{0,6},{1,7},{2,4},{3,5},{4,2},{5,3},{6,0},{7,1},{8,14},{9,15},{10,... | collective-permute-start | bytes 442376 | tf_op jit(solution)/shard_map/ppermute | solution.py:46
  63.8 4.6 %forward.3 = (f32[192,512]{1,0:T(8,128)S(1)}, f32[192,512]{1,0:T(8,128)S(1)}, f32[96,3072]{1,0:T(8,128)S(1)}, bf16[96,3072]{1,0:T(8,128)(2,1)S(1)}) custom-call(bf16[96,3072]{1,0:T(8,128)(2,1)S(1)} %constant_dynamic-update-slice_fusion.4.mine.refs_10_, bf16[96,3072]{1,0:T(8,128)(2,1)S(1)} %collective-permute-done.14.far.refs_2_, ...), custom_call_target="tpu_custom_call" | custom-call | flops 24159191040 | bytes 167116800 | tf_op jit(solution)/shard_map/forward/pallas_call | solution.py:169
  68.4 3.5 %collective-permute-done.18 = bf16[24,3072]{1,0:T(8,128)(2,1)S(1)} collective-permute-done((bf16[24,3072]{1,0:T(8,128)(2,1)S(1)}, bf16[24,3072]{1,0:T(8,128)(2,1)S(1)}, u32[]{:S(2)}, u32[]{:S(2)}) %collective-permute-start.18) | collective-permute-done | bytes 147488 | tf_op jit(solution)/shard_map/ppermute | solution.py:46
  75.3 2.8 %collective-permute-start.23 = (bf16[24,3072]{1,0:T(8,128)(2,1)S(1)}, bf16[24,3072]{1,0:T(8,128)(2,1)S(1)}, u32[]{:S(2)}, u32[]{:S(2)}) collective-permute-start(bf16[24,3072]{1,0:T(8,128)(2,1)S(1)} %get-tuple-element.199), channel_id=1, source_target_pairs={{0,2},{1,3},{2,0},{3,1},{4,6},{5,7},{6,4},{7,5},{8,10},{9,11},{10,... | collective-permute-start | bytes 442376 | tf_op jit(solution)/shard_map/ppermute | solution.py:46
  78.3 4.0 %collective-permute-done.21 = bf16[24,3072]{1,0:T(8,128)(2,1)S(1)} collective-permute-done((bf16[24,3072]{1,0:T(8,128)(2,1)S(1)}, bf16[24,3072]{1,0:T(8,128)(2,1)S(1)}, u32[]{:S(2)}, u32[]{:S(2)}) %collective-permute-start.21) | collective-permute-done | bytes 147488 | tf_op jit(solution)/shard_map/ppermute | solution.py:46
  82.3 6.5 %collective-permute-done.22 = bf16[24,3072]{1,0:T(8,128)(2,1)S(1)} collective-permute-done((bf16[24,3072]{1,0:T(8,128)(2,1)S(1)}, bf16[24,3072]{1,0:T(8,128)(2,1)S(1)}, u32[]{:S(2)}, u32[]{:S(2)}) %collective-permute-start.22) | collective-permute-done | bytes 147488 | tf_op jit(solution)/shard_map/ppermute | solution.py:46
  90.4 2.1 %collective-permute-start.26 = (bf16[24,3072]{1,0:T(8,128)(2,1)S(1)}, bf16[24,3072]{1,0:T(8,128)(2,1)S(1)}, u32[]{:S(2)}, u32[]{:S(2)}) collective-permute-start(bf16[24,3072]{1,0:T(8,128)(2,1)S(1)} %get-tuple-element.198), channel_id=1, source_target_pairs={{0,7},{1,6},{2,5},{3,4},{4,3},{5,2},{6,1},{7,0},{8,15},{9,14},{10,... | collective-permute-start | bytes 442376 | tf_op jit(solution)/shard_map/ppermute | solution.py:46
  92.5 3.3 %collective-permute-start.28 = (bf16[24,3072]{1,0:T(8,128)(2,1)S(1)}, bf16[24,3072]{1,0:T(8,128)(2,1)S(1)}, u32[]{:S(2)}, u32[]{:S(2)}) collective-permute-start(bf16[24,3072]{1,0:T(8,128)(2,1)S(1)} %get-tuple-element.196), channel_id=1, source_target_pairs={{0,3},{1,2},{2,1},{3,0},{4,7},{5,6},{6,5},{7,4},{8,11},{9,10},{10,... | collective-permute-start | bytes 442376 | tf_op jit(solution)/shard_map/ppermute | solution.py:46
  96.0 3.9 %collective-permute-done.26 = bf16[24,3072]{1,0:T(8,128)(2,1)S(1)} collective-permute-done((bf16[24,3072]{1,0:T(8,128)(2,1)S(1)}, bf16[24,3072]{1,0:T(8,128)(2,1)S(1)}, u32[]{:S(2)}, u32[]{:S(2)}) %collective-permute-start.26) | collective-permute-done | bytes 147488 | tf_op jit(solution)/shard_map/ppermute | solution.py:46
  100.0 5.5 %collective-permute-done.27 = bf16[24,3072]{1,0:T(8,128)(2,1)S(1)} collective-permute-done((bf16[24,3072]{1,0:T(8,128)(2,1)S(1)}, bf16[24,3072]{1,0:T(8,128)(2,1)S(1)}, u32[]{:S(2)}, u32[]{:S(2)}) %collective-permute-start.27) | collective-permute-done | bytes 147488 | tf_op jit(solution)/shard_map/ppermute | solution.py:46
  110.0 9.0 %gradients.1 = (bf16[1,3072,512]{2,1,0:T(8,128)(2,1)S(1)}, bf16[1,3072,512]{2,1,0:T(8,128)(2,1)S(1)}) custom-call(bf16[96,3072]{1,0:T(8,128)(2,1)S(1)} %get-tuple-element.175.refs_0_, bf16[96,3072]{1,0:T(8,128)(2,1)S(1)} %collective-permute-done.37.refs_1_, bf16[96,3072]{1,0:T(8,128)(2,1)S(1)} %collective-permute-done.29.refs_2_, ...), custom_call_target="tpu_custom_call" | custom-call | flops 54358179840 | bytes 165150720 | tf_op jit(solution)/shard_map/gradients/pallas_call | solution.py:243
  119.0 3.1 %collective-permute-done.35.refs_0_ = bf16[96,3072]{1,0:T(8,128)(2,1)S(1)} collective-permute-done((bf16[96,3072]{1,0:T(8,128)(2,1)S(1)}, bf16[96,3072]{1,0:T(8,128)(2,1)S(1)}, u32[]{:S(2)}, u32[]{:S(2)}) %collective-permute-start.35) | collective-permute-done | bytes 589856 | tf_op jit(solution)/shard_map/ppermute | solution.py:41
  124.1 4.1 %gradients_sum.1 = (bf16[1,3072,512]{2,1,0:T(8,128)(2,1)}, bf16[1,3072,512]{2,1,0:T(8,128)(2,1)}) custom-call(bf16[96,3072]{1,0:T(8,128)(2,1)S(1)} %collective-permute-done.35.refs_0_, bf16[96,3072]{1,0:T(8,128)(2,1)S(1)} %collective-permute-done.39.refs_1_, bf16[96,3072]{1,0:T(8,128)(2,1)S(1)} %collective-permute-done.14.far.refs_2_, ...), custom_call_target="tpu_custom_call" | custom-call | flops 18119393280 | bytes 117964800 | tf_op jit(solution)/shard_map/gradients_sum/pallas_call | solution.py:243
  (104 shorter events, 28.0 us)
Async XLA Ops:
  0.6 22.7 %collective-permute-start.5 = (bf16[3072,512]{1,0:T(8,128)(2,1)}, bf16[3072,512]{1,0:T(8,128)(2,1)S(1)}, u32[]{:S(2)}, u32[]{:S(2)}) collective-permute-start(bf16[3072,512]{1,0:T(8,128)(2,1)} %bitcast.3), channel_id=1, source_target_pairs={{0,8},{8,0},{16,24},{24,16},{1,9},{9,1},{17,25},{25,17},{2,10},{10... | collective-permute-start | bytes 9437192 | tf_op jit(solution)/shard_map/ppermute | solution.py:41
  4.0 19.4 %collective-permute-start.3 = (bf16[96,3072]{1,0:T(8,128)(2,1)S(1)}, bf16[96,3072]{1,0:T(8,128)(2,1)S(1)}, u32[]{:S(2)}, u32[]{:S(2)}) collective-permute-start(bf16[96,3072]{1,0:T(8,128)(2,1)S(1)} %get-tuple-element.106), channel_id=1, source_target_pairs={{0,1},{1,0},{2,3},{3,2},{4,5},{5,4},{6,7},{7,6},{8,9},{9,8},{10,11... | collective-permute-start | bytes 1769480 | tf_op jit(solution)/shard_map/ppermute | solution.py:46
  10.4 12.9 %collective-permute-start.1 = (bf16[24,3072]{1,0:T(8,128)(2,1)S(1)}, bf16[24,3072]{1,0:T(8,128)(2,1)S(1)}, u32[]{:S(2)}, u32[]{:S(2)}) collective-permute-start(bf16[24,3072]{1,0:T(8,128)(2,1)S(1)} %get-tuple-element.104), channel_id=1, source_target_pairs={{0,4},{1,5},{2,6},{3,7},{4,0},{5,1},{6,2},{7,3},{8,12},{9,13},{10,... | collective-permute-start | bytes 442376 | tf_op jit(solution)/shard_map/ppermute | solution.py:46
  10.4 12.9 %collective-permute-start.2 = (bf16[24,3072]{1,0:T(8,128)(2,1)S(1)}, bf16[24,3072]{1,0:T(8,128)(2,1)S(1)}, u32[]{:S(2)}, u32[]{:S(2)}) collective-permute-start(bf16[24,3072]{1,0:T(8,128)(2,1)S(1)} %get-tuple-element.105), channel_id=1, source_target_pairs={{0,2},{1,3},{2,0},{3,1},{4,6},{5,7},{6,4},{7,5},{8,10},{9,11},{10,... | collective-permute-start | bytes 442376 | tf_op jit(solution)/shard_map/ppermute | solution.py:46
  23.4 16.4 %collective-permute-start.10 = (bf16[3072,512]{1,0:T(8,128)(2,1)S(1)}, bf16[3072,512]{1,0:T(8,128)(2,1)S(1)}, u32[]{:S(2)}, u32[]{:S(2)}) collective-permute-start(bf16[3072,512]{1,0:T(8,128)(2,1)S(1)} %bitcast.6), channel_id=1, source_target_pairs={{0,8},{8,0},{16,24},{24,16},{1,9},{9,1},{17,25},{25,17},{2,10},{10... | collective-permute-start | bytes 9437192 | tf_op jit(solution)/shard_map/ppermute | solution.py:41
  23.6 16.2 %collective-permute-start.9 = (bf16[96,3072]{1,0:T(8,128)(2,1)S(1)}, bf16[96,3072]{1,0:T(8,128)(2,1)S(1)}, u32[]{:S(2)}, u32[]{:S(2)}) collective-permute-start(bf16[96,3072]{1,0:T(8,128)(2,1)S(1)} %constant_dynamic-update-slice_fusion.mine.refs_6_), channel_id=1, source_target_pairs={{0,16},{8,24},{16,0},{24,8},{1,17},{9,25},{17,1},{25,9},{2,18},{10... | collective-permute-start | bytes 1769480 | tf_op jit(solution)/shard_map/ppermute | solution.py:41
  27.7 12.1 %collective-permute-start.7 = (bf16[24,3072]{1,0:T(8,128)(2,1)S(1)}, bf16[24,3072]{1,0:T(8,128)(2,1)S(1)}, u32[]{:S(2)}, u32[]{:S(2)}) collective-permute-start(bf16[24,3072]{1,0:T(8,128)(2,1)S(1)} %get-tuple-element.208), channel_id=1, source_target_pairs={{0,4},{1,5},{2,6},{3,7},{4,0},{5,1},{6,2},{7,3},{8,12},{9,13},{10,... | collective-permute-start | bytes 442376 | tf_op jit(solution)/shard_map/ppermute | solution.py:46
  27.7 12.1 %collective-permute-start.8 = (bf16[24,3072]{1,0:T(8,128)(2,1)S(1)}, bf16[24,3072]{1,0:T(8,128)(2,1)S(1)}, u32[]{:S(2)}, u32[]{:S(2)}) collective-permute-start(bf16[24,3072]{1,0:T(8,128)(2,1)S(1)} %get-tuple-element.207), channel_id=1, source_target_pairs={{0,2},{1,3},{2,0},{3,1},{4,6},{5,7},{6,4},{7,5},{8,10},{9,11},{10,... | collective-permute-start | bytes 442376 | tf_op jit(solution)/shard_map/ppermute | solution.py:46
  39.9 15.7 %collective-permute-start.14 = (bf16[96,3072]{1,0:T(8,128)(2,1)S(1)}, bf16[96,3072]{1,0:T(8,128)(2,1)S(1)}, u32[]{:S(2)}, u32[]{:S(2)}) collective-permute-start(bf16[96,3072]{1,0:T(8,128)(2,1)S(1)} %constant_dynamic-update-slice_fusion.4.mine.refs_10_), channel_id=1, source_target_pairs={{0,16},{8,24},{16,0},{24,8},{1,17},{9,25},{17,1},{25,9},{2,18},{10... | collective-permute-start | bytes 1769480 | tf_op jit(solution)/shard_map/ppermute | solution.py:41
  41.0 14.7 %collective-permute-start.15 = (bf16[96,3072]{1,0:T(8,128)(2,1)S(1)}, bf16[96,3072]{1,0:T(8,128)(2,1)S(1)}, u32[]{:S(2)}, u32[]{:S(2)}) collective-permute-start(bf16[96,3072]{1,0:T(8,128)(2,1)S(1)} %get-tuple-element.130), channel_id=1, source_target_pairs={{0,1},{1,0},{2,3},{3,2},{4,5},{5,4},{6,7},{7,6},{8,9},{9,8},{10,11... | collective-permute-start | bytes 1769480 | tf_op jit(solution)/shard_map/ppermute | solution.py:46
  44.0 11.6 %collective-permute-start.12 = (bf16[24,3072]{1,0:T(8,128)(2,1)S(1)}, bf16[24,3072]{1,0:T(8,128)(2,1)S(1)}, u32[]{:S(2)}, u32[]{:S(2)}) collective-permute-start(bf16[24,3072]{1,0:T(8,128)(2,1)S(1)} %get-tuple-element.119), channel_id=1, source_target_pairs={{0,4},{1,5},{2,6},{3,7},{4,0},{5,1},{6,2},{7,3},{8,12},{9,13},{10,... | collective-permute-start | bytes 442376 | tf_op jit(solution)/shard_map/ppermute | solution.py:46
  55.7 16.3 %collective-permute-start.20 = (bf16[96,3072]{1,0:T(8,128)(2,1)S(1)}, bf16[96,3072]{1,0:T(8,128)(2,1)S(1)}, u32[]{:S(2)}, u32[]{:S(2)}) collective-permute-start(bf16[96,3072]{1,0:T(8,128)(2,1)S(1)} %get-tuple-element.136), channel_id=1, source_target_pairs={{0,16},{8,24},{16,0},{24,8},{1,17},{9,25},{17,1},{25,9},{2,18},{10... | collective-permute-start | bytes 1769480 | tf_op jit(solution)/shard_map/ppermute | solution.py:41
  60.0 12.0 %collective-permute-start.18 = (bf16[24,3072]{1,0:T(8,128)(2,1)S(1)}, bf16[24,3072]{1,0:T(8,128)(2,1)S(1)}, u32[]{:S(2)}, u32[]{:S(2)}) collective-permute-start(bf16[24,3072]{1,0:T(8,128)(2,1)S(1)} %get-tuple-element.204), channel_id=1, source_target_pairs={{0,4},{1,5},{2,6},{3,7},{4,0},{5,1},{6,2},{7,3},{8,12},{9,13},{10,... | collective-permute-start | bytes 442376 | tf_op jit(solution)/shard_map/ppermute | solution.py:46
  60.0 12.0 %collective-permute-start.19 = (bf16[24,3072]{1,0:T(8,128)(2,1)S(1)}, bf16[24,3072]{1,0:T(8,128)(2,1)S(1)}, u32[]{:S(2)}, u32[]{:S(2)}) collective-permute-start(bf16[24,3072]{1,0:T(8,128)(2,1)S(1)} %get-tuple-element.203), channel_id=1, source_target_pairs={{0,2},{1,3},{2,0},{3,1},{4,6},{5,7},{6,4},{7,5},{8,10},{9,11},{10,... | collective-permute-start | bytes 442376 | tf_op jit(solution)/shard_map/ppermute | solution.py:46
  72.0 16.8 %collective-permute-start.24 = (bf16[96,3072]{1,0:T(8,128)(2,1)S(1)}, bf16[96,3072]{1,0:T(8,128)(2,1)S(1)}, u32[]{:S(2)}, u32[]{:S(2)}) collective-permute-start(bf16[96,3072]{1,0:T(8,128)(2,1)S(1)} %get-tuple-element.143), channel_id=1, source_target_pairs={{0,16},{8,24},{16,0},{24,8},{1,17},{9,25},{17,1},{25,9},{2,18},{10... | collective-permute-start | bytes 1769480 | tf_op jit(solution)/shard_map/ppermute | solution.py:41
  73.2 15.5 %collective-permute-start.25 = (f32[192,512]{1,0:T(8,128)S(1)}, f32[192,512]{1,0:T(8,128)S(1)}, u32[]{:S(2)}, u32[]{:S(2)}) collective-permute-start(f32[192,512]{1,0:T(8,128)S(1)} %get-tuple-element.148), channel_id=1, source_target_pairs={{0,8},{8,0},{16,24},{24,16},{1,9},{9,1},{17,25},{25,17},{2,10},{10... | collective-permute-start | bytes 1179656 | tf_op jit(solution)/shard_map/ppermute | solution.py:41
  75.3 13.4 %collective-permute-start.22 = (bf16[24,3072]{1,0:T(8,128)(2,1)S(1)}, bf16[24,3072]{1,0:T(8,128)(2,1)S(1)}, u32[]{:S(2)}, u32[]{:S(2)}) collective-permute-start(bf16[24,3072]{1,0:T(8,128)(2,1)S(1)} %get-tuple-element.200), channel_id=1, source_target_pairs={{0,4},{1,5},{2,6},{3,7},{4,0},{5,1},{6,2},{7,3},{8,12},{9,13},{10,... | collective-permute-start | bytes 442376 | tf_op jit(solution)/shard_map/ppermute | solution.py:46
  75.3 13.4 %collective-permute-start.23 = (bf16[24,3072]{1,0:T(8,128)(2,1)S(1)}, bf16[24,3072]{1,0:T(8,128)(2,1)S(1)}, u32[]{:S(2)}, u32[]{:S(2)}) collective-permute-start(bf16[24,3072]{1,0:T(8,128)(2,1)S(1)} %get-tuple-element.199), channel_id=1, source_target_pairs={{0,2},{1,3},{2,0},{3,1},{4,6},{5,7},{6,4},{7,5},{8,10},{9,11},{10,... | collective-permute-start | bytes 442376 | tf_op jit(solution)/shard_map/ppermute | solution.py:46
  88.8 16.7 %collective-permute-start.29 = (bf16[96,3072]{1,0:T(8,128)(2,1)S(1)}, bf16[96,3072]{1,0:T(8,128)(2,1)S(1)}, u32[]{:S(2)}, u32[]{:S(2)}) collective-permute-start(bf16[96,3072]{1,0:T(8,128)(2,1)S(1)} %get-tuple-element.175.refs_0_), channel_id=1, source_target_pairs={{0,16},{8,24},{16,0},{24,8},{1,17},{9,25},{17,1},{25,9},{2,18},{10... | collective-permute-start | bytes 1769480 | tf_op jit(solution)/shard_map/ppermute | solution.py:41
  92.5 13.0 %collective-permute-start.27 = (bf16[24,3072]{1,0:T(8,128)(2,1)S(1)}, bf16[24,3072]{1,0:T(8,128)(2,1)S(1)}, u32[]{:S(2)}, u32[]{:S(2)}) collective-permute-start(bf16[24,3072]{1,0:T(8,128)(2,1)S(1)} %get-tuple-element.197), channel_id=1, source_target_pairs={{0,5},{1,4},{2,7},{3,6},{4,1},{5,0},{6,3},{7,2},{8,13},{9,12},{10,... | collective-permute-start | bytes 442376 | tf_op jit(solution)/shard_map/ppermute | solution.py:46
  92.5 13.0 %collective-permute-start.28 = (bf16[24,3072]{1,0:T(8,128)(2,1)S(1)}, bf16[24,3072]{1,0:T(8,128)(2,1)S(1)}, u32[]{:S(2)}, u32[]{:S(2)}) collective-permute-start(bf16[24,3072]{1,0:T(8,128)(2,1)S(1)} %get-tuple-element.196), channel_id=1, source_target_pairs={{0,3},{1,2},{2,1},{3,0},{4,7},{5,6},{6,5},{7,4},{8,11},{9,10},{10,... | collective-permute-start | bytes 442376 | tf_op jit(solution)/shard_map/ppermute | solution.py:46
  106.7 15.4 %collective-permute-start.35 = (bf16[96,3072]{1,0:T(8,128)(2,1)S(1)}, bf16[96,3072]{1,0:T(8,128)(2,1)S(1)}, u32[]{:S(2)}, u32[]{:S(2)}) collective-permute-start(bf16[96,3072]{1,0:T(8,128)(2,1)S(1)} %get-tuple-element.169.refs_4_), channel_id=1, source_target_pairs={{0,16},{8,24},{16,0},{24,8},{1,17},{9,25},{17,1},{25,9},{2,18},{10... | collective-permute-start | bytes 1769480 | tf_op jit(solution)/shard_map/ppermute | solution.py:41
  108.3 13.8 %collective-permute-start.36 = (bf16[96,3072]{1,0:T(8,128)(2,1)S(1)}, bf16[96,3072]{1,0:T(8,128)(2,1)S(1)}, u32[]{:S(2)}, u32[]{:S(2)}) collective-permute-start(bf16[96,3072]{1,0:T(8,128)(2,1)S(1)} %collective-permute-done.14.far.refs_2_), channel_id=1, source_target_pairs={{0,8},{8,0},{16,24},{24,16},{1,9},{9,1},{17,25},{25,17},{2,10},{10... | collective-permute-start | bytes 1769480 | tf_op jit(solution)/shard_map/ppermute | solution.py:41
  108.5 13.8 %collective-permute-start.34 = (bf16[24,3072]{1,0:T(8,128)(2,1)S(1)}, bf16[24,3072]{1,0:T(8,128)(2,1)S(1)}, u32[]{:S(2)}, u32[]{:S(2)}) collective-permute-start(bf16[24,3072]{1,0:T(8,128)(2,1)S(1)} %get-tuple-element.170), channel_id=1, source_target_pairs={{0,1},{1,0},{2,3},{3,2},{4,5},{5,4},{6,7},{7,6},{8,9},{9,8},{10,11... | collective-permute-start | bytes 442376 | tf_op jit(solution)/shard_map/ppermute | solution.py:46
  (24 other events, 177.0 us)

commit v6 on v5

--- a/solution.py
+++ b/solution.py
@@ -91,9 +91,6 @@
 def place(name, kernel, first, values, sizes, with_slots):
     per_dev, features = values.shape
     slots = sum(sizes)
-    wanted = sizes
-    if any(size % 8 for size in sizes):
-        sizes = [slots]
     steps = 2
     cols = lambda rows: pl.BlockSpec((rows, features // steps), lambda i: (0, i))
     whole = lambda *shape: pl.BlockSpec(shape, lambda i: (0, 0))
@@ -109,11 +106,7 @@
         2 * slots * per_dev * features,
         2 * (per_dev + slots) * features,
     )(first, values)
-    parts = list(outs[with_slots:])
-    if len(parts) < len(wanted):
-        starts = [sum(wanted[:j]) for j in range(len(wanted))]
-        parts = [parts[0][start : start + size] for start, size in zip(starts, wanted)]
-    return outs[0], parts
+    return outs[0], outs[with_slots:]
 
 
 def clamp_parts(latent):
@@ -286,7 +279,7 @@
     enc = enc_weight[0]
     dec = dec_weight[0]
     pairs = experts // 2
-    sizes = [capacity] * pairs + [pairs * capacity]
+    sizes = [pairs * capacity] * 2
     by_slot, parts = place(
         "place",
         functools.partial(place_kernel, capacity, pairs),
@@ -295,7 +288,7 @@
         sizes,
         True,
     )
-    direct, via = parts[:pairs], parts[pairs]
+    direct, via = parts
     _, parts = place(
         "place_target",
         place_target_kernel,
@@ -304,7 +297,7 @@
         sizes,
         False,
     )
-    goal_direct, goal_via = parts[:pairs], parts[pairs]
+    goal_direct, goal_via = parts
 
     def outer(v, k, step=0):
         distance = 2 * ((pairs - k) % pairs) + step
@@ -327,7 +320,7 @@
         sides = [clamp_parts(jnp.concatenate([pre[c], got[c]], axis=0)) for c in (slice(size), slice(size, None))]
         return [v for side in sides for v in side]
 
-    out_direct = spread(direct)
+    out_direct, goal_direct = spread(cut(direct)), cut(goal_direct)
     out_via = pass_on(via, 1)
     enc_o = swap(enc, 1)
     *out_direct, out_via, goal_via, shift_o, enc_o = gate(out_direct + [out_via, goal_via, shift_o, enc_o])

time: 129 us -> 129 us (level)
  no operation moved by 1% of the time
where the time goes in v6:
time: 129 us; the launch traced here: 128 us
  waiting for transfers between devices  55.6 us (43%)
  starting transfers between devices  40.7 us (32%)
  Pallas kernels  25.4 us (20%)
  local copies, waits for them, and re-layouts  4.14 us (3%)
  other arithmetic  1.41 us (1%)
    ppermute x21, waiting for transfers between devices, pass_on(): return lax.ppermute(v, 'expert', [(i, i ^ distance) for i in range(n)])  50.1 us
    ppermute x21, starting transfers between devices, pass_on(): return lax.ppermute(v, 'expert', [(i, i ^ distance) for i in range(n)])  31.3 us
    pallas_call x2, Pallas kernels, gradients(): call(functools.partial(gradients_kernel, tiles, count), 'gradients_sum' i...  13.1 us
    ppermute x19, starting transfers between devices, swap(): return lax.ppermute(v, 'dp', [(i, i ^ distance) for i in range(n)])  9.43 us
    pallas_call x2, Pallas kernels, forward(): call(functools.partial(forward_kernel, steps), 'forward', [jax.ShapeDtype...  9.16 us
    ppermute x19, waiting for transfers between devices, swap(): return lax.ppermute(v, 'dp', [(i, i ^ distance) for i in range(n)])  5.44 us
    unnamed x22, local copies, waits for them, and re-layouts  3.77 us
  transfers between devices with their start and end apart: 40, of which 17 were waited for; matrix products, arithmetic and copies ran while one was open for 1% of the time, Pallas kernels for 17%

profile of v6, /device:TPU:0, one launch (start us, length us, event | category | flops | bytes accessed | tf_op | source)
XLA Modules:
  0.0 128.4 jit_solution(6279096574903359150)
XLA Ops:
  4.0 2.6 %collective-permute-start.3 = (bf16[96,3072]{1,0:T(8,128)(2,1)S(1)}, bf16[96,3072]{1,0:T(8,128)(2,1)S(1)}, u32[]{:S(2)}, u32[]{:S(2)}) collective-permute-start(bf16[96,3072]{1,0:T(8,128)(2,1)S(1)} %get-tuple-element.94), channel_id=1, source_target_pairs={{0,1},{1,0},{2,3},{3,2},{4,5},{5,4},{6,7},{7,6},{8,9},{9,8},{10,11... | collective-permute-start | bytes 1769480 | tf_op jit(solution)/shard_map/ppermute | solution.py:46
  6.8 3.7 %collective-permute-start = (bf16[24,3072]{1,0:T(8,128)(2,1)S(1)}, bf16[24,3072]{1,0:T(8,128)(2,1)S(1)}, u32[]{:S(2)}, u32[]{:S(2)}) collective-permute-start(bf16[24,3072]{1,0:T(8,128)(2,1)S(1)} %get-tuple-element.201), channel_id=1, source_target_pairs={{0,6},{1,7},{2,4},{3,5},{4,2},{5,3},{6,0},{7,1},{8,14},{9,15},{10,... | collective-permute-start | bytes 442376 | tf_op jit(solution)/shard_map/ppermute | solution.py:46
  12.1 3.4 %collective-permute-done = bf16[24,3072]{1,0:T(8,128)(2,1)S(1)} collective-permute-done((bf16[24,3072]{1,0:T(8,128)(2,1)S(1)}, bf16[24,3072]{1,0:T(8,128)(2,1)S(1)}, u32[]{:S(2)}, u32[]{:S(2)}) %collective-permute-start) | collective-permute-done | bytes 147488 | tf_op jit(solution)/shard_map/ppermute | solution.py:46
  15.5 8.0 %collective-permute-done.1 = bf16[24,3072]{1,0:T(8,128)(2,1)S(1)} collective-permute-done((bf16[24,3072]{1,0:T(8,128)(2,1)S(1)}, bf16[24,3072]{1,0:T(8,128)(2,1)S(1)}, u32[]{:S(2)}, u32[]{:S(2)}) %collective-permute-start.1) | collective-permute-done | bytes 147488 | tf_op jit(solution)/shard_map/ppermute | solution.py:46
  25.2 2.5 %collective-permute-start.6 = (bf16[24,3072]{1,0:T(8,128)(2,1)S(1)}, bf16[24,3072]{1,0:T(8,128)(2,1)S(1)}, u32[]{:S(2)}, u32[]{:S(2)}) collective-permute-start(bf16[24,3072]{1,0:T(8,128)(2,1)S(1)} %get-tuple-element.197), channel_id=1, source_target_pairs={{0,6},{1,7},{2,4},{3,5},{4,2},{5,3},{6,0},{7,1},{8,14},{9,15},{10,... | collective-permute-start | bytes 442376 | tf_op jit(solution)/shard_map/ppermute | solution.py:46
  29.7 4.2 %collective-permute-done.6 = bf16[24,3072]{1,0:T(8,128)(2,1)S(1)} collective-permute-done((bf16[24,3072]{1,0:T(8,128)(2,1)S(1)}, bf16[24,3072]{1,0:T(8,128)(2,1)S(1)}, u32[]{:S(2)}, u32[]{:S(2)}) %collective-permute-start.6) | collective-permute-done | bytes 147488 | tf_op jit(solution)/shard_map/ppermute | solution.py:46
  33.9 5.9 %collective-permute-done.7 = bf16[24,3072]{1,0:T(8,128)(2,1)S(1)} collective-permute-done((bf16[24,3072]{1,0:T(8,128)(2,1)S(1)}, bf16[24,3072]{1,0:T(8,128)(2,1)S(1)}, u32[]{:S(2)}, u32[]{:S(2)}) %collective-permute-start.7) | collective-permute-done | bytes 147488 | tf_op jit(solution)/shard_map/ppermute | solution.py:46
  41.6 2.5 %collective-permute-start.11 = (bf16[24,3072]{1,0:T(8,128)(2,1)S(1)}, bf16[24,3072]{1,0:T(8,128)(2,1)S(1)}, u32[]{:S(2)}, u32[]{:S(2)}) collective-permute-start(bf16[24,3072]{1,0:T(8,128)(2,1)S(1)} %get-tuple-element.106), channel_id=1, source_target_pairs={{0,6},{1,7},{2,4},{3,5},{4,2},{5,3},{6,0},{7,1},{8,14},{9,15},{10,... | collective-permute-start | bytes 442376 | tf_op jit(solution)/shard_map/ppermute | solution.py:46
  44.0 1.9 %collective-permute-start.13 = (bf16[24,3072]{1,0:T(8,128)(2,1)S(1)}, bf16[24,3072]{1,0:T(8,128)(2,1)S(1)}, u32[]{:S(2)}, u32[]{:S(2)}) collective-permute-start(bf16[24,3072]{1,0:T(8,128)(2,1)S(1)} %get-tuple-element.108), channel_id=1, source_target_pairs={{0,2},{1,3},{2,0},{3,1},{4,6},{5,7},{6,4},{7,5},{8,10},{9,11},{10,... | collective-permute-start | bytes 442376 | tf_op jit(solution)/shard_map/ppermute | solution.py:46
  46.0 4.6 %forward.2 = (f32[192,512]{1,0:T(8,128)S(1)}, f32[192,512]{1,0:T(8,128)S(1)}, f32[96,3072]{1,0:T(8,128)S(1)}, bf16[96,3072]{1,0:T(8,128)(2,1)S(1)}) custom-call(bf16[96,3072]{1,0:T(8,128)(2,1)S(1)} %constant_dynamic-update-slice_fusion.mine.refs_6_, bf16[96,3072]{1,0:T(8,128)(2,1)S(1)} %collective-permute-done.9.far.refs_8_, ...), custom_call_target="tpu_custom_call" | custom-call | flops 24159191040 | bytes 167116800 | tf_op jit(solution)/shard_map/forward/pallas_call | solution.py:162
  50.6 5.0 %collective-permute-done.12 = bf16[24,3072]{1,0:T(8,128)(2,1)S(1)} collective-permute-done((bf16[24,3072]{1,0:T(8,128)(2,1)S(1)}, bf16[24,3072]{1,0:T(8,128)(2,1)S(1)}, u32[]{:S(2)}, u32[]{:S(2)}) %collective-permute-start.12) | collective-permute-done | bytes 147488 | tf_op jit(solution)/shard_map/ppermute | solution.py:46
  57.5 2.5 %collective-permute-start.17 = (bf16[24,3072]{1,0:T(8,128)(2,1)S(1)}, bf16[24,3072]{1,0:T(8,128)(2,1)S(1)}, u32[]{:S(2)}, u32[]{:S(2)}) collective-permute-start(bf16[24,3072]{1,0:T(8,128)(2,1)S(1)} %get-tuple-element.193), channel_id=1, source_target_pairs={{0,6},{1,7},{2,4},{3,5},{4,2},{5,3},{6,0},{7,1},{8,14},{9,15},{10,... | collective-permute-start | bytes 442376 | tf_op jit(solution)/shard_map/ppermute | solution.py:46
  63.8 4.6 %forward.3 = (f32[192,512]{1,0:T(8,128)S(1)}, f32[192,512]{1,0:T(8,128)S(1)}, f32[96,3072]{1,0:T(8,128)S(1)}, bf16[96,3072]{1,0:T(8,128)(2,1)S(1)}) custom-call(bf16[96,3072]{1,0:T(8,128)(2,1)S(1)} %constant_dynamic-update-slice_fusion.4.mine.refs_10_, bf16[96,3072]{1,0:T(8,128)(2,1)S(1)} %collective-permute-done.14.far.refs_2_, ...), custom_call_target="tpu_custom_call" | custom-call | flops 24159191040 | bytes 167116800 | tf_op jit(solution)/shard_map/forward/pallas_call | solution.py:162
  68.5 3.5 %collective-permute-done.18 = bf16[24,3072]{1,0:T(8,128)(2,1)S(1)} collective-permute-done((bf16[24,3072]{1,0:T(8,128)(2,1)S(1)}, bf16[24,3072]{1,0:T(8,128)(2,1)S(1)}, u32[]{:S(2)}, u32[]{:S(2)}) %collective-permute-start.18) | collective-permute-done | bytes 147488 | tf_op jit(solution)/shard_map/ppermute | solution.py:46
  75.4 2.8 %collective-permute-start.23 = (bf16[24,3072]{1,0:T(8,128)(2,1)S(1)}, bf16[24,3072]{1,0:T(8,128)(2,1)S(1)}, u32[]{:S(2)}, u32[]{:S(2)}) collective-permute-start(bf16[24,3072]{1,0:T(8,128)(2,1)S(1)} %get-tuple-element.187), channel_id=1, source_target_pairs={{0,2},{1,3},{2,0},{3,1},{4,6},{5,7},{6,4},{7,5},{8,10},{9,11},{10,... | collective-permute-start | bytes 442376 | tf_op jit(solution)/shard_map/ppermute | solution.py:46
  78.4 4.0 %collective-permute-done.21 = bf16[24,3072]{1,0:T(8,128)(2,1)S(1)} collective-permute-done((bf16[24,3072]{1,0:T(8,128)(2,1)S(1)}, bf16[24,3072]{1,0:T(8,128)(2,1)S(1)}, u32[]{:S(2)}, u32[]{:S(2)}) %collective-permute-start.21) | collective-permute-done | bytes 147488 | tf_op jit(solution)/shard_map/ppermute | solution.py:46
  82.4 6.5 %collective-permute-done.22 = bf16[24,3072]{1,0:T(8,128)(2,1)S(1)} collective-permute-done((bf16[24,3072]{1,0:T(8,128)(2,1)S(1)}, bf16[24,3072]{1,0:T(8,128)(2,1)S(1)}, u32[]{:S(2)}, u32[]{:S(2)}) %collective-permute-start.22) | collective-permute-done | bytes 147488 | tf_op jit(solution)/shard_map/ppermute | solution.py:46
  90.5 2.2 %collective-permute-start.26 = (bf16[24,3072]{1,0:T(8,128)(2,1)S(1)}, bf16[24,3072]{1,0:T(8,128)(2,1)S(1)}, u32[]{:S(2)}, u32[]{:S(2)}) collective-permute-start(bf16[24,3072]{1,0:T(8,128)(2,1)S(1)} %get-tuple-element.186), channel_id=1, source_target_pairs={{0,7},{1,6},{2,5},{3,4},{4,3},{5,2},{6,1},{7,0},{8,15},{9,14},{10,... | collective-permute-start | bytes 442376 | tf_op jit(solution)/shard_map/ppermute | solution.py:46
  92.6 3.3 %collective-permute-start.28 = (bf16[24,3072]{1,0:T(8,128)(2,1)S(1)}, bf16[24,3072]{1,0:T(8,128)(2,1)S(1)}, u32[]{:S(2)}, u32[]{:S(2)}) collective-permute-start(bf16[24,3072]{1,0:T(8,128)(2,1)S(1)} %get-tuple-element.184), channel_id=1, source_target_pairs={{0,3},{1,2},{2,1},{3,0},{4,7},{5,6},{6,5},{7,4},{8,11},{9,10},{10,... | collective-permute-start | bytes 442376 | tf_op jit(solution)/shard_map/ppermute | solution.py:46
  96.1 4.0 %collective-permute-done.26 = bf16[24,3072]{1,0:T(8,128)(2,1)S(1)} collective-permute-done((bf16[24,3072]{1,0:T(8,128)(2,1)S(1)}, bf16[24,3072]{1,0:T(8,128)(2,1)S(1)}, u32[]{:S(2)}, u32[]{:S(2)}) %collective-permute-start.26) | collective-permute-done | bytes 147488 | tf_op jit(solution)/shard_map/ppermute | solution.py:46
  100.0 5.5 %collective-permute-done.27 = bf16[24,3072]{1,0:T(8,128)(2,1)S(1)} collective-permute-done((bf16[24,3072]{1,0:T(8,128)(2,1)S(1)}, bf16[24,3072]{1,0:T(8,128)(2,1)S(1)}, u32[]{:S(2)}, u32[]{:S(2)}) %collective-permute-start.27) | collective-permute-done | bytes 147488 | tf_op jit(solution)/shard_map/ppermute | solution.py:46
  110.1 9.0 %gradients.1 = (bf16[1,3072,512]{2,1,0:T(8,128)(2,1)S(1)}, bf16[1,3072,512]{2,1,0:T(8,128)(2,1)S(1)}) custom-call(bf16[96,3072]{1,0:T(8,128)(2,1)S(1)} %get-tuple-element.163.refs_0_, bf16[96,3072]{1,0:T(8,128)(2,1)S(1)} %collective-permute-done.37.refs_1_, bf16[96,3072]{1,0:T(8,128)(2,1)S(1)} %collective-permute-done.29.refs_2_, ...), custom_call_target="tpu_custom_call" | custom-call | flops 54358179840 | bytes 165150720 | tf_op jit(solution)/shard_map/gradients/pallas_call | solution.py:236
  119.1 3.1 %collective-permute-done.35.refs_0_ = bf16[96,3072]{1,0:T(8,128)(2,1)S(1)} collective-permute-done((bf16[96,3072]{1,0:T(8,128)(2,1)S(1)}, bf16[96,3072]{1,0:T(8,128)(2,1)S(1)}, u32[]{:S(2)}, u32[]{:S(2)}) %collective-permute-start.35) | collective-permute-done | bytes 589856 | tf_op jit(solution)/shard_map/ppermute | solution.py:41
  124.2 4.1 %gradients_sum.1 = (bf16[1,3072,512]{2,1,0:T(8,128)(2,1)}, bf16[1,3072,512]{2,1,0:T(8,128)(2,1)}) custom-call(bf16[96,3072]{1,0:T(8,128)(2,1)S(1)} %collective-permute-done.35.refs_0_, bf16[96,3072]{1,0:T(8,128)(2,1)S(1)} %collective-permute-done.39.refs_1_, bf16[96,3072]{1,0:T(8,128)(2,1)S(1)} %collective-permute-done.14.far.refs_2_, ...), custom_call_target="tpu_custom_call" | custom-call | flops 18119393280 | bytes 117964800 | tf_op jit(solution)/shard_map/gradients_sum/pallas_call | solution.py:236
  (106 shorter events, 28.2 us)
Async XLA Ops:
  0.6 22.8 %collective-permute-start.5 = (bf16[3072,512]{1,0:T(8,128)(2,1)}, bf16[3072,512]{1,0:T(8,128)(2,1)S(1)}, u32[]{:S(2)}, u32[]{:S(2)}) collective-permute-start(bf16[3072,512]{1,0:T(8,128)(2,1)} %bitcast.3), channel_id=1, source_target_pairs={{0,8},{8,0},{16,24},{24,16},{1,9},{9,1},{17,25},{25,17},{2,10},{10... | collective-permute-start | bytes 9437192 | tf_op jit(solution)/shard_map/ppermute | solution.py:41
  4.0 19.5 %collective-permute-start.3 = (bf16[96,3072]{1,0:T(8,128)(2,1)S(1)}, bf16[96,3072]{1,0:T(8,128)(2,1)S(1)}, u32[]{:S(2)}, u32[]{:S(2)}) collective-permute-start(bf16[96,3072]{1,0:T(8,128)(2,1)S(1)} %get-tuple-element.94), channel_id=1, source_target_pairs={{0,1},{1,0},{2,3},{3,2},{4,5},{5,4},{6,7},{7,6},{8,9},{9,8},{10,11... | collective-permute-start | bytes 1769480 | tf_op jit(solution)/shard_map/ppermute | solution.py:46
  10.5 12.9 %collective-permute-start.1 = (bf16[24,3072]{1,0:T(8,128)(2,1)S(1)}, bf16[24,3072]{1,0:T(8,128)(2,1)S(1)}, u32[]{:S(2)}, u32[]{:S(2)}) collective-permute-start(bf16[24,3072]{1,0:T(8,128)(2,1)S(1)} %get-tuple-element.200), channel_id=1, source_target_pairs={{0,4},{1,5},{2,6},{3,7},{4,0},{5,1},{6,2},{7,3},{8,12},{9,13},{10,... | collective-permute-start | bytes 442376 | tf_op jit(solution)/shard_map/ppermute | solution.py:46
  10.5 12.9 %collective-permute-start.2 = (bf16[24,3072]{1,0:T(8,128)(2,1)S(1)}, bf16[24,3072]{1,0:T(8,128)(2,1)S(1)}, u32[]{:S(2)}, u32[]{:S(2)}) collective-permute-start(bf16[24,3072]{1,0:T(8,128)(2,1)S(1)} %get-tuple-element.199), channel_id=1, source_target_pairs={{0,2},{1,3},{2,0},{3,1},{4,6},{5,7},{6,4},{7,5},{8,10},{9,11},{10,... | collective-permute-start | bytes 442376 | tf_op jit(solution)/shard_map/ppermute | solution.py:46
  23.5 16.4 %collective-permute-start.10 = (bf16[3072,512]{1,0:T(8,128)(2,1)S(1)}, bf16[3072,512]{1,0:T(8,128)(2,1)S(1)}, u32[]{:S(2)}, u32[]{:S(2)}) collective-permute-start(bf16[3072,512]{1,0:T(8,128)(2,1)S(1)} %bitcast.6), channel_id=1, source_target_pairs={{0,8},{8,0},{16,24},{24,16},{1,9},{9,1},{17,25},{25,17},{2,10},{10... | collective-permute-start | bytes 9437192 | tf_op jit(solution)/shard_map/ppermute | solution.py:41
  23.6 16.2 %collective-permute-start.9 = (bf16[96,3072]{1,0:T(8,128)(2,1)S(1)}, bf16[96,3072]{1,0:T(8,128)(2,1)S(1)}, u32[]{:S(2)}, u32[]{:S(2)}) collective-permute-start(bf16[96,3072]{1,0:T(8,128)(2,1)S(1)} %constant_dynamic-update-slice_fusion.mine.refs_6_), channel_id=1, source_target_pairs={{0,16},{8,24},{16,0},{24,8},{1,17},{9,25},{17,1},{25,9},{2,18},{10... | collective-permute-start | bytes 1769480 | tf_op jit(solution)/shard_map/ppermute | solution.py:41
  27.8 12.1 %collective-permute-start.7 = (bf16[24,3072]{1,0:T(8,128)(2,1)S(1)}, bf16[24,3072]{1,0:T(8,128)(2,1)S(1)}, u32[]{:S(2)}, u32[]{:S(2)}) collective-permute-start(bf16[24,3072]{1,0:T(8,128)(2,1)S(1)} %get-tuple-element.196), channel_id=1, source_target_pairs={{0,4},{1,5},{2,6},{3,7},{4,0},{5,1},{6,2},{7,3},{8,12},{9,13},{10,... | collective-permute-start | bytes 442376 | tf_op jit(solution)/shard_map/ppermute | solution.py:46
  27.8 12.1 %collective-permute-start.8 = (bf16[24,3072]{1,0:T(8,128)(2,1)S(1)}, bf16[24,3072]{1,0:T(8,128)(2,1)S(1)}, u32[]{:S(2)}, u32[]{:S(2)}) collective-permute-start(bf16[24,3072]{1,0:T(8,128)(2,1)S(1)} %get-tuple-element.195), channel_id=1, source_target_pairs={{0,2},{1,3},{2,0},{3,1},{4,6},{5,7},{6,4},{7,5},{8,10},{9,11},{10,... | collective-permute-start | bytes 442376 | tf_op jit(solution)/shard_map/ppermute | solution.py:46
  39.9 15.6 %collective-permute-start.14 = (bf16[96,3072]{1,0:T(8,128)(2,1)S(1)}, bf16[96,3072]{1,0:T(8,128)(2,1)S(1)}, u32[]{:S(2)}, u32[]{:S(2)}) collective-permute-start(bf16[96,3072]{1,0:T(8,128)(2,1)S(1)} %constant_dynamic-update-slice_fusion.4.mine.refs_10_), channel_id=1, source_target_pairs={{0,16},{8,24},{16,0},{24,8},{1,17},{9,25},{17,1},{25,9},{2,18},{10... | collective-permute-start | bytes 1769480 | tf_op jit(solution)/shard_map/ppermute | solution.py:41
  41.1 14.7 %collective-permute-start.15 = (bf16[96,3072]{1,0:T(8,128)(2,1)S(1)}, bf16[96,3072]{1,0:T(8,128)(2,1)S(1)}, u32[]{:S(2)}, u32[]{:S(2)}) collective-permute-start(bf16[96,3072]{1,0:T(8,128)(2,1)S(1)} %get-tuple-element.118), channel_id=1, source_target_pairs={{0,1},{1,0},{2,3},{3,2},{4,5},{5,4},{6,7},{7,6},{8,9},{9,8},{10,11... | collective-permute-start | bytes 1769480 | tf_op jit(solution)/shard_map/ppermute | solution.py:46
  44.0 11.5 %collective-permute-start.12 = (bf16[24,3072]{1,0:T(8,128)(2,1)S(1)}, bf16[24,3072]{1,0:T(8,128)(2,1)S(1)}, u32[]{:S(2)}, u32[]{:S(2)}) collective-permute-start(bf16[24,3072]{1,0:T(8,128)(2,1)S(1)} %get-tuple-element.107), channel_id=1, source_target_pairs={{0,4},{1,5},{2,6},{3,7},{4,0},{5,1},{6,2},{7,3},{8,12},{9,13},{10,... | collective-permute-start | bytes 442376 | tf_op jit(solution)/shard_map/ppermute | solution.py:46
  55.8 16.3 %collective-permute-start.20 = (bf16[96,3072]{1,0:T(8,128)(2,1)S(1)}, bf16[96,3072]{1,0:T(8,128)(2,1)S(1)}, u32[]{:S(2)}, u32[]{:S(2)}) collective-permute-start(bf16[96,3072]{1,0:T(8,128)(2,1)S(1)} %get-tuple-element.124), channel_id=1, source_target_pairs={{0,16},{8,24},{16,0},{24,8},{1,17},{9,25},{17,1},{25,9},{2,18},{10... | collective-permute-start | bytes 1769480 | tf_op jit(solution)/shard_map/ppermute | solution.py:41
  60.0 12.0 %collective-permute-start.18 = (bf16[24,3072]{1,0:T(8,128)(2,1)S(1)}, bf16[24,3072]{1,0:T(8,128)(2,1)S(1)}, u32[]{:S(2)}, u32[]{:S(2)}) collective-permute-start(bf16[24,3072]{1,0:T(8,128)(2,1)S(1)} %get-tuple-element.192), channel_id=1, source_target_pairs={{0,4},{1,5},{2,6},{3,7},{4,0},{5,1},{6,2},{7,3},{8,12},{9,13},{10,... | collective-permute-start | bytes 442376 | tf_op jit(solution)/shard_map/ppermute | solution.py:46
  60.0 12.0 %collective-permute-start.19 = (bf16[24,3072]{1,0:T(8,128)(2,1)S(1)}, bf16[24,3072]{1,0:T(8,128)(2,1)S(1)}, u32[]{:S(2)}, u32[]{:S(2)}) collective-permute-start(bf16[24,3072]{1,0:T(8,128)(2,1)S(1)} %get-tuple-element.191), channel_id=1, source_target_pairs={{0,2},{1,3},{2,0},{3,1},{4,6},{5,7},{6,4},{7,5},{8,10},{9,11},{10,... | collective-permute-start | bytes 442376 | tf_op jit(solution)/shard_map/ppermute | solution.py:46
  72.0 16.8 %collective-permute-start.24 = (bf16[96,3072]{1,0:T(8,128)(2,1)S(1)}, bf16[96,3072]{1,0:T(8,128)(2,1)S(1)}, u32[]{:S(2)}, u32[]{:S(2)}) collective-permute-start(bf16[96,3072]{1,0:T(8,128)(2,1)S(1)} %get-tuple-element.131), channel_id=1, source_target_pairs={{0,16},{8,24},{16,0},{24,8},{1,17},{9,25},{17,1},{25,9},{2,18},{10... | collective-permute-start | bytes 1769480 | tf_op jit(solution)/shard_map/ppermute | solution.py:41
  73.3 15.5 %collective-permute-start.25 = (f32[192,512]{1,0:T(8,128)S(1)}, f32[192,512]{1,0:T(8,128)S(1)}, u32[]{:S(2)}, u32[]{:S(2)}) collective-permute-start(f32[192,512]{1,0:T(8,128)S(1)} %get-tuple-element.136), channel_id=1, source_target_pairs={{0,8},{8,0},{16,24},{24,16},{1,9},{9,1},{17,25},{25,17},{2,10},{10... | collective-permute-start | bytes 1179656 | tf_op jit(solution)/shard_map/ppermute | solution.py:41
  75.4 13.4 %collective-permute-start.22 = (bf16[24,3072]{1,0:T(8,128)(2,1)S(1)}, bf16[24,3072]{1,0:T(8,128)(2,1)S(1)}, u32[]{:S(2)}, u32[]{:S(2)}) collective-permute-start(bf16[24,3072]{1,0:T(8,128)(2,1)S(1)} %get-tuple-element.188), channel_id=1, source_target_pairs={{0,4},{1,5},{2,6},{3,7},{4,0},{5,1},{6,2},{7,3},{8,12},{9,13},{10,... | collective-permute-start | bytes 442376 | tf_op jit(solution)/shard_map/ppermute | solution.py:46
  75.4 13.4 %collective-permute-start.23 = (bf16[24,3072]{1,0:T(8,128)(2,1)S(1)}, bf16[24,3072]{1,0:T(8,128)(2,1)S(1)}, u32[]{:S(2)}, u32[]{:S(2)}) collective-permute-start(bf16[24,3072]{1,0:T(8,128)(2,1)S(1)} %get-tuple-element.187), channel_id=1, source_target_pairs={{0,2},{1,3},{2,0},{3,1},{4,6},{5,7},{6,4},{7,5},{8,10},{9,11},{10,... | collective-permute-start | bytes 442376 | tf_op jit(solution)/shard_map/ppermute | solution.py:46
  88.8 16.7 %collective-permute-start.29 = (bf16[96,3072]{1,0:T(8,128)(2,1)S(1)}, bf16[96,3072]{1,0:T(8,128)(2,1)S(1)}, u32[]{:S(2)}, u32[]{:S(2)}) collective-permute-start(bf16[96,3072]{1,0:T(8,128)(2,1)S(1)} %get-tuple-element.163.refs_0_), channel_id=1, source_target_pairs={{0,16},{8,24},{16,0},{24,8},{1,17},{9,25},{17,1},{25,9},{2,18},{10... | collective-permute-start | bytes 1769480 | tf_op jit(solution)/shard_map/ppermute | solution.py:41
  92.6 12.9 %collective-permute-start.27 = (bf16[24,3072]{1,0:T(8,128)(2,1)S(1)}, bf16[24,3072]{1,0:T(8,128)(2,1)S(1)}, u32[]{:S(2)}, u32[]{:S(2)}) collective-permute-start(bf16[24,3072]{1,0:T(8,128)(2,1)S(1)} %get-tuple-element.185), channel_id=1, source_target_pairs={{0,5},{1,4},{2,7},{3,6},{4,1},{5,0},{6,3},{7,2},{8,13},{9,12},{10,... | collective-permute-start | bytes 442376 | tf_op jit(solution)/shard_map/ppermute | solution.py:46
  92.6 12.9 %collective-permute-start.28 = (bf16[24,3072]{1,0:T(8,128)(2,1)S(1)}, bf16[24,3072]{1,0:T(8,128)(2,1)S(1)}, u32[]{:S(2)}, u32[]{:S(2)}) collective-permute-start(bf16[24,3072]{1,0:T(8,128)(2,1)S(1)} %get-tuple-element.184), channel_id=1, source_target_pairs={{0,3},{1,2},{2,1},{3,0},{4,7},{5,6},{6,5},{7,4},{8,11},{9,10},{10,... | collective-permute-start | bytes 442376 | tf_op jit(solution)/shard_map/ppermute | solution.py:46
  106.8 15.4 %collective-permute-start.35 = (bf16[96,3072]{1,0:T(8,128)(2,1)S(1)}, bf16[96,3072]{1,0:T(8,128)(2,1)S(1)}, u32[]{:S(2)}, u32[]{:S(2)}) collective-permute-start(bf16[96,3072]{1,0:T(8,128)(2,1)S(1)} %get-tuple-element.157.refs_4_), channel_id=1, source_target_pairs={{0,16},{8,24},{16,0},{24,8},{1,17},{9,25},{17,1},{25,9},{2,18},{10... | collective-permute-start | bytes 1769480 | tf_op jit(solution)/shard_map/ppermute | solution.py:41
  108.4 13.8 %collective-permute-start.36 = (bf16[96,3072]{1,0:T(8,128)(2,1)S(1)}, bf16[96,3072]{1,0:T(8,128)(2,1)S(1)}, u32[]{:S(2)}, u32[]{:S(2)}) collective-permute-start(bf16[96,3072]{1,0:T(8,128)(2,1)S(1)} %collective-permute-done.14.far.refs_2_), channel_id=1, source_target_pairs={{0,8},{8,0},{16,24},{24,16},{1,9},{9,1},{17,25},{25,17},{2,10},{10... | collective-permute-start | bytes 1769480 | tf_op jit(solution)/shard_map/ppermute | solution.py:41
  108.5 13.8 %collective-permute-start.34 = (bf16[24,3072]{1,0:T(8,128)(2,1)S(1)}, bf16[24,3072]{1,0:T(8,128)(2,1)S(1)}, u32[]{:S(2)}, u32[]{:S(2)}) collective-permute-start(bf16[24,3072]{1,0:T(8,128)(2,1)S(1)} %get-tuple-element.158), channel_id=1, source_target_pairs={{0,1},{1,0},{2,3},{3,2},{4,5},{5,4},{6,7},{7,6},{8,9},{9,8},{10,11... | collective-permute-start | bytes 442376 | tf_op jit(solution)/shard_map/ppermute | solution.py:46
  (24 other events, 174.4 us)

commit v7 on v6

--- a/solution.py
+++ b/solution.py
@@ -358,7 +358,8 @@
     *home1, home_via, error0, efar0, cfar0, cmine0, error1, sides1[0], mine1, far1 = gate(
         home1 + [home_via[0], error0, efar0, cfar0, cmine0, error1, sides1[0], mine1, far1]
     )
-    efar1 = swap(error1, half)
+    split = error1.shape[0] // 2
+    efar1a, efar1b = swap(error1[:split], half), swap(error1[split:], half)
     ecross0, enear1, cmine1 = swap(efar0, 1), swap(error1, 1), swap(mine1, 1)
     home_via, far1 = gate([home_via, far1], ecross0, enear1)
     home1 = [pass_on(home_via, 1)] + home1
@@ -371,12 +372,19 @@
         dec,
         (),
     )
-    efar1, cfar1, *before = gate([efar1, cfar1, *before])
-    ecross1 = swap(efar1, 1)
-    homes = gate([join(home0), join(home1)], efar1)
+    homes = gate([join(home0), join(home1)], before[0])
     recon = collect(by_slot, *homes)
+    ecross1a = swap(after(efar1a, before[0]), 1)
+    efar1b, ecross1a, cfar1, recon, *before = gate([efar1b, ecross1a, cfar1, recon, *before])
+    ecross1b = swap(efar1b, 1)
+    parts = lambda v: [v[: v.shape[0] // 2], v[v.shape[0] // 2 :]]
     grad_enc, grad_dec = gradients(
-        [efar1, ecross1], [far1, cfar1], [sides1[2]], [sides1[3]], dec, before
+        [efar1a, efar1b, ecross1a, ecross1b],
+        parts(far1) + parts(cfar1),
+        parts(sides1[2]),
+        parts(sides1[3]),
+        dec,
+        before,
     )
     return recon, grad_enc, grad_dec
 

time: 129 us -> 129 us (level)
    ppermute x21, waiting for transfers between devices: 50.1 us -> 47.3 us  [pass_on(): return lax.ppermute(v, 'expert', [(i, i ^ distance) for i in range(n)])]
    ppermute x19 -> x21, waiting for transfers between devices: 5.44 us -> 8.04 us  [swap(): return lax.ppermute(v, 'dp', [(i, i ^ distance) for i in range(n)])]
    ppermute x19 -> x21, starting transfers between devices: 9.43 us -> 8.72 us  [swap(): return lax.ppermute(v, 'dp', [(i, i ^ distance) for i in range(n)])]
  transfers between devices with their start and end apart: 40 -> 42, of which waited for: 17 -> 18; matrix products, arithmetic and copies ran while one was open for 1% -> 2% of each run, Pallas kernels for 17% -> 17%
where the time goes in v7:
time: 129 us
  waiting for transfers between devices  55.4 us (43%)
  starting transfers between devices  40.8 us (32%)
  Pallas kernels  25.5 us (20%)
  local copies, waits for them, and re-layouts  4.3 us (3%)
  other arithmetic  1.4 us (1%)
    ppermute x21, waiting for transfers between devices, pass_on(): return lax.ppermute(v, 'expert', [(i, i ^ distance) for i in range(n)])  47.3 us
    ppermute x21, starting transfers between devices, pass_on(): return lax.ppermute(v, 'expert', [(i, i ^ distance) for i in range(n)])  32.1 us
    pallas_call x2, Pallas kernels, gradients(): call(functools.partial(gradients_kernel, tiles, count), 'gradients_sum' i...  13.1 us
    pallas_call x2, Pallas kernels, forward(): call(functools.partial(forward_kernel, steps), 'forward', [jax.ShapeDtype...  9.18 us
    ppermute x21, starting transfers between devices, swap(): return lax.ppermute(v, 'dp', [(i, i ^ distance) for i in range(n)])  8.72 us
    ppermute x21, waiting for transfers between devices, swap(): return lax.ppermute(v, 'dp', [(i, i ^ distance) for i in range(n)])  8.04 us
    unnamed x22, local copies, waits for them, and re-layouts  3.77 us
  transfers between devices with their start and end apart: 42, of which 18 were waited for; matrix products, arithmetic and copies ran while one was open for 2% of the time, Pallas kernels for 17%

profile of v7, /device:TPU:0, one launch (start us, length us, event | category | flops | bytes accessed | tf_op | source)
XLA Modules:
  0.0 128.6 jit_solution(6706604075047142190)
XLA Ops:
  4.0 2.6 %collective-permute-start.3 = (bf16[96,3072]{1,0:T(8,128)(2,1)S(1)}, bf16[96,3072]{1,0:T(8,128)(2,1)S(1)}, u32[]{:S(2)}, u32[]{:S(2)}) collective-permute-start(bf16[96,3072]{1,0:T(8,128)(2,1)S(1)} %get-tuple-element.97), channel_id=1, source_target_pairs={{0,1},{1,0},{2,3},{3,2},{4,5},{5,4},{6,7},{7,6},{8,9},{9,8},{10,11... | collective-permute-start | bytes 1769480 | tf_op jit(solution)/shard_map/ppermute | solution.py:46
  6.8 3.7 %collective-permute-start = (bf16[24,3072]{1,0:T(8,128)(2,1)S(1)}, bf16[24,3072]{1,0:T(8,128)(2,1)S(1)}, u32[]{:S(2)}, u32[]{:S(2)}) collective-permute-start(bf16[24,3072]{1,0:T(8,128)(2,1)S(1)} %get-tuple-element.213), channel_id=1, source_target_pairs={{0,6},{1,7},{2,4},{3,5},{4,2},{5,3},{6,0},{7,1},{8,14},{9,15},{10,... | collective-permute-start | bytes 442376 | tf_op jit(solution)/shard_map/ppermute | solution.py:46
  12.1 3.4 %collective-permute-done = bf16[24,3072]{1,0:T(8,128)(2,1)S(1)} collective-permute-done((bf16[24,3072]{1,0:T(8,128)(2,1)S(1)}, bf16[24,3072]{1,0:T(8,128)(2,1)S(1)}, u32[]{:S(2)}, u32[]{:S(2)}) %collective-permute-start) | collective-permute-done | bytes 147488 | tf_op jit(solution)/shard_map/ppermute | solution.py:46
  15.5 8.0 %collective-permute-done.1 = bf16[24,3072]{1,0:T(8,128)(2,1)S(1)} collective-permute-done((bf16[24,3072]{1,0:T(8,128)(2,1)S(1)}, bf16[24,3072]{1,0:T(8,128)(2,1)S(1)}, u32[]{:S(2)}, u32[]{:S(2)}) %collective-permute-start.1) | collective-permute-done | bytes 147488 | tf_op jit(solution)/shard_map/ppermute | solution.py:46
  25.2 2.5 %collective-permute-start.6 = (bf16[24,3072]{1,0:T(8,128)(2,1)S(1)}, bf16[24,3072]{1,0:T(8,128)(2,1)S(1)}, u32[]{:S(2)}, u32[]{:S(2)}) collective-permute-start(bf16[24,3072]{1,0:T(8,128)(2,1)S(1)} %get-tuple-element.209), channel_id=1, source_target_pairs={{0,6},{1,7},{2,4},{3,5},{4,2},{5,3},{6,0},{7,1},{8,14},{9,15},{10,... | collective-permute-start | bytes 442376 | tf_op jit(solution)/shard_map/ppermute | solution.py:46
  29.7 4.2 %collective-permute-done.6 = bf16[24,3072]{1,0:T(8,128)(2,1)S(1)} collective-permute-done((bf16[24,3072]{1,0:T(8,128)(2,1)S(1)}, bf16[24,3072]{1,0:T(8,128)(2,1)S(1)}, u32[]{:S(2)}, u32[]{:S(2)}) %collective-permute-start.6) | collective-permute-done | bytes 147488 | tf_op jit(solution)/shard_map/ppermute | solution.py:46
  33.9 5.9 %collective-permute-done.7 = bf16[24,3072]{1,0:T(8,128)(2,1)S(1)} collective-permute-done((bf16[24,3072]{1,0:T(8,128)(2,1)S(1)}, bf16[24,3072]{1,0:T(8,128)(2,1)S(1)}, u32[]{:S(2)}, u32[]{:S(2)}) %collective-permute-start.7) | collective-permute-done | bytes 147488 | tf_op jit(solution)/shard_map/ppermute | solution.py:46
  41.6 2.5 %collective-permute-start.11 = (bf16[24,3072]{1,0:T(8,128)(2,1)S(1)}, bf16[24,3072]{1,0:T(8,128)(2,1)S(1)}, u32[]{:S(2)}, u32[]{:S(2)}) collective-permute-start(bf16[24,3072]{1,0:T(8,128)(2,1)S(1)} %get-tuple-element.109), channel_id=1, source_target_pairs={{0,6},{1,7},{2,4},{3,5},{4,2},{5,3},{6,0},{7,1},{8,14},{9,15},{10,... | collective-permute-start | bytes 442376 | tf_op jit(solution)/shard_map/ppermute | solution.py:46
  44.0 1.9 %collective-permute-start.13 = (bf16[24,3072]{1,0:T(8,128)(2,1)S(1)}, bf16[24,3072]{1,0:T(8,128)(2,1)S(1)}, u32[]{:S(2)}, u32[]{:S(2)}) collective-permute-start(bf16[24,3072]{1,0:T(8,128)(2,1)S(1)} %get-tuple-element.111), channel_id=1, source_target_pairs={{0,2},{1,3},{2,0},{3,1},{4,6},{5,7},{6,4},{7,5},{8,10},{9,11},{10,... | collective-permute-start | bytes 442376 | tf_op jit(solution)/shard_map/ppermute | solution.py:46
  46.0 4.6 %forward.2 = (f32[192,512]{1,0:T(8,128)S(1)}, f32[192,512]{1,0:T(8,128)S(1)}, f32[96,3072]{1,0:T(8,128)S(1)}, bf16[96,3072]{1,0:T(8,128)(2,1)S(1)}) custom-call(bf16[96,3072]{1,0:T(8,128)(2,1)S(1)} %constant_dynamic-update-slice_fusion.mine.refs_6_, bf16[96,3072]{1,0:T(8,128)(2,1)S(1)} %collective-permute-done.9.far.refs_8_, ...), custom_call_target="tpu_custom_call" | custom-call | flops 24159191040 | bytes 167116800 | tf_op jit(solution)/shard_map/forward/pallas_call | solution.py:162
  50.6 5.0 %collective-permute-done.12 = bf16[24,3072]{1,0:T(8,128)(2,1)S(1)} collective-permute-done((bf16[24,3072]{1,0:T(8,128)(2,1)S(1)}, bf16[24,3072]{1,0:T(8,128)(2,1)S(1)}, u32[]{:S(2)}, u32[]{:S(2)}) %collective-permute-start.12) | collective-permute-done | bytes 147488 | tf_op jit(solution)/shard_map/ppermute | solution.py:46
  57.5 2.5 %collective-permute-start.17 = (bf16[24,3072]{1,0:T(8,128)(2,1)S(1)}, bf16[24,3072]{1,0:T(8,128)(2,1)S(1)}, u32[]{:S(2)}, u32[]{:S(2)}) collective-permute-start(bf16[24,3072]{1,0:T(8,128)(2,1)S(1)} %get-tuple-element.205), channel_id=1, source_target_pairs={{0,6},{1,7},{2,4},{3,5},{4,2},{5,3},{6,0},{7,1},{8,14},{9,15},{10,... | collective-permute-start | bytes 442376 | tf_op jit(solution)/shard_map/ppermute | solution.py:46
  63.8 4.6 %forward.3 = (f32[192,512]{1,0:T(8,128)S(1)}, f32[192,512]{1,0:T(8,128)S(1)}, f32[96,3072]{1,0:T(8,128)S(1)}, bf16[96,3072]{1,0:T(8,128)(2,1)S(1)}) custom-call(bf16[96,3072]{1,0:T(8,128)(2,1)S(1)} %constant_dynamic-update-slice_fusion.4.mine.refs_10_, bf16[96,3072]{1,0:T(8,128)(2,1)S(1)} %collective-permute-done.14.far, ...), custom_call_target="tpu_custom_call" | custom-call | flops 24159191040 | bytes 167116800 | tf_op jit(solution)/shard_map/forward/pallas_call | solution.py:162
  68.5 3.5 %collective-permute-done.18 = bf16[24,3072]{1,0:T(8,128)(2,1)S(1)} collective-permute-done((bf16[24,3072]{1,0:T(8,128)(2,1)S(1)}, bf16[24,3072]{1,0:T(8,128)(2,1)S(1)}, u32[]{:S(2)}, u32[]{:S(2)}) %collective-permute-start.18) | collective-permute-done | bytes 147488 | tf_op jit(solution)/shard_map/ppermute | solution.py:46
  75.4 2.8 %collective-permute-start.23 = (bf16[24,3072]{1,0:T(8,128)(2,1)S(1)}, bf16[24,3072]{1,0:T(8,128)(2,1)S(1)}, u32[]{:S(2)}, u32[]{:S(2)}) collective-permute-start(bf16[24,3072]{1,0:T(8,128)(2,1)S(1)} %get-tuple-element.199), channel_id=1, source_target_pairs={{0,2},{1,3},{2,0},{3,1},{4,6},{5,7},{6,4},{7,5},{8,10},{9,11},{10,... | collective-permute-start | bytes 442376 | tf_op jit(solution)/shard_map/ppermute | solution.py:46
  78.5 3.9 %collective-permute-done.21 = bf16[24,3072]{1,0:T(8,128)(2,1)S(1)} collective-permute-done((bf16[24,3072]{1,0:T(8,128)(2,1)S(1)}, bf16[24,3072]{1,0:T(8,128)(2,1)S(1)}, u32[]{:S(2)}, u32[]{:S(2)}) %collective-permute-start.21) | collective-permute-done | bytes 147488 | tf_op jit(solution)/shard_map/ppermute | solution.py:46
  82.4 5.3 %collective-permute-done.22 = bf16[24,3072]{1,0:T(8,128)(2,1)S(1)} collective-permute-done((bf16[24,3072]{1,0:T(8,128)(2,1)S(1)}, bf16[24,3072]{1,0:T(8,128)(2,1)S(1)}, u32[]{:S(2)}, u32[]{:S(2)}) %collective-permute-start.22) | collective-permute-done | bytes 147488 | tf_op jit(solution)/shard_map/ppermute | solution.py:46
  88.1 2.8 %collective-permute-start.26 = (bf16[24,3072]{1,0:T(8,128)(2,1)S(1)}, bf16[24,3072]{1,0:T(8,128)(2,1)S(1)}, u32[]{:S(2)}, u32[]{:S(2)}) collective-permute-start(bf16[24,3072]{1,0:T(8,128)(2,1)S(1)} %get-tuple-element.198), channel_id=1, source_target_pairs={{0,7},{1,6},{2,5},{3,4},{4,3},{5,2},{6,1},{7,0},{8,15},{9,14},{10,... | collective-permute-start | bytes 442376 | tf_op jit(solution)/shard_map/ppermute | solution.py:46
  91.7 3.5 %collective-permute-start.28 = (bf16[24,3072]{1,0:T(8,128)(2,1)S(1)}, bf16[24,3072]{1,0:T(8,128)(2,1)S(1)}, u32[]{:S(2)}, u32[]{:S(2)}) collective-permute-start(bf16[24,3072]{1,0:T(8,128)(2,1)S(1)} %get-tuple-element.196), channel_id=1, source_target_pairs={{0,3},{1,2},{2,1},{3,0},{4,7},{5,6},{6,5},{7,4},{8,11},{9,10},{10,... | collective-permute-start | bytes 442376 | tf_op jit(solution)/shard_map/ppermute | solution.py:46
  95.5 2.2 %collective-permute-done.26 = bf16[24,3072]{1,0:T(8,128)(2,1)S(1)} collective-permute-done((bf16[24,3072]{1,0:T(8,128)(2,1)S(1)}, bf16[24,3072]{1,0:T(8,128)(2,1)S(1)}, u32[]{:S(2)}, u32[]{:S(2)}) %collective-permute-start.26) | collective-permute-done | bytes 147488 | tf_op jit(solution)/shard_map/ppermute | solution.py:46
  97.6 5.8 %collective-permute-done.27 = bf16[24,3072]{1,0:T(8,128)(2,1)S(1)} collective-permute-done((bf16[24,3072]{1,0:T(8,128)(2,1)S(1)}, bf16[24,3072]{1,0:T(8,128)(2,1)S(1)}, u32[]{:S(2)}, u32[]{:S(2)}) %collective-permute-start.27) | collective-permute-done | bytes 147488 | tf_op jit(solution)/shard_map/ppermute | solution.py:46
  103.5 2.9 %collective-permute-done.29.refs_2_ = bf16[96,3072]{1,0:T(8,128)(2,1)S(1)} collective-permute-done((bf16[96,3072]{1,0:T(8,128)(2,1)S(1)}, bf16[96,3072]{1,0:T(8,128)(2,1)S(1)}, u32[]{:S(2)}, u32[]{:S(2)}) %collective-permute-start.29) | collective-permute-done | bytes 589856 | tf_op jit(solution)/shard_map/ppermute | solution.py:41
  110.0 9.0 %gradients.1 = (bf16[1,3072,512]{2,1,0:T(8,128)(2,1)S(1)}, bf16[1,3072,512]{2,1,0:T(8,128)(2,1)S(1)}) custom-call(bf16[96,3072]{1,0:T(8,128)(2,1)S(1)} %get-tuple-element.154.refs_0_, bf16[96,3072]{1,0:T(8,128)(2,1)S(1)} %collective-permute-done.34.refs_1_, bf16[96,3072]{1,0:T(8,128)(2,1)S(1)} %collective-permute-done.29.refs_2_, ...), custom_call_target="tpu_custom_call" | custom-call | flops 54358179840 | bytes 165150720 | tf_op jit(solution)/shard_map/gradients/pallas_call | solution.py:236
  124.3 4.1 %gradients_sum.1 = (bf16[1,3072,512]{2,1,0:T(8,128)(2,1)}, bf16[1,3072,512]{2,1,0:T(8,128)(2,1)}) custom-call(bf16[48,3072]{1,0:T(8,128)(2,1)S(1)} %collective-permute-done.33.refs_0_, bf16[48,3072]{1,0:T(8,128)(2,1)S(1)} %collective-permute-done.32.refs_1_, bf16[48,3072]{1,0:T(8,128)(2,1)S(1)} %collective-permute-done.38.refs_2_, ...), custom_call_target="tpu_custom_call" | custom-call | flops 18119393280 | bytes 117964800 | tf_op jit(solution)/shard_map/gradients_sum/pallas_call | solution.py:236
  (115 shorter events, 30.4 us)
Async XLA Ops:
  0.6 22.8 %collective-permute-start.5 = (bf16[3072,512]{1,0:T(8,128)(2,1)}, bf16[3072,512]{1,0:T(8,128)(2,1)S(1)}, u32[]{:S(2)}, u32[]{:S(2)}) collective-permute-start(bf16[3072,512]{1,0:T(8,128)(2,1)} %bitcast.3), channel_id=1, source_target_pairs={{0,8},{8,0},{16,24},{24,16},{1,9},{9,1},{17,25},{25,17},{2,10},{10... | collective-permute-start | bytes 9437192 | tf_op jit(solution)/shard_map/ppermute | solution.py:41
  4.0 19.5 %collective-permute-start.3 = (bf16[96,3072]{1,0:T(8,128)(2,1)S(1)}, bf16[96,3072]{1,0:T(8,128)(2,1)S(1)}, u32[]{:S(2)}, u32[]{:S(2)}) collective-permute-start(bf16[96,3072]{1,0:T(8,128)(2,1)S(1)} %get-tuple-element.97), channel_id=1, source_target_pairs={{0,1},{1,0},{2,3},{3,2},{4,5},{5,4},{6,7},{7,6},{8,9},{9,8},{10,11... | collective-permute-start | bytes 1769480 | tf_op jit(solution)/shard_map/ppermute | solution.py:46
  10.5 12.9 %collective-permute-start.1 = (bf16[24,3072]{1,0:T(8,128)(2,1)S(1)}, bf16[24,3072]{1,0:T(8,128)(2,1)S(1)}, u32[]{:S(2)}, u32[]{:S(2)}) collective-permute-start(bf16[24,3072]{1,0:T(8,128)(2,1)S(1)} %get-tuple-element.212), channel_id=1, source_target_pairs={{0,4},{1,5},{2,6},{3,7},{4,0},{5,1},{6,2},{7,3},{8,12},{9,13},{10,... | collective-permute-start | bytes 442376 | tf_op jit(solution)/shard_map/ppermute | solution.py:46
  10.5 12.9 %collective-permute-start.2 = (bf16[24,3072]{1,0:T(8,128)(2,1)S(1)}, bf16[24,3072]{1,0:T(8,128)(2,1)S(1)}, u32[]{:S(2)}, u32[]{:S(2)}) collective-permute-start(bf16[24,3072]{1,0:T(8,128)(2,1)S(1)} %get-tuple-element.211), channel_id=1, source_target_pairs={{0,2},{1,3},{2,0},{3,1},{4,6},{5,7},{6,4},{7,5},{8,10},{9,11},{10,... | collective-permute-start | bytes 442376 | tf_op jit(solution)/shard_map/ppermute | solution.py:46
  23.5 16.4 %collective-permute-start.10 = (bf16[3072,512]{1,0:T(8,128)(2,1)S(1)}, bf16[3072,512]{1,0:T(8,128)(2,1)S(1)}, u32[]{:S(2)}, u32[]{:S(2)}) collective-permute-start(bf16[3072,512]{1,0:T(8,128)(2,1)S(1)} %bitcast.6), channel_id=1, source_target_pairs={{0,8},{8,0},{16,24},{24,16},{1,9},{9,1},{17,25},{25,17},{2,10},{10... | collective-permute-start | bytes 9437192 | tf_op jit(solution)/shard_map/ppermute | solution.py:41
  23.6 16.2 %collective-permute-start.9 = (bf16[96,3072]{1,0:T(8,128)(2,1)S(1)}, bf16[96,3072]{1,0:T(8,128)(2,1)S(1)}, u32[]{:S(2)}, u32[]{:S(2)}) collective-permute-start(bf16[96,3072]{1,0:T(8,128)(2,1)S(1)} %constant_dynamic-update-slice_fusion.mine.refs_6_), channel_id=1, source_target_pairs={{0,16},{8,24},{16,0},{24,8},{1,17},{9,25},{17,1},{25,9},{2,18},{10... | collective-permute-start | bytes 1769480 | tf_op jit(solution)/shard_map/ppermute | solution.py:41
  27.8 12.1 %collective-permute-start.7 = (bf16[24,3072]{1,0:T(8,128)(2,1)S(1)}, bf16[24,3072]{1,0:T(8,128)(2,1)S(1)}, u32[]{:S(2)}, u32[]{:S(2)}) collective-permute-start(bf16[24,3072]{1,0:T(8,128)(2,1)S(1)} %get-tuple-element.208), channel_id=1, source_target_pairs={{0,4},{1,5},{2,6},{3,7},{4,0},{5,1},{6,2},{7,3},{8,12},{9,13},{10,... | collective-permute-start | bytes 442376 | tf_op jit(solution)/shard_map/ppermute | solution.py:46
  27.8 12.1 %collective-permute-start.8 = (bf16[24,3072]{1,0:T(8,128)(2,1)S(1)}, bf16[24,3072]{1,0:T(8,128)(2,1)S(1)}, u32[]{:S(2)}, u32[]{:S(2)}) collective-permute-start(bf16[24,3072]{1,0:T(8,128)(2,1)S(1)} %get-tuple-element.207), channel_id=1, source_target_pairs={{0,2},{1,3},{2,0},{3,1},{4,6},{5,7},{6,4},{7,5},{8,10},{9,11},{10,... | collective-permute-start | bytes 442376 | tf_op jit(solution)/shard_map/ppermute | solution.py:46
  39.9 15.6 %collective-permute-start.14 = (bf16[96,3072]{1,0:T(8,128)(2,1)S(1)}, bf16[96,3072]{1,0:T(8,128)(2,1)S(1)}, u32[]{:S(2)}, u32[]{:S(2)}) collective-permute-start(bf16[96,3072]{1,0:T(8,128)(2,1)S(1)} %constant_dynamic-update-slice_fusion.4.mine.refs_10_), channel_id=1, source_target_pairs={{0,16},{8,24},{16,0},{24,8},{1,17},{9,25},{17,1},{25,9},{2,18},{10... | collective-permute-start | bytes 1769480 | tf_op jit(solution)/shard_map/ppermute | solution.py:41
  41.1 14.7 %collective-permute-start.15 = (bf16[96,3072]{1,0:T(8,128)(2,1)S(1)}, bf16[96,3072]{1,0:T(8,128)(2,1)S(1)}, u32[]{:S(2)}, u32[]{:S(2)}) collective-permute-start(bf16[96,3072]{1,0:T(8,128)(2,1)S(1)} %get-tuple-element.121), channel_id=1, source_target_pairs={{0,1},{1,0},{2,3},{3,2},{4,5},{5,4},{6,7},{7,6},{8,9},{9,8},{10,11... | collective-permute-start | bytes 1769480 | tf_op jit(solution)/shard_map/ppermute | solution.py:46
  44.0 11.5 %collective-permute-start.12 = (bf16[24,3072]{1,0:T(8,128)(2,1)S(1)}, bf16[24,3072]{1,0:T(8,128)(2,1)S(1)}, u32[]{:S(2)}, u32[]{:S(2)}) collective-permute-start(bf16[24,3072]{1,0:T(8,128)(2,1)S(1)} %get-tuple-element.110), channel_id=1, source_target_pairs={{0,4},{1,5},{2,6},{3,7},{4,0},{5,1},{6,2},{7,3},{8,12},{9,13},{10,... | collective-permute-start | bytes 442376 | tf_op jit(solution)/shard_map/ppermute | solution.py:46
  55.8 16.3 %collective-permute-start.20 = (bf16[96,3072]{1,0:T(8,128)(2,1)S(1)}, bf16[96,3072]{1,0:T(8,128)(2,1)S(1)}, u32[]{:S(2)}, u32[]{:S(2)}) collective-permute-start(bf16[96,3072]{1,0:T(8,128)(2,1)S(1)} %get-tuple-element.131), channel_id=1, source_target_pairs={{0,16},{8,24},{16,0},{24,8},{1,17},{9,25},{17,1},{25,9},{2,18},{10... | collective-permute-start | bytes 1769480 | tf_op jit(solution)/shard_map/ppermute | solution.py:41
  60.0 12.0 %collective-permute-start.18 = (bf16[24,3072]{1,0:T(8,128)(2,1)S(1)}, bf16[24,3072]{1,0:T(8,128)(2,1)S(1)}, u32[]{:S(2)}, u32[]{:S(2)}) collective-permute-start(bf16[24,3072]{1,0:T(8,128)(2,1)S(1)} %get-tuple-element.204), channel_id=1, source_target_pairs={{0,4},{1,5},{2,6},{3,7},{4,0},{5,1},{6,2},{7,3},{8,12},{9,13},{10,... | collective-permute-start | bytes 442376 | tf_op jit(solution)/shard_map/ppermute | solution.py:46
  60.0 12.0 %collective-permute-start.19 = (bf16[24,3072]{1,0:T(8,128)(2,1)S(1)}, bf16[24,3072]{1,0:T(8,128)(2,1)S(1)}, u32[]{:S(2)}, u32[]{:S(2)}) collective-permute-start(bf16[24,3072]{1,0:T(8,128)(2,1)S(1)} %get-tuple-element.203), channel_id=1, source_target_pairs={{0,2},{1,3},{2,0},{3,1},{4,6},{5,7},{6,4},{7,5},{8,10},{9,11},{10,... | collective-permute-start | bytes 442376 | tf_op jit(solution)/shard_map/ppermute | solution.py:46
  72.0 15.7 %collective-permute-start.24 = (bf16[96,3072]{1,0:T(8,128)(2,1)S(1)}, bf16[96,3072]{1,0:T(8,128)(2,1)S(1)}, u32[]{:S(2)}, u32[]{:S(2)}) collective-permute-start(bf16[96,3072]{1,0:T(8,128)(2,1)S(1)} %get-tuple-element.135), channel_id=1, source_target_pairs={{0,16},{8,24},{16,0},{24,8},{1,17},{9,25},{17,1},{25,9},{2,18},{10... | collective-permute-start | bytes 1769480 | tf_op jit(solution)/shard_map/ppermute | solution.py:41
  75.4 12.3 %collective-permute-start.22 = (bf16[24,3072]{1,0:T(8,128)(2,1)S(1)}, bf16[24,3072]{1,0:T(8,128)(2,1)S(1)}, u32[]{:S(2)}, u32[]{:S(2)}) collective-permute-start(bf16[24,3072]{1,0:T(8,128)(2,1)S(1)} %get-tuple-element.200), channel_id=1, source_target_pairs={{0,4},{1,5},{2,6},{3,7},{4,0},{5,1},{6,2},{7,3},{8,12},{9,13},{10,... | collective-permute-start | bytes 442376 | tf_op jit(solution)/shard_map/ppermute | solution.py:46
  75.4 12.3 %collective-permute-start.23 = (bf16[24,3072]{1,0:T(8,128)(2,1)S(1)}, bf16[24,3072]{1,0:T(8,128)(2,1)S(1)}, u32[]{:S(2)}, u32[]{:S(2)}) collective-permute-start(bf16[24,3072]{1,0:T(8,128)(2,1)S(1)} %get-tuple-element.199), channel_id=1, source_target_pairs={{0,2},{1,3},{2,0},{3,1},{4,6},{5,7},{6,4},{7,5},{8,10},{9,11},{10,... | collective-permute-start | bytes 442376 | tf_op jit(solution)/shard_map/ppermute | solution.py:46
  90.9 12.6 %collective-permute-start.27 = (bf16[24,3072]{1,0:T(8,128)(2,1)S(1)}, bf16[24,3072]{1,0:T(8,128)(2,1)S(1)}, u32[]{:S(2)}, u32[]{:S(2)}) collective-permute-start(bf16[24,3072]{1,0:T(8,128)(2,1)S(1)} %get-tuple-element.197), channel_id=1, source_target_pairs={{0,5},{1,4},{2,7},{3,6},{4,1},{5,0},{6,3},{7,2},{8,13},{9,12},{10,... | collective-permute-start | bytes 442376 | tf_op jit(solution)/shard_map/ppermute | solution.py:46
  90.9 15.5 %collective-permute-start.29 = (bf16[96,3072]{1,0:T(8,128)(2,1)S(1)}, bf16[96,3072]{1,0:T(8,128)(2,1)S(1)}, u32[]{:S(2)}, u32[]{:S(2)}) collective-permute-start(bf16[96,3072]{1,0:T(8,128)(2,1)S(1)} %get-tuple-element.154.refs_0_), channel_id=1, source_target_pairs={{0,16},{8,24},{16,0},{24,8},{1,17},{9,25},{17,1},{25,9},{2,18},{10... | collective-permute-start | bytes 1769480 | tf_op jit(solution)/shard_map/ppermute | solution.py:41
  91.7 11.8 %collective-permute-start.28 = (bf16[24,3072]{1,0:T(8,128)(2,1)S(1)}, bf16[24,3072]{1,0:T(8,128)(2,1)S(1)}, u32[]{:S(2)}, u32[]{:S(2)}) collective-permute-start(bf16[24,3072]{1,0:T(8,128)(2,1)S(1)} %get-tuple-element.196), channel_id=1, source_target_pairs={{0,3},{1,2},{2,1},{3,0},{4,7},{5,6},{6,5},{7,4},{8,11},{9,10},{10,... | collective-permute-start | bytes 442376 | tf_op jit(solution)/shard_map/ppermute | solution.py:46
  95.4 14.3 %collective-permute-start.34 = (bf16[96,3072]{1,0:T(8,128)(2,1)S(1)}, bf16[96,3072]{1,0:T(8,128)(2,1)S(1)}, u32[]{:S(2)}, u32[]{:S(2)}) collective-permute-start(bf16[96,3072]{1,0:T(8,128)(2,1)S(1)} %get-tuple-element.154.refs_0_), channel_id=1, source_target_pairs={{0,8},{8,0},{16,24},{24,16},{1,9},{9,1},{17,25},{25,17},{2,10},{10... | collective-permute-start | bytes 1769480 | tf_op jit(solution)/shard_map/ppermute | solution.py:41
  106.9 12.2 %collective-permute-start.33 = (bf16[48,3072]{1,0:T(8,128)(2,1)S(1)}, bf16[48,3072]{1,0:T(8,128)(2,1)S(1)}, u32[]{:S(2)}, u32[]{:S(2)}) collective-permute-start(bf16[48,3072]{1,0:T(8,128)(2,1)S(1)} %get-tuple-element.193), channel_id=1, source_target_pairs={{0,16},{8,24},{16,0},{24,8},{1,17},{9,25},{17,1},{25,9},{2,18},{10... | collective-permute-start | bytes 884744 | tf_op jit(solution)/shard_map/ppermute | solution.py:41
  108.3 14.4 %collective-permute-start.32 = (bf16[48,3072]{1,0:T(8,128)(2,1)S(1)}, bf16[48,3072]{1,0:T(8,128)(2,1)S(1)}, u32[]{:S(2)}, u32[]{:S(2)}) collective-permute-start(bf16[48,3072]{1,0:T(8,128)(2,1)S(1)} %get-tuple-element.194), channel_id=1, source_target_pairs={{0,16},{8,24},{16,0},{24,8},{1,17},{9,25},{17,1},{25,9},{2,18},{10... | collective-permute-start | bytes 884744 | tf_op jit(solution)/shard_map/ppermute | solution.py:41
  109.7 13.0 %collective-permute-start.39 = (bf16[96,3072]{1,0:T(8,128)(2,1)S(1)}, bf16[96,3072]{1,0:T(8,128)(2,1)S(1)}, u32[]{:S(2)}, u32[]{:S(2)}) collective-permute-start(bf16[96,3072]{1,0:T(8,128)(2,1)S(1)} %collective-permute-done.14.far), channel_id=1, source_target_pairs={{0,8},{8,0},{16,24},{24,16},{1,9},{9,1},{17,25},{25,17},{2,10},{10... | collective-permute-start | bytes 1769480 | tf_op jit(solution)/shard_map/ppermute | solution.py:41
  (26 other events, 192.7 us)

commit v8 on v7

--- a/solution.py
+++ b/solution.py
@@ -12,7 +12,7 @@
 GROUPS = 2
 f32 = jnp.float32
 bf16 = jnp.bfloat16
-VMEM_LIMIT = 36 * 1024 * 1024
+VMEM_LIMIT = 32 * 1024 * 1024
 WEIGH = 10
 
 

time: 129 us -> 129 us (level)
  waiting for transfers between devices: 55.4 us -> 57.3 us
  local copies, waits for them, and re-layouts: 4.3 us -> 2.41 us
    unnamed x22 -> x18, local copies, waits for them, and re-layouts: 3.77 us -> 1.88 us
    ppermute x21, waiting for transfers between devices: 47.3 us -> 49.2 us  [pass_on(): return lax.ppermute(v, 'expert', [(i, i ^ distance) for i in range(n)])]
where the time goes in v8:
time: 129 us
  waiting for transfers between devices  57.3 us (44%)
  starting transfers between devices  40.8 us (32%)
  Pallas kernels  25.5 us (20%)
  local copies, waits for them, and re-layouts  2.41 us (2%)
  other arithmetic  1.41 us (1%)
    ppermute x21, waiting for transfers between devices, pass_on(): return lax.ppermute(v, 'expert', [(i, i ^ distance) for i in range(n)])  49.2 us
    ppermute x21, starting transfers between devices, pass_on(): return lax.ppermute(v, 'expert', [(i, i ^ distance) for i in range(n)])  32.1 us
    pallas_call x2, Pallas kernels, gradients(): call(functools.partial(gradients_kernel, tiles, count), 'gradients_sum' i...  13.1 us
    pallas_call x2, Pallas kernels, forward(): call(functools.partial(forward_kernel, steps), 'forward', [jax.ShapeDtype...  9.18 us
    ppermute x21, starting transfers between devices, swap(): return lax.ppermute(v, 'dp', [(i, i ^ distance) for i in range(n)])  8.72 us
    ppermute x21, waiting for transfers between devices, swap(): return lax.ppermute(v, 'dp', [(i, i ^ distance) for i in range(n)])  8.04 us
  transfers between devices with their start and end apart: 42, of which 18 were waited for; matrix products, arithmetic and copies ran while one was open for 2% of the time, Pallas kernels for 17%

profile of v8, /device:TPU:0, one launch (start us, length us, event | category | flops | bytes accessed | tf_op | source)
XLA Modules:
  0.0 128.5 jit_solution(8870963392694473506)
XLA Ops:
  4.0 2.6 %collective-permute-start.3 = (bf16[96,3072]{1,0:T(8,128)(2,1)S(1)}, bf16[96,3072]{1,0:T(8,128)(2,1)S(1)}, u32[]{:S(2)}, u32[]{:S(2)}) collective-permute-start(bf16[96,3072]{1,0:T(8,128)(2,1)S(1)} %get-tuple-element.97), channel_id=1, source_target_pairs={{0,1},{1,0},{2,3},{3,2},{4,5},{5,4},{6,7},{7,6},{8,9},{9,8},{10,11... | collective-permute-start | bytes 1769480 | tf_op jit(solution)/shard_map/ppermute | solution.py:46
  6.8 3.7 %collective-permute-start = (bf16[24,3072]{1,0:T(8,128)(2,1)S(1)}, bf16[24,3072]{1,0:T(8,128)(2,1)S(1)}, u32[]{:S(2)}, u32[]{:S(2)}) collective-permute-start(bf16[24,3072]{1,0:T(8,128)(2,1)S(1)} %get-tuple-element.213), channel_id=1, source_target_pairs={{0,6},{1,7},{2,4},{3,5},{4,2},{5,3},{6,0},{7,1},{8,14},{9,15},{10,... | collective-permute-start | bytes 442376 | tf_op jit(solution)/shard_map/ppermute | solution.py:46
  12.1 3.4 %collective-permute-done = bf16[24,3072]{1,0:T(8,128)(2,1)S(1)} collective-permute-done((bf16[24,3072]{1,0:T(8,128)(2,1)S(1)}, bf16[24,3072]{1,0:T(8,128)(2,1)S(1)}, u32[]{:S(2)}, u32[]{:S(2)}) %collective-permute-start) | collective-permute-done | bytes 147488 | tf_op jit(solution)/shard_map/ppermute | solution.py:46
  15.5 8.0 %collective-permute-done.1 = bf16[24,3072]{1,0:T(8,128)(2,1)S(1)} collective-permute-done((bf16[24,3072]{1,0:T(8,128)(2,1)S(1)}, bf16[24,3072]{1,0:T(8,128)(2,1)S(1)}, u32[]{:S(2)}, u32[]{:S(2)}) %collective-permute-start.1) | collective-permute-done | bytes 147488 | tf_op jit(solution)/shard_map/ppermute | solution.py:46
  25.2 2.5 %collective-permute-start.6 = (bf16[24,3072]{1,0:T(8,128)(2,1)S(1)}, bf16[24,3072]{1,0:T(8,128)(2,1)S(1)}, u32[]{:S(2)}, u32[]{:S(2)}) collective-permute-start(bf16[24,3072]{1,0:T(8,128)(2,1)S(1)} %get-tuple-element.209), channel_id=1, source_target_pairs={{0,6},{1,7},{2,4},{3,5},{4,2},{5,3},{6,0},{7,1},{8,14},{9,15},{10,... | collective-permute-start | bytes 442376 | tf_op jit(solution)/shard_map/ppermute | solution.py:46
  29.7 4.2 %collective-permute-done.6 = bf16[24,3072]{1,0:T(8,128)(2,1)S(1)} collective-permute-done((bf16[24,3072]{1,0:T(8,128)(2,1)S(1)}, bf16[24,3072]{1,0:T(8,128)(2,1)S(1)}, u32[]{:S(2)}, u32[]{:S(2)}) %collective-permute-start.6) | collective-permute-done | bytes 147488 | tf_op jit(solution)/shard_map/ppermute | solution.py:46
  33.9 5.9 %collective-permute-done.7 = bf16[24,3072]{1,0:T(8,128)(2,1)S(1)} collective-permute-done((bf16[24,3072]{1,0:T(8,128)(2,1)S(1)}, bf16[24,3072]{1,0:T(8,128)(2,1)S(1)}, u32[]{:S(2)}, u32[]{:S(2)}) %collective-permute-start.7) | collective-permute-done | bytes 147488 | tf_op jit(solution)/shard_map/ppermute | solution.py:46
  41.6 2.5 %collective-permute-start.11 = (bf16[24,3072]{1,0:T(8,128)(2,1)S(1)}, bf16[24,3072]{1,0:T(8,128)(2,1)S(1)}, u32[]{:S(2)}, u32[]{:S(2)}) collective-permute-start(bf16[24,3072]{1,0:T(8,128)(2,1)S(1)} %get-tuple-element.109), channel_id=1, source_target_pairs={{0,6},{1,7},{2,4},{3,5},{4,2},{5,3},{6,0},{7,1},{8,14},{9,15},{10,... | collective-permute-start | bytes 442376 | tf_op jit(solution)/shard_map/ppermute | solution.py:46
  44.0 1.9 %collective-permute-start.13 = (bf16[24,3072]{1,0:T(8,128)(2,1)S(1)}, bf16[24,3072]{1,0:T(8,128)(2,1)S(1)}, u32[]{:S(2)}, u32[]{:S(2)}) collective-permute-start(bf16[24,3072]{1,0:T(8,128)(2,1)S(1)} %get-tuple-element.111), channel_id=1, source_target_pairs={{0,2},{1,3},{2,0},{3,1},{4,6},{5,7},{6,4},{7,5},{8,10},{9,11},{10,... | collective-permute-start | bytes 442376 | tf_op jit(solution)/shard_map/ppermute | solution.py:46
  46.0 4.6 %forward.2 = (f32[192,512]{1,0:T(8,128)S(1)}, f32[192,512]{1,0:T(8,128)S(1)}, f32[96,3072]{1,0:T(8,128)S(1)}, bf16[96,3072]{1,0:T(8,128)(2,1)S(1)}) custom-call(bf16[96,3072]{1,0:T(8,128)(2,1)S(1)} %constant_dynamic-update-slice_fusion.mine.refs_6_, bf16[96,3072]{1,0:T(8,128)(2,1)S(1)} %collective-permute-done.9.far.refs_8_, ...), custom_call_target="tpu_custom_call" | custom-call | flops 24159191040 | bytes 167116800 | tf_op jit(solution)/shard_map/forward/pallas_call | solution.py:162
  50.6 4.9 %collective-permute-done.12 = bf16[24,3072]{1,0:T(8,128)(2,1)S(1)} collective-permute-done((bf16[24,3072]{1,0:T(8,128)(2,1)S(1)}, bf16[24,3072]{1,0:T(8,128)(2,1)S(1)}, u32[]{:S(2)}, u32[]{:S(2)}) %collective-permute-start.12) | collective-permute-done | bytes 147488 | tf_op jit(solution)/shard_map/ppermute | solution.py:46
  57.5 2.5 %collective-permute-start.17 = (bf16[24,3072]{1,0:T(8,128)(2,1)S(1)}, bf16[24,3072]{1,0:T(8,128)(2,1)S(1)}, u32[]{:S(2)}, u32[]{:S(2)}) collective-permute-start(bf16[24,3072]{1,0:T(8,128)(2,1)S(1)} %get-tuple-element.205), channel_id=1, source_target_pairs={{0,6},{1,7},{2,4},{3,5},{4,2},{5,3},{6,0},{7,1},{8,14},{9,15},{10,... | collective-permute-start | bytes 442376 | tf_op jit(solution)/shard_map/ppermute | solution.py:46
  61.9 4.6 %forward.3 = (f32[192,512]{1,0:T(8,128)S(1)}, f32[192,512]{1,0:T(8,128)S(1)}, f32[96,3072]{1,0:T(8,128)S(1)}, bf16[96,3072]{1,0:T(8,128)(2,1)S(1)}) custom-call(bf16[96,3072]{1,0:T(8,128)(2,1)S(1)} %constant_dynamic-update-slice_fusion.4.mine.refs_10_, bf16[96,3072]{1,0:T(8,128)(2,1)S(1)} %collective-permute-done.14.far, ...), custom_call_target="tpu_custom_call" | custom-call | flops 24159191040 | bytes 167116800 | tf_op jit(solution)/shard_map/forward/pallas_call | solution.py:162
  66.6 5.4 %collective-permute-done.18 = bf16[24,3072]{1,0:T(8,128)(2,1)S(1)} collective-permute-done((bf16[24,3072]{1,0:T(8,128)(2,1)S(1)}, bf16[24,3072]{1,0:T(8,128)(2,1)S(1)}, u32[]{:S(2)}, u32[]{:S(2)}) %collective-permute-start.18) | collective-permute-done | bytes 147488 | tf_op jit(solution)/shard_map/ppermute | solution.py:46
  75.4 2.8 %collective-permute-start.23 = (bf16[24,3072]{1,0:T(8,128)(2,1)S(1)}, bf16[24,3072]{1,0:T(8,128)(2,1)S(1)}, u32[]{:S(2)}, u32[]{:S(2)}) collective-permute-start(bf16[24,3072]{1,0:T(8,128)(2,1)S(1)} %get-tuple-element.199), channel_id=1, source_target_pairs={{0,2},{1,3},{2,0},{3,1},{4,6},{5,7},{6,4},{7,5},{8,10},{9,11},{10,... | collective-permute-start | bytes 442376 | tf_op jit(solution)/shard_map/ppermute | solution.py:46
  78.5 3.9 %collective-permute-done.21 = bf16[24,3072]{1,0:T(8,128)(2,1)S(1)} collective-permute-done((bf16[24,3072]{1,0:T(8,128)(2,1)S(1)}, bf16[24,3072]{1,0:T(8,128)(2,1)S(1)}, u32[]{:S(2)}, u32[]{:S(2)}) %collective-permute-start.21) | collective-permute-done | bytes 147488 | tf_op jit(solution)/shard_map/ppermute | solution.py:46
  82.4 5.3 %collective-permute-done.22 = bf16[24,3072]{1,0:T(8,128)(2,1)S(1)} collective-permute-done((bf16[24,3072]{1,0:T(8,128)(2,1)S(1)}, bf16[24,3072]{1,0:T(8,128)(2,1)S(1)}, u32[]{:S(2)}, u32[]{:S(2)}) %collective-permute-start.22) | collective-permute-done | bytes 147488 | tf_op jit(solution)/shard_map/ppermute | solution.py:46
  88.1 2.8 %collective-permute-start.26 = (bf16[24,3072]{1,0:T(8,128)(2,1)S(1)}, bf16[24,3072]{1,0:T(8,128)(2,1)S(1)}, u32[]{:S(2)}, u32[]{:S(2)}) collective-permute-start(bf16[24,3072]{1,0:T(8,128)(2,1)S(1)} %get-tuple-element.198), channel_id=1, source_target_pairs={{0,7},{1,6},{2,5},{3,4},{4,3},{5,2},{6,1},{7,0},{8,15},{9,14},{10,... | collective-permute-start | bytes 442376 | tf_op jit(solution)/shard_map/ppermute | solution.py:46
  91.7 3.5 %collective-permute-start.28 = (bf16[24,3072]{1,0:T(8,128)(2,1)S(1)}, bf16[24,3072]{1,0:T(8,128)(2,1)S(1)}, u32[]{:S(2)}, u32[]{:S(2)}) collective-permute-start(bf16[24,3072]{1,0:T(8,128)(2,1)S(1)} %get-tuple-element.196), channel_id=1, source_target_pairs={{0,3},{1,2},{2,1},{3,0},{4,7},{5,6},{6,5},{7,4},{8,11},{9,10},{10,... | collective-permute-start | bytes 442376 | tf_op jit(solution)/shard_map/ppermute | solution.py:46
  95.5 2.2 %collective-permute-done.26 = bf16[24,3072]{1,0:T(8,128)(2,1)S(1)} collective-permute-done((bf16[24,3072]{1,0:T(8,128)(2,1)S(1)}, bf16[24,3072]{1,0:T(8,128)(2,1)S(1)}, u32[]{:S(2)}, u32[]{:S(2)}) %collective-permute-start.26) | collective-permute-done | bytes 147488 | tf_op jit(solution)/shard_map/ppermute | solution.py:46
  97.6 5.8 %collective-permute-done.27 = bf16[24,3072]{1,0:T(8,128)(2,1)S(1)} collective-permute-done((bf16[24,3072]{1,0:T(8,128)(2,1)S(1)}, bf16[24,3072]{1,0:T(8,128)(2,1)S(1)}, u32[]{:S(2)}, u32[]{:S(2)}) %collective-permute-start.27) | collective-permute-done | bytes 147488 | tf_op jit(solution)/shard_map/ppermute | solution.py:46
  103.5 2.9 %collective-permute-done.29.refs_2_ = bf16[96,3072]{1,0:T(8,128)(2,1)S(1)} collective-permute-done((bf16[96,3072]{1,0:T(8,128)(2,1)S(1)}, bf16[96,3072]{1,0:T(8,128)(2,1)S(1)}, u32[]{:S(2)}, u32[]{:S(2)}) %collective-permute-start.29) | collective-permute-done | bytes 589856 | tf_op jit(solution)/shard_map/ppermute | solution.py:41
  110.0 9.0 %gradients.1 = (bf16[1,3072,512]{2,1,0:T(8,128)(2,1)S(1)}, bf16[1,3072,512]{2,1,0:T(8,128)(2,1)S(1)}) custom-call(bf16[96,3072]{1,0:T(8,128)(2,1)S(1)} %get-tuple-element.154.refs_0_, bf16[96,3072]{1,0:T(8,128)(2,1)S(1)} %collective-permute-done.34.refs_1_, bf16[96,3072]{1,0:T(8,128)(2,1)S(1)} %collective-permute-done.29.refs_2_, ...), custom_call_target="tpu_custom_call" | custom-call | flops 54358179840 | bytes 165150720 | tf_op jit(solution)/shard_map/gradients/pallas_call | solution.py:236
  124.3 4.1 %gradients_sum.1 = (bf16[1,3072,512]{2,1,0:T(8,128)(2,1)}, bf16[1,3072,512]{2,1,0:T(8,128)(2,1)}) custom-call(bf16[48,3072]{1,0:T(8,128)(2,1)S(1)} %collective-permute-done.33.refs_0_, bf16[48,3072]{1,0:T(8,128)(2,1)S(1)} %collective-permute-done.32.refs_1_, bf16[48,3072]{1,0:T(8,128)(2,1)S(1)} %collective-permute-done.38.refs_2_, ...), custom_call_target="tpu_custom_call" | custom-call | flops 18119393280 | bytes 117964800 | tf_op jit(solution)/shard_map/gradients_sum/pallas_call | solution.py:236
  (111 shorter events, 28.5 us)
Async XLA Ops:
  0.6 22.8 %collective-permute-start.5 = (bf16[3072,512]{1,0:T(8,128)(2,1)}, bf16[3072,512]{1,0:T(8,128)(2,1)S(1)}, u32[]{:S(2)}, u32[]{:S(2)}) collective-permute-start(bf16[3072,512]{1,0:T(8,128)(2,1)} %bitcast.3), channel_id=1, source_target_pairs={{0,8},{8,0},{16,24},{24,16},{1,9},{9,1},{17,25},{25,17},{2,10},{10... | collective-permute-start | bytes 9437192 | tf_op jit(solution)/shard_map/ppermute | solution.py:41
  4.0 19.5 %collective-permute-start.3 = (bf16[96,3072]{1,0:T(8,128)(2,1)S(1)}, bf16[96,3072]{1,0:T(8,128)(2,1)S(1)}, u32[]{:S(2)}, u32[]{:S(2)}) collective-permute-start(bf16[96,3072]{1,0:T(8,128)(2,1)S(1)} %get-tuple-element.97), channel_id=1, source_target_pairs={{0,1},{1,0},{2,3},{3,2},{4,5},{5,4},{6,7},{7,6},{8,9},{9,8},{10,11... | collective-permute-start | bytes 1769480 | tf_op jit(solution)/shard_map/ppermute | solution.py:46
  10.5 12.9 %collective-permute-start.1 = (bf16[24,3072]{1,0:T(8,128)(2,1)S(1)}, bf16[24,3072]{1,0:T(8,128)(2,1)S(1)}, u32[]{:S(2)}, u32[]{:S(2)}) collective-permute-start(bf16[24,3072]{1,0:T(8,128)(2,1)S(1)} %get-tuple-element.212), channel_id=1, source_target_pairs={{0,4},{1,5},{2,6},{3,7},{4,0},{5,1},{6,2},{7,3},{8,12},{9,13},{10,... | collective-permute-start | bytes 442376 | tf_op jit(solution)/shard_map/ppermute | solution.py:46
  10.5 12.9 %collective-permute-start.2 = (bf16[24,3072]{1,0:T(8,128)(2,1)S(1)}, bf16[24,3072]{1,0:T(8,128)(2,1)S(1)}, u32[]{:S(2)}, u32[]{:S(2)}) collective-permute-start(bf16[24,3072]{1,0:T(8,128)(2,1)S(1)} %get-tuple-element.211), channel_id=1, source_target_pairs={{0,2},{1,3},{2,0},{3,1},{4,6},{5,7},{6,4},{7,5},{8,10},{9,11},{10,... | collective-permute-start | bytes 442376 | tf_op jit(solution)/shard_map/ppermute | solution.py:46
  23.5 16.4 %collective-permute-start.10 = (bf16[3072,512]{1,0:T(8,128)(2,1)S(1)}, bf16[3072,512]{1,0:T(8,128)(2,1)S(1)}, u32[]{:S(2)}, u32[]{:S(2)}) collective-permute-start(bf16[3072,512]{1,0:T(8,128)(2,1)S(1)} %bitcast.6), channel_id=1, source_target_pairs={{0,8},{8,0},{16,24},{24,16},{1,9},{9,1},{17,25},{25,17},{2,10},{10... | collective-permute-start | bytes 9437192 | tf_op jit(solution)/shard_map/ppermute | solution.py:41
  23.6 16.2 %collective-permute-start.9 = (bf16[96,3072]{1,0:T(8,128)(2,1)S(1)}, bf16[96,3072]{1,0:T(8,128)(2,1)S(1)}, u32[]{:S(2)}, u32[]{:S(2)}) collective-permute-start(bf16[96,3072]{1,0:T(8,128)(2,1)S(1)} %constant_dynamic-update-slice_fusion.mine.refs_6_), channel_id=1, source_target_pairs={{0,16},{8,24},{16,0},{24,8},{1,17},{9,25},{17,1},{25,9},{2,18},{10... | collective-permute-start | bytes 1769480 | tf_op jit(solution)/shard_map/ppermute | solution.py:41
  27.8 12.1 %collective-permute-start.7 = (bf16[24,3072]{1,0:T(8,128)(2,1)S(1)}, bf16[24,3072]{1,0:T(8,128)(2,1)S(1)}, u32[]{:S(2)}, u32[]{:S(2)}) collective-permute-start(bf16[24,3072]{1,0:T(8,128)(2,1)S(1)} %get-tuple-element.208), channel_id=1, source_target_pairs={{0,4},{1,5},{2,6},{3,7},{4,0},{5,1},{6,2},{7,3},{8,12},{9,13},{10,... | collective-permute-start | bytes 442376 | tf_op jit(solution)/shard_map/ppermute | solution.py:46
  27.8 12.1 %collective-permute-start.8 = (bf16[24,3072]{1,0:T(8,128)(2,1)S(1)}, bf16[24,3072]{1,0:T(8,128)(2,1)S(1)}, u32[]{:S(2)}, u32[]{:S(2)}) collective-permute-start(bf16[24,3072]{1,0:T(8,128)(2,1)S(1)} %get-tuple-element.207), channel_id=1, source_target_pairs={{0,2},{1,3},{2,0},{3,1},{4,6},{5,7},{6,4},{7,5},{8,10},{9,11},{10,... | collective-permute-start | bytes 442376 | tf_op jit(solution)/shard_map/ppermute | solution.py:46
  39.9 15.5 %collective-permute-start.14 = (bf16[96,3072]{1,0:T(8,128)(2,1)S(1)}, bf16[96,3072]{1,0:T(8,128)(2,1)S(1)}, u32[]{:S(2)}, u32[]{:S(2)}) collective-permute-start(bf16[96,3072]{1,0:T(8,128)(2,1)S(1)} %constant_dynamic-update-slice_fusion.4.mine.refs_10_), channel_id=1, source_target_pairs={{0,16},{8,24},{16,0},{24,8},{1,17},{9,25},{17,1},{25,9},{2,18},{10... | collective-permute-start | bytes 1769480 | tf_op jit(solution)/shard_map/ppermute | solution.py:41
  41.1 14.7 %collective-permute-start.15 = (bf16[96,3072]{1,0:T(8,128)(2,1)S(1)}, bf16[96,3072]{1,0:T(8,128)(2,1)S(1)}, u32[]{:S(2)}, u32[]{:S(2)}) collective-permute-start(bf16[96,3072]{1,0:T(8,128)(2,1)S(1)} %get-tuple-element.121), channel_id=1, source_target_pairs={{0,1},{1,0},{2,3},{3,2},{4,5},{5,4},{6,7},{7,6},{8,9},{9,8},{10,11... | collective-permute-start | bytes 1769480 | tf_op jit(solution)/shard_map/ppermute | solution.py:46
  44.0 11.4 %collective-permute-start.12 = (bf16[24,3072]{1,0:T(8,128)(2,1)S(1)}, bf16[24,3072]{1,0:T(8,128)(2,1)S(1)}, u32[]{:S(2)}, u32[]{:S(2)}) collective-permute-start(bf16[24,3072]{1,0:T(8,128)(2,1)S(1)} %get-tuple-element.110), channel_id=1, source_target_pairs={{0,4},{1,5},{2,6},{3,7},{4,0},{5,1},{6,2},{7,3},{8,12},{9,13},{10,... | collective-permute-start | bytes 442376 | tf_op jit(solution)/shard_map/ppermute | solution.py:46
  55.8 16.3 %collective-permute-start.20 = (bf16[96,3072]{1,0:T(8,128)(2,1)S(1)}, bf16[96,3072]{1,0:T(8,128)(2,1)S(1)}, u32[]{:S(2)}, u32[]{:S(2)}) collective-permute-start(bf16[96,3072]{1,0:T(8,128)(2,1)S(1)} %get-tuple-element.131), channel_id=1, source_target_pairs={{0,16},{8,24},{16,0},{24,8},{1,17},{9,25},{17,1},{25,9},{2,18},{10... | collective-permute-start | bytes 1769480 | tf_op jit(solution)/shard_map/ppermute | solution.py:41
  60.0 12.0 %collective-permute-start.18 = (bf16[24,3072]{1,0:T(8,128)(2,1)S(1)}, bf16[24,3072]{1,0:T(8,128)(2,1)S(1)}, u32[]{:S(2)}, u32[]{:S(2)}) collective-permute-start(bf16[24,3072]{1,0:T(8,128)(2,1)S(1)} %get-tuple-element.204), channel_id=1, source_target_pairs={{0,4},{1,5},{2,6},{3,7},{4,0},{5,1},{6,2},{7,3},{8,12},{9,13},{10,... | collective-permute-start | bytes 442376 | tf_op jit(solution)/shard_map/ppermute | solution.py:46
  60.0 12.0 %collective-permute-start.19 = (bf16[24,3072]{1,0:T(8,128)(2,1)S(1)}, bf16[24,3072]{1,0:T(8,128)(2,1)S(1)}, u32[]{:S(2)}, u32[]{:S(2)}) collective-permute-start(bf16[24,3072]{1,0:T(8,128)(2,1)S(1)} %get-tuple-element.203), channel_id=1, source_target_pairs={{0,2},{1,3},{2,0},{3,1},{4,6},{5,7},{6,4},{7,5},{8,10},{9,11},{10,... | collective-permute-start | bytes 442376 | tf_op jit(solution)/shard_map/ppermute | solution.py:46
  72.0 15.7 %collective-permute-start.24 = (bf16[96,3072]{1,0:T(8,128)(2,1)S(1)}, bf16[96,3072]{1,0:T(8,128)(2,1)S(1)}, u32[]{:S(2)}, u32[]{:S(2)}) collective-permute-start(bf16[96,3072]{1,0:T(8,128)(2,1)S(1)} %get-tuple-element.135), channel_id=1, source_target_pairs={{0,16},{8,24},{16,0},{24,8},{1,17},{9,25},{17,1},{25,9},{2,18},{10... | collective-permute-start | bytes 1769480 | tf_op jit(solution)/shard_map/ppermute | solution.py:41
  75.4 12.3 %collective-permute-start.22 = (bf16[24,3072]{1,0:T(8,128)(2,1)S(1)}, bf16[24,3072]{1,0:T(8,128)(2,1)S(1)}, u32[]{:S(2)}, u32[]{:S(2)}) collective-permute-start(bf16[24,3072]{1,0:T(8,128)(2,1)S(1)} %get-tuple-element.200), channel_id=1, source_target_pairs={{0,4},{1,5},{2,6},{3,7},{4,0},{5,1},{6,2},{7,3},{8,12},{9,13},{10,... | collective-permute-start | bytes 442376 | tf_op jit(solution)/shard_map/ppermute | solution.py:46
  75.4 12.3 %collective-permute-start.23 = (bf16[24,3072]{1,0:T(8,128)(2,1)S(1)}, bf16[24,3072]{1,0:T(8,128)(2,1)S(1)}, u32[]{:S(2)}, u32[]{:S(2)}) collective-permute-start(bf16[24,3072]{1,0:T(8,128)(2,1)S(1)} %get-tuple-element.199), channel_id=1, source_target_pairs={{0,2},{1,3},{2,0},{3,1},{4,6},{5,7},{6,4},{7,5},{8,10},{9,11},{10,... | collective-permute-start | bytes 442376 | tf_op jit(solution)/shard_map/ppermute | solution.py:46
  90.9 12.6 %collective-permute-start.27 = (bf16[24,3072]{1,0:T(8,128)(2,1)S(1)}, bf16[24,3072]{1,0:T(8,128)(2,1)S(1)}, u32[]{:S(2)}, u32[]{:S(2)}) collective-permute-start(bf16[24,3072]{1,0:T(8,128)(2,1)S(1)} %get-tuple-element.197), channel_id=1, source_target_pairs={{0,5},{1,4},{2,7},{3,6},{4,1},{5,0},{6,3},{7,2},{8,13},{9,12},{10,... | collective-permute-start | bytes 442376 | tf_op jit(solution)/shard_map/ppermute | solution.py:46
  90.9 15.5 %collective-permute-start.29 = (bf16[96,3072]{1,0:T(8,128)(2,1)S(1)}, bf16[96,3072]{1,0:T(8,128)(2,1)S(1)}, u32[]{:S(2)}, u32[]{:S(2)}) collective-permute-start(bf16[96,3072]{1,0:T(8,128)(2,1)S(1)} %get-tuple-element.154.refs_0_), channel_id=1, source_target_pairs={{0,16},{8,24},{16,0},{24,8},{1,17},{9,25},{17,1},{25,9},{2,18},{10... | collective-permute-start | bytes 1769480 | tf_op jit(solution)/shard_map/ppermute | solution.py:41
  91.7 11.8 %collective-permute-start.28 = (bf16[24,3072]{1,0:T(8,128)(2,1)S(1)}, bf16[24,3072]{1,0:T(8,128)(2,1)S(1)}, u32[]{:S(2)}, u32[]{:S(2)}) collective-permute-start(bf16[24,3072]{1,0:T(8,128)(2,1)S(1)} %get-tuple-element.196), channel_id=1, source_target_pairs={{0,3},{1,2},{2,1},{3,0},{4,7},{5,6},{6,5},{7,4},{8,11},{9,10},{10,... | collective-permute-start | bytes 442376 | tf_op jit(solution)/shard_map/ppermute | solution.py:46
  95.4 14.3 %collective-permute-start.34 = (bf16[96,3072]{1,0:T(8,128)(2,1)S(1)}, bf16[96,3072]{1,0:T(8,128)(2,1)S(1)}, u32[]{:S(2)}, u32[]{:S(2)}) collective-permute-start(bf16[96,3072]{1,0:T(8,128)(2,1)S(1)} %get-tuple-element.154.refs_0_), channel_id=1, source_target_pairs={{0,8},{8,0},{16,24},{24,16},{1,9},{9,1},{17,25},{25,17},{2,10},{10... | collective-permute-start | bytes 1769480 | tf_op jit(solution)/shard_map/ppermute | solution.py:41
  106.9 12.2 %collective-permute-start.33 = (bf16[48,3072]{1,0:T(8,128)(2,1)S(1)}, bf16[48,3072]{1,0:T(8,128)(2,1)S(1)}, u32[]{:S(2)}, u32[]{:S(2)}) collective-permute-start(bf16[48,3072]{1,0:T(8,128)(2,1)S(1)} %get-tuple-element.193), channel_id=1, source_target_pairs={{0,16},{8,24},{16,0},{24,8},{1,17},{9,25},{17,1},{25,9},{2,18},{10... | collective-permute-start | bytes 884744 | tf_op jit(solution)/shard_map/ppermute | solution.py:41
  108.3 14.4 %collective-permute-start.32 = (bf16[48,3072]{1,0:T(8,128)(2,1)S(1)}, bf16[48,3072]{1,0:T(8,128)(2,1)S(1)}, u32[]{:S(2)}, u32[]{:S(2)}) collective-permute-start(bf16[48,3072]{1,0:T(8,128)(2,1)S(1)} %get-tuple-element.194), channel_id=1, source_target_pairs={{0,16},{8,24},{16,0},{24,8},{1,17},{9,25},{17,1},{25,9},{2,18},{10... | collective-permute-start | bytes 884744 | tf_op jit(solution)/shard_map/ppermute | solution.py:41
  109.7 13.0 %collective-permute-start.39 = (bf16[96,3072]{1,0:T(8,128)(2,1)S(1)}, bf16[96,3072]{1,0:T(8,128)(2,1)S(1)}, u32[]{:S(2)}, u32[]{:S(2)}) collective-permute-start(bf16[96,3072]{1,0:T(8,128)(2,1)S(1)} %collective-permute-done.14.far), channel_id=1, source_target_pairs={{0,8},{8,0},{16,24},{24,16},{1,9},{9,1},{17,25},{25,17},{2,10},{10... | collective-permute-start | bytes 1769480 | tf_op jit(solution)/shard_map/ppermute | solution.py:41
  (24 other events, 166.3 us)
